TPU v7x, 32 devices: a whole 2x2x4 slice. The times are simulated.
32 devices in a mesh: parts: 2 (over x), dev: 16 (over z, y, core).
Axes of the slice: x: 2, y: 2, z: 4, core: 2. Of those that a mesh axis runs over, the one named last changes fastest.
Arguments:
- tokens: bfloat16 [256, 3072], P(('parts', 'dev')), parts along dimension 0, may hold values from -6 to 6
- grad_out: bfloat16 [256, 3072], P(('parts', 'dev')), parts along dimension 0, may hold values from -6 to 6
- expert_ids: int32 [256, 2], P(('parts', 'dev')), parts along dimension 0, may hold values from 0 to 7, all different within a row; in each aligned block of 8 rows (0 to 7, 8 to 15, ...) at most 4 rows name the same one
- gate_probs: float32 [256, 2], P(('parts', 'dev')), parts along dimension 0, may hold values from 0.1 to 1
- device_expert: int32 [16], replicated, may hold values from 0 to 3, as said below
- w_in: bfloat16 [3072, 2, 4096], P(None, None, 'dev'), may hold values from -0.109375 to 0.109375
- w_down: bfloat16 [4096, 3072], P('dev'), may hold values from -0.1875 to 0.1875
Outputs:
- grad_tokens: bfloat16 [256, 3072], P(('parts', 'dev')), parts along dimension 0
- grad_gates: float32 [256, 2], P(('parts', 'dev')), parts along dimension 0
- grad_w_in: bfloat16 [6144, 2, 4096], P('parts', None, 'dev'), parts along dimension 0
- grad_w_down: bfloat16 [8192, 3072], P(('parts', 'dev')), parts along dimension 0
There are 2 independent parts, one for each index of `parts`. A program takes and returns all parts, laid end to end along the dimension named above; an argument that names none is the same for every part. Nothing has to cross between parts.
Inputs may be any that keep to these rules, and one draw needn't show every extreme that they name: `expert_ids`: each token names 2 different experts; among the 8 tokens of one device no expert is named more than 4 times. `device_expert`: each of the 4 experts is held by a multiple of 2 devices, at least that many, at drawn positions along the axis.
All inputs are finite; a program needn't handle non-finite values.
Results may differ from a plain program's by a relative error of at most 0.0065.
Values may be sent and summed in bfloat16 or wider, within the bound.
No kernel may reach another device: no remote copies, remote signals or barrier semaphores. Data moves between devices by JAX's collectives and lax.ppermute only.
A program may use at most 64 MiB of HBM per device.

v0:
```python
import jax
import jax.numpy as jnp
from jax import lax
from jax.sharding import PartitionSpec as P

EXP_WIN = 4
MOST = 4


HIGHEST = lax.Precision.HIGHEST


def route_tables(expert_ids, gate_probs):
    experts = jnp.arange(EXP_WIN, dtype=jnp.int32)
    matched = (expert_ids[:, :, None] == experts[None, None, :]).astype(jnp.int32)
    hit_flags = jnp.sum(matched, 1)
    weights = jnp.sum(gate_probs[:, :, None] * matched.astype(jnp.float32), 1)
    slot_rank = jnp.cumsum(hit_flags, 0) - hit_flags
    places = jnp.arange(MOST, dtype=jnp.int32)
    select = (
        (slot_rank[None, :, :] == places[:, None, None]) & (hit_flags[None, :, :] > 0)
    ).astype(jnp.float32)
    select = jnp.transpose(select, (2, 0, 1))
    slot_gates = jnp.einsum("emr,re->em", select, weights, precision=HIGHEST)
    return (select, slot_gates)


def shards(tokens, grad_out, expert_ids, gate_probs, device_expert, w_in, w_down):
    dev_count = lax.axis_size("dev")
    my_index = lax.axis_index("dev")
    tok_rows = tokens.shape[0]
    experts = jnp.arange(EXP_WIN, dtype=jnp.int32)
    my_expert = jnp.sum(
        jnp.where(jnp.arange(dev_count, dtype=jnp.int32) == my_index, device_expert, 0)
    )
    expert_hot = (experts == my_expert).astype(jnp.float32)
    token_all, grad_all = (
        lax.all_gather(tokens, "dev", axis=0, tiled=True),
        lax.all_gather(grad_out, "dev", axis=0, tiled=True),
    )
    ids_all = lax.all_gather(expert_ids, "dev", axis=0, tiled=True)
    probs_all = lax.all_gather(gate_probs, "dev", axis=0, tiled=True)
    select_all, gates_all = jax.vmap(route_tables)(
        ids_all.reshape(dev_count, tok_rows, -1), probs_all.reshape(dev_count, tok_rows, -1)
    )
    select_mine = jnp.einsum("nemt,e->nmt", select_all, expert_hot, precision=HIGHEST)
    gates_mine = jnp.einsum("nem,e->nm", gates_all, expert_hot, precision=HIGHEST)
    select_half = select_mine.astype(jnp.bfloat16)
    token_rows = jnp.einsum(
        "nmt,ntd->nmd",
        select_half,
        token_all.reshape(dev_count, tok_rows, -1),
        preferred_element_type=jnp.float32,
    ).astype(jnp.bfloat16)
    grad_rows = jnp.einsum(
        "nmt,ntd->nmd",
        select_half,
        grad_all.reshape(dev_count, tok_rows, -1),
        preferred_element_type=jnp.float32,
    ).astype(jnp.bfloat16)
    flat_rows = dev_count * MOST
    token_flat = token_rows.reshape(flat_rows, -1)
    grad_flat = grad_rows.reshape(flat_rows, -1)
    slot_prob = gates_mine.reshape(flat_rows)
    projected = jnp.einsum("rd,dkh->rkh", token_flat, w_in, preferred_element_type=jnp.float32)
    gate_pre = projected[:, 0, :]
    up_pre = projected[:, 1, :]
    logistic = jax.nn.sigmoid(gate_pre)
    activated = gate_pre * logistic
    hidden = (activated * up_pre).astype(jnp.bfloat16)
    hidden_back = jnp.einsum("rd,hd->rh", grad_flat, w_down, preferred_element_type=jnp.float32)
    gate_part = jnp.sum(hidden.astype(jnp.float32) * hidden_back, 1).reshape(dev_count, MOST)
    hidden_grad = slot_prob[:, None] * hidden_back
    pre_grads = jnp.stack(
        [
            hidden_grad * up_pre * logistic * (1.0 + gate_pre * (1.0 - logistic)),
            hidden_grad * activated,
        ],
        1,
    ).astype(jnp.bfloat16)
    grad_w_in = jnp.einsum(
        "rd,rkh->dkh", token_flat, pre_grads, preferred_element_type=jnp.float32
    ).astype(jnp.bfloat16)
    scaled = (slot_prob[:, None] * grad_flat.astype(jnp.float32)).astype(jnp.bfloat16)
    grad_w_down = jnp.einsum(
        "rh,rd->hd", hidden, scaled, preferred_element_type=jnp.float32
    ).astype(jnp.bfloat16)
    token_part = jnp.einsum(
        "rkh,dkh->rd", pre_grads, w_in, preferred_element_type=jnp.float32
    ).reshape(dev_count, MOST, -1)
    grad_sum = lax.psum_scatter(
        jnp.einsum("nmt,nmd->ntd", select_mine, token_part, precision=HIGHEST).reshape(
            lax.axis_size("dev") * tok_rows, -1
        ),
        "dev",
        scatter_dimension=0,
        tiled=True,
    )
    gate_terms = jnp.einsum(
        "nmt,nm,e->nte", select_mine, gate_part, expert_hot, precision=HIGHEST
    ).reshape(dev_count * tok_rows, EXP_WIN)
    gate_sum = lax.psum_scatter(gate_terms, "dev", scatter_dimension=0, tiled=True)
    matched = (expert_ids[:, :, None] == experts[None, None, :]).astype(jnp.float32)
    grad_gates = jnp.einsum("te,tke->tk", gate_sum, matched, precision=HIGHEST)
    return (grad_sum.astype(jnp.bfloat16), grad_gates, grad_w_in, grad_w_down)


def solution(mesh):
    return jax.shard_map(
        shards,
        mesh=mesh,
        in_specs=(
            P(("parts", "dev"), None),
            P(("parts", "dev"), None),
            P(("parts", "dev"), None),
            P(("parts", "dev"), None),
            P(),
            P(None, None, "dev"),
            P("dev", None),
        ),
        out_specs=(
            P(("parts", "dev"), None),
            P(("parts", "dev"), None),
            P("parts", None, "dev"),
            P(("parts", "dev"), None),
        ),
        check_vma=False,
    )
```

profile of v0, /device:TPU:0, one launch (start us, length us, event | category | flops | bytes accessed | tf_op | source)
XLA Modules:
  0.0 219.0 jit_solution(14431396175585574287)
XLA Ops:
  7.2 0.0 copy-start
  7.2 0.0 reduce-scatter.2.cloned.1.call-start
  7.2 1.4 fusion.29
  8.7 0.6 compare_convert_fusion
  9.3 23.4 %all-gather = s32[16,8,2]{1,2,0:T(2,128)S(1)} all-gather(s32[1,8,2]{1,2,0:T(2,128)} %bitcast.96), channel_id=1, replica_groups=mesh['parts'=2,'dev'=16] {'dev'}, dimensions={0}, use_global_device_ids=true | all-gather | bytes 1088 | tf_op jit(solution)/shard_map/all_gather | solution.py:41
  32.7 0.1 copy.35
  32.8 0.1 copy.36
  32.9 0.1 copy.37
  33.0 19.8 %all_gather.15 = bf16[128,3072]{1,0:T(8,128)(2,1)S(1)} all-gather(bf16[8,3072]{1,0:T(8,128)(2,1)} %param.7), channel_id=1, replica_groups=mesh['parts'=2,'dev'=16] {'dev'}, dimensions={0}, use_global_device_ids=true | all-gather | bytes 835584 | tf_op jit(solution)/shard_map/all_gather | solution.py:38
  52.9 0.1 select_reduce_fusion
  53.0 0.0 copy-start.4
  53.0 0.6 copy-done.4
  53.6 1.1 convolution_convert_fusion.2
  54.7 1.1 reshape.76
  55.8 20.6 %all-gather.1 = f32[16,8,2]{1,2,0:T(2,128)} all-gather(f32[1,8,2]{1,2,0:T(2,128)} %bitcast.98), channel_id=1, replica_groups=mesh['parts'=2,'dev'=16] {'dev'}, dimensions={0}, use_global_device_ids=true | all-gather | bytes 1088 | tf_op jit(solution)/shard_map/all_gather | solution.py:42
  76.4 1.4 copy.38
  77.7 1.3 fusion.19
  79.0 1.4 copy.48
  80.5 1.1 fusion.6
  81.6 0.7 multiply_reduce_fusion.1
  82.4 0.1 mul.62
  82.4 19.8 %all_gather.14 = bf16[128,3072]{1,0:T(8,128)(2,1)S(1)} all-gather(bf16[8,3072]{1,0:T(8,128)(2,1)} %param.8), channel_id=1, replica_groups=mesh['parts'=2,'dev'=16] {'dev'}, dimensions={0}, use_global_device_ids=true | all-gather | bytes 835584 | tf_op jit(solution)/shard_map/all_gather | solution.py:39
  102.3 2.0 multiply_convert_fusion
  104.3 1.8 reshape.57
  106.1 0.7 fusion.1
  106.8 0.7 copy-done.2
  107.5 0.1 copy-done.3
  107.6 1.3 fusion.22
  108.9 0.6 copy-done.5
  109.5 0.0 copy-done.6
  109.5 2.0 convolution_bitcast_fusion.1
  111.4 2.3 %reshape.60 = f32[16,4,3072]{2,1,0:T(4,128)} reshape(f32[64,3072]{1,0:T(8,128)} %convolution_bitcast_fusion.1) | data formatting | bytes 1572864 | tf_op jit(solution)/shard_map/reshape | solution.py:90
  113.7 4.0 %convolution_bitcast_fusion = f32[128,3072]{1,0:T(8,128)} fusion(f32[16,4,8]{2,1,0:T(4,128)} %copy-done.4, f32[16,4,3072]{2,1,0:T(4,128)} %reshape.60), kind=kOutput, calls=%fused_computation.2 | convolution fusion | flops 18874368 | bytes 2361344 | tf_op jit(solution)/shard_map/nmt,nmd->ntd/dot_general | solution.py:92
  117.7 0.0 reduce-scatter.2.cloned.1.call-update
  117.8 0.1 copy.41
  117.9 0.7 reshape.78
  118.6 1.2 dynamic-slice
  120.5 1.0 fusion.33
  121.5 0.7 multiply_bitcast_fusion
  122.2 60.8 %all-reduce = f32[128,4]{1,0:T(8,128)} all-reduce(f32[128,4]{1,0:T(8,128)} %multiply_bitcast_fusion), channel_id=3, replica_groups=mesh['parts'=2,'dev'=16] {'dev'}, use_global_device_ids=true, to_apply=%region_6.7.clone | all-reduce | flops 512 | bytes 4096
  183.1 0.7 constant_dynamic-slice_fusion
  183.8 0.2 fusion.23
  184.0 0.7 copy.57
  184.6 1.8 convolution_convert_fusion
  186.4 20.6 %copy.42 = bf16[3072,2,256]{2,1,0:T(2,128)(2,1)} copy(bf16[3072,2,256]{2,0,1:T(8,128)(2,1)S(1)} %convolution_convert_fusion) | data formatting | bytes 6291456
  207.0 0.8 convert_element_type.62
  207.8 2.8 %convolution_convert_fusion.1 = bf16[256,3072]{1,0:T(8,128)(2,1)} fusion(bf16[64,3072]{1,0:T(8,128)(2,1)} %convert_element_type.62, f32[64,2,256]{2,0,1:T(8,128)} %copy-done.8), kind=kOutput, calls=%fused_computation.1 | convolution fusion | flops 101548032 | bytes 2097152 | tf_op jit(solution)/shard_map/rh,rd->hd/dot_general | solution.py:85
  210.7 1.5 convert_element_type.54
  (22 shorter events, 0.1 us)
Async XLA Ops:
  7.2 99.0 %copy-start = (bf16[3072,2,256]{2,1,0:T(2,128)(2,1)S(1)}, bf16[3072,2,256]{2,1,0:T(2,128)(2,1)}, u32[]{:S(2)}) copy-start(bf16[3072,2,256]{2,1,0:T(2,128)(2,1)} %param.12) | copy-start | bytes 9437188
  7.2 203.5 %reduce-scatter.2.cloned.1.call-start = ((), (), s32[]{:S(2)}) async-start(), calls=%async_computation.1 | async-start | bytes 1671168 | tf_op jit(solution)/shard_map/reduce_scatter | solution.py:91
  9.3 43.7 %copy-start.9 = (f32[4]{0:T(128)}, f32[4]{0:T(128)S(1)}, u32[]{:S(2)}) copy-start(f32[4]{0:T(128)S(1)} %compare_convert_fusion) | copy-start | bytes 52
  32.9 20.1 %copy-start.7 = (s32[16,4,8]{2,1,0:T(4,128)}, s32[16,4,8]{2,1,0:T(4,128)S(1)}, u32[]{:S(2)}) copy-start(s32[16,4,8]{2,1,0:T(4,128)S(1)} %copy.36) | copy-start | bytes 6148
  53.0 0.6 copy-start.4
  106.1 1.4 copy-start.2
  106.1 1.5 copy-start.3
  107.6 1.3 copy-start.8
  108.9 0.6 copy-start.5
  108.9 0.6 copy-start.6
  111.4 6.3 %copy-start.11 = (s32[8,2]{0,1:T(2,128)S(1)}, s32[8,2]{0,1:T(2,128)}, u32[]{:S(2)}) copy-start(s32[8,2]{0,1:T(2,128)} %param.9) | copy-start | bytes 196
  111.4 10.1 %copy-start.10 = (f32[4]{0:T(128)S(1)}, f32[4]{0:T(128)}, u32[]{:S(2)}) copy-start(f32[4]{0:T(128)} %copy-done.9) | copy-start | bytes 52
  186.4 20.6 %copy-start.1 = (bf16[16,4,3072]{2,1,0:T(4,128)(2,1)S(1)}, bf16[16,4,3072]{2,1,0:T(4,128)(2,1)}, u32[]{:S(2)}) copy-start(bf16[16,4,3072]{2,1,0:T(4,128)(2,1)} %get-tuple-element.23) | copy-start | bytes 1179652
Sparse Core Ops, SparseCore 0:
  117.9 58.1 reduce-scatter.1
where the time goes:
time: 220 us; the launch traced here: 219 us
  blocking collectives  144 us (65%)
  local copies, waits for them, and re-layouts  35.2 us (16%)
  matrix products  18 us (8%)
  between operations  14.8 us (7%)
  other arithmetic  6.54 us (3%)
    unnamed x1, blocking collectives  60.8 us
    unnamed x28, local copies, waits for them, and re-layouts  24.7 us
    all_gather x1, blocking collectives, shards(): ids_all = lax.all_gather(expert_ids, 'dev', axis=0, tiled=True)  23.4 us
    all_gather x1, blocking collectives, shards(): probs_all = lax.all_gather(gate_probs, 'dev', axis=0, tiled=True)  20.6 us
    all_gather x1, blocking collectives, shards(): lax.all_gather(tokens, 'dev', axis=0, tiled=True)  19.8 us
    all_gather x1, blocking collectives, shards(): lax.all_gather(grad_out, 'dev', axis=0, tiled=True)  19.8 us
  transfers between devices with their start and end apart: 1, of which 0 were waited for; matrix products, arithmetic and copies ran while one was open for 14% of the time, Pallas kernels for 0%

commit v1 on v0

v1 whole, which is shorter than its diff:
```python
import functools

import jax
import jax.numpy as jnp
from jax import lax
from jax.experimental import pallas as pl
from jax.experimental.pallas import tpu as pltpu
from jax.sharding import PartitionSpec as P

EXP_WIN = 4
META = 128
BF = jnp.bfloat16
F32 = jnp.float32
VMEM = pl.BlockSpec(memory_space=pltpu.VMEM)
SMEM = pl.BlockSpec(memory_space=pltpu.SMEM)
NT = (((1,), (1,)), ((), ()))
TN = (((0,), (0,)), ((), ()))


def params():
    return pltpu.CompilerParams(vmem_limit_bytes=48 << 20)


def xor_swap(value, bit):
    n = lax.axis_size("dev")
    return lax.ppermute(value, "dev", [(i, i ^ bit) for i in range(n)])


def xor_bits(n):
    bits = []
    bit = n // 2
    while bit:
        bits.append(bit)
        bit //= 2
    return bits


def pack_kernel(tok_ref, grad_ref, ids_ref, prob_ref, out_ref):
    rows, width = tok_ref.shape
    out_ref[:, :width] = tok_ref[...]
    out_ref[:, width : 2 * width] = grad_ref[...]
    top = ids_ref.shape[0]
    diag = lax.broadcasted_iota(jnp.int32, (rows, rows), 0) == lax.broadcasted_iota(
        jnp.int32, (rows, rows), 1
    )
    lane = lax.broadcasted_iota(jnp.int32, (rows, META), 1)
    expert = lane % EXP_WIN
    flag = jnp.zeros((rows, META), F32)
    prob = jnp.zeros((rows, META), F32)
    for k in range(top):
        ids = jnp.broadcast_to(ids_ref[k : k + 1, :].astype(F32), (rows, rows))
        val = jnp.broadcast_to(prob_ref[k : k + 1, :], (rows, rows))
        ids = jnp.sum(jnp.where(diag, ids, 0.0), 1, keepdims=True)
        val = jnp.sum(jnp.where(diag, val, 0.0), 1, keepdims=True)
        hit = expert.astype(F32) == ids
        flag = jnp.where(hit, 1.0, flag)
        prob = prob + jnp.where(hit, val, 0.0)
    high = prob.astype(BF).astype(F32)
    mid = (prob - high).astype(BF).astype(F32)
    low = prob - high - mid
    part = lane // EXP_WIN
    meta = jnp.where(part == 0, flag, 0.0)
    meta = jnp.where(part == 1, high, meta)
    meta = jnp.where(part == 2, mid, meta)
    meta = jnp.where(part == 3, low, meta)
    out_ref[:, 2 * width :] = meta.astype(BF)


def split_kernel(w_ref, out_ref):
    hid = w_ref.shape[2]
    block = w_ref[...]
    out_ref[:, :hid] = block[:, 0, :]
    out_ref[:, hid:] = block[:, 1, :]


def split_weights(w_in, block=512):
    d, two, hid = w_in.shape
    return pl.pallas_call(
        split_kernel,
        grid=(d // block,),
        in_specs=[pl.BlockSpec((block, two, hid), lambda i: (i, 0, 0))],
        out_specs=pl.BlockSpec((block, two * hid), lambda i: (i, 0)),
        out_shape=jax.ShapeDtypeStruct((d, two * hid), BF),
        compiler_params=params(),
        cost_estimate=pl.CostEstimate(
            flops=0, bytes_accessed=30 * d * two * hid, transcendentals=0
        ),
    )(w_in)


def put_gate(out_ref, value, expert, width):
    rows = value.shape[0]
    lane = lax.broadcasted_iota(jnp.int32, (rows, META), 1)
    high = value.astype(BF).astype(F32)
    low = value - high
    pair = jnp.where(lane == expert, high, 0.0)
    pair = jnp.where(lane == expert + EXP_WIN, low, pair)
    out_ref[:, width:] = pair.astype(out_ref.dtype)


def token_part(pre, w_ref, out_ref, width, step=768):
    for c in range(0, width, step):
        out_ref[:, c : c + step] = lax.dot_general(
            pre, w_ref[c : c + step, :], NT, preferred_element_type=F32
        ).astype(out_ref.dtype)


def main_kernel(n, owner_ref, me_ref, *refs):
    pieces, refs = refs[:n], refs[n:]
    w_ref, down_ref, tok_ref, scaled_ref, pre_ref, hid_ref, gate_ref, send_ref, grad_ref = refs
    rows = pieces[0].shape[0]
    width = down_ref.shape[1]
    hid = down_ref.shape[0]
    expert = owner_ref[me_ref[0]]
    metas = []
    for i in range(0, n, 2):
        pair = [pieces[i][...].astype(F32), pieces[i + 1][...].astype(F32)]
        both = jnp.concatenate(pair, 0)
        here = pl.ds(i * rows, 2 * rows)
        tok_ref[here, :] = both[:, :width].astype(BF)
        grad_ref[here, :] = both[:, width : 2 * width].astype(BF)
        metas.append(both[:, 2 * width :])
    meta = jnp.concatenate(metas, 0)
    lane = lax.broadcasted_iota(jnp.int32, meta.shape, 1)
    routed = jnp.sum(jnp.where(lane == expert, meta, 0.0), 1, keepdims=True)
    prob = jnp.sum(
        jnp.where((lane >= EXP_WIN) & (lane % EXP_WIN == expert), meta, 0.0), 1, keepdims=True
    )
    projected = jnp.dot(tok_ref[...], w_ref[...], preferred_element_type=F32)
    gate, up = projected[:, :hid], projected[:, hid:]
    back = lax.dot_general(grad_ref[...], down_ref[...], NT, preferred_element_type=F32)
    logistic = jax.nn.sigmoid(gate)
    activated = gate * logistic
    hidden = (activated * up).astype(BF)
    hid_ref[...] = hidden
    gate_sum = routed * jnp.sum(hidden.astype(F32) * back, 1, keepdims=True)
    hidden_grad = prob * back
    pre_gate = hidden_grad * up * logistic * (1.0 + gate * (1.0 - logistic))
    pre_ref[:, :hid] = pre_gate.astype(BF)
    pre_ref[:, hid:] = (hidden_grad * activated).astype(BF)
    gate_ref[...] = jnp.broadcast_to(gate_sum, gate_ref.shape)
    half = n * rows // 2
    put_gate(send_ref, gate_sum[half:], expert, width)
    token_part(pre_ref[half:, :], w_ref, send_ref, width)
    scaled_ref[...] = (prob * grad_ref[...].astype(F32)).astype(BF)


def own_kernel(owner_ref, me_ref, pre_ref, w_ref, gate_ref, out_ref):
    half = out_ref.shape[0]
    width = w_ref.shape[0]
    put_gate(out_ref, gate_ref[:half, :1], owner_ref[me_ref[0]], width)
    token_part(pre_ref[:half, :], w_ref, out_ref, width)


def add_kernel(own_ref, got_ref, keep_ref, send_ref=None):
    total = own_ref[...] + got_ref[...].astype(F32)
    half = keep_ref.shape[0]
    width = total.shape[1] - META
    keep_ref[...] = total[:half]
    if send_ref is not None:
        send_ref[:, :width] = total[half:, :width].astype(BF)
        tail = total[half:, width:]
        lane = lax.broadcasted_iota(jnp.int32, tail.shape, 1)
        value = tail + pltpu.roll(tail, META - EXP_WIN, 1)
        high = value.astype(BF).astype(F32)
        low = pltpu.roll(value - high, EXP_WIN, 1)
        pair = jnp.where(lane < EXP_WIN, high, jnp.where(lane < 2 * EXP_WIN, low, 0.0))
        send_ref[:, width:] = pair.astype(BF)


def add_step(own, got):
    rows, width = own.shape
    half = rows // 2
    return pl.pallas_call(
        add_kernel,
        in_specs=[VMEM, VMEM],
        out_specs=[VMEM, VMEM],
        out_shape=[
            jax.ShapeDtypeStruct((half, width), F32),
            jax.ShapeDtypeStruct((half, width), BF),
        ],
        compiler_params=params(),
        cost_estimate=pl.CostEstimate(
            flops=rows * width, bytes_accessed=8 * rows * width, transcendentals=0
        ),
    )(own, got)


def last_kernel(own_ref, got_ref, ids_ref, tok_ref, gates_ref):
    total = own_ref[...] + got_ref[...].astype(F32)
    rows = total.shape[0]
    width = total.shape[1] - META
    tok_ref[...] = total[:, :width].astype(BF)
    tail = total[:, width:]
    value = tail + pltpu.roll(tail, META - EXP_WIN, 1)
    lane = lax.broadcasted_iota(jnp.int32, (rows, META), 1)
    diag = lax.broadcasted_iota(jnp.int32, (rows, rows), 0) == lax.broadcasted_iota(
        jnp.int32, (rows, rows), 1
    )
    for k in range(ids_ref.shape[0]):
        ids = jnp.broadcast_to(ids_ref[k : k + 1, :].astype(F32), (rows, rows))
        ids = jnp.sum(jnp.where(diag, ids, 0.0), 1, keepdims=True)
        hit = (lane.astype(F32) == ids) & (lane < EXP_WIN)
        column = jnp.sum(jnp.where(hit, value, 0.0), 1, keepdims=True)
        square = jnp.where(diag, jnp.broadcast_to(column, (rows, rows)), 0.0)
        gates_ref[k : k + 1, :] = jnp.sum(square, 0, keepdims=True)


def win_kernel(tok_ref, pre_ref, out_ref):
    hid = out_ref.shape[2]
    block = lax.dot_general(tok_ref[...], pre_ref[...], TN, preferred_element_type=F32)
    out_ref[:, 0, :] = block[:, :hid].astype(BF)
    out_ref[:, 1, :] = block[:, hid:].astype(BF)


def grad_in(tok, pre, block=256):
    rows, d = tok.shape
    hid = pre.shape[1] // 2
    return pl.pallas_call(
        win_kernel,
        grid=(d // block,),
        in_specs=[
            pl.BlockSpec((rows, block), lambda i: (0, i)),
            pl.BlockSpec((rows, 2 * hid), lambda i: (0, 0)),
        ],
        out_specs=pl.BlockSpec((block, 2, hid), lambda i: (i, 0, 0)),
        out_shape=jax.ShapeDtypeStruct((d, 2, hid), BF),
        compiler_params=params(),
        cost_estimate=pl.CostEstimate(
            flops=4 * rows * d * hid, bytes_accessed=30 * d * hid, transcendentals=0
        ),
    )(tok, pre)


def down_kernel(hid_ref, scaled_ref, out_ref):
    out_ref[...] = lax.dot_general(
        hid_ref[...], scaled_ref[...], TN, preferred_element_type=F32
    ).astype(BF)


def grad_down(hidden, scaled, block=768):
    rows, d = scaled.shape
    hid = hidden.shape[1]
    return pl.pallas_call(
        down_kernel,
        grid=(d // block,),
        in_specs=[
            pl.BlockSpec((rows, hid), lambda i: (0, 0)),
            pl.BlockSpec((rows, block), lambda i: (0, i)),
        ],
        out_specs=pl.BlockSpec((hid, block), lambda i: (0, i)),
        out_shape=jax.ShapeDtypeStruct((hid, d), BF),
        compiler_params=params(),
        cost_estimate=pl.CostEstimate(
            flops=2 * rows * d * hid, bytes_accessed=4 * d * hid, transcendentals=0
        ),
    )(hidden, scaled)


def shards(tokens, grad_out, expert_ids, gate_probs, device_expert, w_in, w_down):
    n = lax.axis_size("dev")
    me = lax.axis_index("dev").astype(jnp.int32).reshape(1)
    rows, width = tokens.shape
    hid = w_down.shape[0]
    ids_t = expert_ids.T
    probs_t = gate_probs.T
    bits = xor_bits(n)

    own = pl.pallas_call(
        pack_kernel,
        in_specs=[VMEM] * 4,
        out_specs=VMEM,
        out_shape=jax.ShapeDtypeStruct((rows, 2 * width + META), BF),
        compiler_params=params(),
    )(tokens, grad_out, ids_t, probs_t)

    held = {0: own}
    order = [0]
    for bit in bits:
        for o in order:
            held[o ^ bit] = xor_swap(held[o], bit)
        order = order + [o ^ bit for o in order]

    w_flat = split_weights(w_in)
    total = n * rows
    half = total // 2
    tok, scaled, pre, hidden, gate, send = pl.pallas_call(
        functools.partial(main_kernel, n),
        in_specs=[SMEM, SMEM] + [VMEM] * (n + 2),
        out_specs=[VMEM] * 6,
        out_shape=[
            jax.ShapeDtypeStruct((total, width), BF),
            jax.ShapeDtypeStruct((total, width), BF),
            jax.ShapeDtypeStruct((total, 2 * hid), BF),
            jax.ShapeDtypeStruct((total, hid), BF),
            jax.ShapeDtypeStruct((total, META), F32),
            jax.ShapeDtypeStruct((half, width + META), BF),
        ],
        scratch_shapes=[pltpu.VMEM((total, width), BF)],
        compiler_params=params(),
    )(device_expert, me, *[held[o] for o in order], w_flat, w_down)

    got = xor_swap(send, 1)
    mine = pl.pallas_call(
        own_kernel,
        in_specs=[SMEM, SMEM] + [VMEM] * 3,
        out_specs=VMEM,
        out_shape=jax.ShapeDtypeStruct((half, width + META), F32),
        compiler_params=params(),
    )(device_expert, me, pre, w_flat, gate)
    for bit in bits[-2::-1]:
        mine, send = add_step(mine, got)
        got = xor_swap(send, bit)

    grad_w_down = grad_down(hidden, scaled)
    grad_w_in = grad_in(tok, pre)
    grad_tokens, gates_t = pl.pallas_call(
        last_kernel,
        in_specs=[VMEM] * 3,
        out_specs=[VMEM] * 2,
        out_shape=[
            jax.ShapeDtypeStruct((rows, width), BF),
            jax.ShapeDtypeStruct((expert_ids.shape[1], rows), F32),
        ],
        compiler_params=params(),
    )(mine, got, ids_t)
    return grad_tokens, gates_t.T, grad_w_in, grad_w_down


def solution(mesh):
    return jax.shard_map(
        shards,
        mesh=mesh,
        in_specs=(
            P(("parts", "dev"), None),
            P(("parts", "dev"), None),
            P(("parts", "dev"), None),
            P(("parts", "dev"), None),
            P(),
            P(None, None, "dev"),
            P("dev", None),
        ),
        out_specs=(
            P(("parts", "dev"), None),
            P(("parts", "dev"), None),
            P("parts", None, "dev"),
            P(("parts", "dev"), None),
        ),
        check_vma=False,
    )
```

time: 220 us -> 66.4 us (0.30)
  blocking collectives: 144 us -> 0 us
  local copies, waits for them, and re-layouts: 35.2 us -> 4.62 us
  Pallas kernels: 0 us -> 25.3 us
  matrix products: 18 us -> 0 us
  waiting for transfers between devices: 0.02 us -> 17.8 us
  starting transfers between devices: 0.04 us -> 17.6 us
  between operations: 14.8 us -> 0.75 us
  other arithmetic: 6.54 us -> 0 us
    all_gather x4 -> x0, blocking collectives: 83.6 us -> none  [the longest x1 23.4 us: shards(): ids_all = lax.all_gather(expert_ids, 'dev', axis=0, tiled=True)]
    unnamed x1 -> x0, blocking collectives: 60.8 us -> none
    pallas_call x0 -> x10, Pallas kernels: none -> 25.3 us  [the longest x1 7.68 us: grad_in(): pl.pallas_call(win_kernel, grid=(d // block,), in_specs=[pl.BlockSpec((ro...]
    unnamed x28 -> x18, local copies, waits for them, and re-layouts: 24.7 us -> 4.62 us
    dot_general x11 -> x0, matrix products: 18 us -> none  [the longest x1 4.02 us: shards(): jnp.einsum('nmt,nmd->ntd', select_mine, token_part, precision=HIGHEST)]
    ppermute x0 -> x19, waiting for transfers between devices: none -> 17.8 us  [xor_swap(): return lax.ppermute(value, 'dev', [(i, i ^ bit) for i in range(n)])]
    ppermute x0 -> x19, starting transfers between devices: none -> 17.6 us  [xor_swap(): return lax.ppermute(value, 'dev', [(i, i ^ bit) for i in range(n)])]
    reshape x4 -> x0, local copies, waits for them, and re-layouts: 5.91 us -> none  [the longest x1 2.26 us: shards(): token_part = jnp.einsum('rkh,dkh->rd', pre_grads, w_in, preferred_element...]
  transfers between devices with their start and end apart: 1 -> 19, of which waited for: 0 -> 8; matrix products, arithmetic and copies ran while one was open for 14% -> 0% of each run, Pallas kernels for 0% -> 29%
where the time goes in v1:
time: 66.4 us; the launch traced here: 66 us
  Pallas kernels  25.3 us (38%)
  waiting for transfers between devices  17.8 us (27%)
  starting transfers between devices  17.6 us (27%)
  local copies, waits for them, and re-layouts  4.62 us (7%)
  between operations  0.75 us (1%)
    ppermute x19, waiting for transfers between devices, xor_swap(): return lax.ppermute(value, 'dev', [(i, i ^ bit) for i in range(n)])  17.8 us
    ppermute x19, starting transfers between devices, xor_swap(): return lax.ppermute(value, 'dev', [(i, i ^ bit) for i in range(n)])  17.6 us
    pallas_call x1, Pallas kernels, grad_in(): pl.pallas_call(win_kernel, grid=(d // block,), in_specs=[pl.BlockSpec((ro...  7.68 us
    pallas_call x1, Pallas kernels, split_weights(): pl.pallas_call(split_kernel, grid=(d // block,), in_specs=[pl.BlockSpec((...  7.38 us
    pallas_call x1, Pallas kernels, shards(): pl.pallas_call(functools.partial(main_kernel, n), in_specs=[SMEM, SMEM] +...  4.92 us
    unnamed x18, local copies, waits for them, and re-layouts  4.62 us
    pallas_call x1, Pallas kernels, grad_down(): pl.pallas_call(down_kernel, grid=(d // block,), in_specs=[pl.BlockSpec((r...  2.42 us
    pallas_call x1, Pallas kernels, shards(): pl.pallas_call(own_kernel, in_specs=[SMEM, SMEM] + [VMEM] * 3, out_specs=...  1.6 us
  transfers between devices with their start and end apart: 19, of which 8 were waited for; matrix products, arithmetic and copies ran while one was open for 0% of the time, Pallas kernels for 29%

profile of v1, /device:TPU:0, one launch (start us, length us, event | category | flops | bytes accessed | tf_op | source)
XLA Modules:
  0.0 66.0 jit_solution(6433174957108129046)
XLA Ops:
  0.6 0.8 %copy-done.3 = bf16[8,3072]{1,0:T(8,128)(2,1)S(1)} copy-done((bf16[8,3072]{1,0:T(8,128)(2,1)S(1)}, bf16[8,3072]{1,0:T(8,128)(2,1)}, u32[]{:S(2)}) %copy-start.3) | copy-done | bytes 49176
  1.4 0.8 %copy-done.4 = bf16[8,3072]{1,0:T(8,128)(2,1)S(1)} copy-done((bf16[8,3072]{1,0:T(8,128)(2,1)S(1)}, bf16[8,3072]{1,0:T(8,128)(2,1)}, u32[]{:S(2)}) %copy-start.4) | copy-done | bytes 49176
  2.2 0.7 %copy-done.5 = s32[8,2]{0,1:T(2,128)S(1)} copy-done((s32[8,2]{0,1:T(2,128)S(1)}, s32[8,2]{0,1:T(2,128)}, u32[]{:S(2)}) %copy-start.5) | copy-done | bytes 88
  2.9 0.7 %copy-done.8 = f32[8,2]{0,1:T(2,128)S(1)} copy-done((f32[8,2]{0,1:T(2,128)S(1)}, f32[8,2]{0,1:T(2,128)}, u32[]{:S(2)}) %copy-start.8) | copy-done | bytes 88
  3.6 0.1 shard_map.102.refs_0_
  3.7 4.1 %collective-permute-start = (bf16[8,6272]{1,0:T(8,128)(2,1)S(1)}, bf16[8,6272]{1,0:T(8,128)(2,1)S(1)}, u32[]{:S(2)}, u32[]{:S(2)}) collective-permute-start(bf16[8,6272]{1,0:T(8,128)(2,1)S(1)} %shard_map.102.refs_0_), channel_id=1, source_target_pairs={{0,8},{1,9},{2,10},{3,11},{4,12},{5,13},{6,14},{7,15},{8,0},{9,1},... | collective-permute-start | bytes 301064 | tf_op jit(solution)/shard_map/ppermute | solution.py:26
  7.8 1.5 %collective-permute-start.3 = (bf16[8,6272]{1,0:T(8,128)(2,1)S(1)}, bf16[8,6272]{1,0:T(8,128)(2,1)S(1)}, u32[]{:S(2)}, u32[]{:S(2)}) collective-permute-start(bf16[8,6272]{1,0:T(8,128)(2,1)S(1)} %shard_map.102.refs_0_), channel_id=1, source_target_pairs={{0,2},{1,3},{2,0},{3,1},{4,6},{5,7},{6,4},{7,5},{8,10},{9,11},{10,... | collective-permute-start | bytes 301064 | tf_op jit(solution)/shard_map/ppermute | solution.py:26
  9.3 1.6 %collective-permute-start.1 = (bf16[8,6272]{1,0:T(8,128)(2,1)S(1)}, bf16[8,6272]{1,0:T(8,128)(2,1)S(1)}, u32[]{:S(2)}, u32[]{:S(2)}) collective-permute-start(bf16[8,6272]{1,0:T(8,128)(2,1)S(1)} %shard_map.102.refs_0_), channel_id=1, source_target_pairs={{0,4},{1,5},{2,6},{3,7},{4,0},{5,1},{6,2},{7,3},{8,12},{9,13},{10,... | collective-permute-start | bytes 301064 | tf_op jit(solution)/shard_map/ppermute | solution.py:26
  10.9 0.0 collective-permute-start.7
  10.9 2.0 %collective-permute-done.refs_1_ = bf16[8,6272]{1,0:T(8,128)(2,1)S(1)} collective-permute-done((bf16[8,6272]{1,0:T(8,128)(2,1)S(1)}, bf16[8,6272]{1,0:T(8,128)(2,1)S(1)}, u32[]{:S(2)}, u32[]{:S(2)}) %collective-permute-start) | collective-permute-done | bytes 100384 | tf_op jit(solution)/shard_map/ppermute | solution.py:26
  12.9 0.7 %collective-permute-start.2 = (bf16[8,6272]{1,0:T(8,128)(2,1)S(1)}, bf16[8,6272]{1,0:T(8,128)(2,1)S(1)}, u32[]{:S(2)}, u32[]{:S(2)}) collective-permute-start(bf16[8,6272]{1,0:T(8,128)(2,1)S(1)} %collective-permute-done.refs_1_), channel_id=1, source_target_pairs={{0,4},{1,5},{2,6},{3,7},{4,0},{5,1},{6,2},{7,3},{8,12},{9,13},{10,... | collective-permute-start | bytes 301064 | tf_op jit(solution)/shard_map/ppermute | solution.py:26
  13.5 0.0 collective-permute-done.3.refs_4_
  13.5 0.7 %collective-permute-done.1.refs_2_ = bf16[8,6272]{1,0:T(8,128)(2,1)S(1)} collective-permute-done((bf16[8,6272]{1,0:T(8,128)(2,1)S(1)}, bf16[8,6272]{1,0:T(8,128)(2,1)S(1)}, u32[]{:S(2)}, u32[]{:S(2)}) %collective-permute-start.1) | collective-permute-done | bytes 100384 | tf_op jit(solution)/shard_map/ppermute | solution.py:26
  14.2 1.3 %collective-permute-start.5 = (bf16[8,6272]{1,0:T(8,128)(2,1)S(1)}, bf16[8,6272]{1,0:T(8,128)(2,1)S(1)}, u32[]{:S(2)}, u32[]{:S(2)}) collective-permute-start(bf16[8,6272]{1,0:T(8,128)(2,1)S(1)} %collective-permute-done.1.refs_2_), channel_id=1, source_target_pairs={{0,2},{1,3},{2,0},{3,1},{4,6},{5,7},{6,4},{7,5},{8,10},{9,11},{10,... | collective-permute-start | bytes 301064 | tf_op jit(solution)/shard_map/ppermute | solution.py:26
  15.5 0.7 %collective-permute-start.4 = (bf16[8,6272]{1,0:T(8,128)(2,1)S(1)}, bf16[8,6272]{1,0:T(8,128)(2,1)S(1)}, u32[]{:S(2)}, u32[]{:S(2)}) collective-permute-start(bf16[8,6272]{1,0:T(8,128)(2,1)S(1)} %collective-permute-done.refs_1_), channel_id=1, source_target_pairs={{0,2},{1,3},{2,0},{3,1},{4,6},{5,7},{6,4},{7,5},{8,10},{9,11},{10,... | collective-permute-start | bytes 301064 | tf_op jit(solution)/shard_map/ppermute | solution.py:26
  16.3 1.2 %collective-permute-done.2.refs_3_ = bf16[8,6272]{1,0:T(8,128)(2,1)S(1)} collective-permute-done((bf16[8,6272]{1,0:T(8,128)(2,1)S(1)}, bf16[8,6272]{1,0:T(8,128)(2,1)S(1)}, u32[]{:S(2)}, u32[]{:S(2)}) %collective-permute-start.2) | collective-permute-done | bytes 100384 | tf_op jit(solution)/shard_map/ppermute | solution.py:26
  17.5 1.6 %collective-permute-start.6 = (bf16[8,6272]{1,0:T(8,128)(2,1)S(1)}, bf16[8,6272]{1,0:T(8,128)(2,1)S(1)}, u32[]{:S(2)}, u32[]{:S(2)}) collective-permute-start(bf16[8,6272]{1,0:T(8,128)(2,1)S(1)} %collective-permute-done.2.refs_3_), channel_id=1, source_target_pairs={{0,2},{1,3},{2,0},{3,1},{4,6},{5,7},{6,4},{7,5},{8,10},{9,11},{10,... | collective-permute-start | bytes 301064 | tf_op jit(solution)/shard_map/ppermute | solution.py:26
  19.1 0.0 collective-permute-start.8
  19.1 0.0 collective-permute-done.9.refs_10_
  19.1 0.5 collective-permute-start.10
  19.6 0.3 collective-permute-done.5.refs_6_
  19.9 0.0 collective-permute-start.13
  19.9 2.1 %collective-permute-done.4.refs_5_ = bf16[8,6272]{1,0:T(8,128)(2,1)S(1)} collective-permute-done((bf16[8,6272]{1,0:T(8,128)(2,1)S(1)}, bf16[8,6272]{1,0:T(8,128)(2,1)S(1)}, u32[]{:S(2)}, u32[]{:S(2)}) %collective-permute-start.4) | collective-permute-done | bytes 100384 | tf_op jit(solution)/shard_map/ppermute | solution.py:26
  22.0 0.0 collective-permute-start.12
  22.0 1.8 %collective-permute-done.6.refs_7_ = bf16[8,6272]{1,0:T(8,128)(2,1)S(1)} collective-permute-done((bf16[8,6272]{1,0:T(8,128)(2,1)S(1)}, bf16[8,6272]{1,0:T(8,128)(2,1)S(1)}, u32[]{:S(2)}, u32[]{:S(2)}) %collective-permute-start.6) | collective-permute-done | bytes 100384 | tf_op jit(solution)/shard_map/ppermute | solution.py:26
  23.8 0.0 collective-permute-start.14
  23.8 7.4 %shard_map.103.refs_16_.w_ref = bf16[3072,512]{1,0:T(8,128)(2,1)S(1)} custom-call(bf16[3072,2,256]{2,1,0:T(2,128)(2,1)} %w_ref.1), custom_call_target="tpu_custom_call" | custom-call | bytes 47185920 | tf_op jit(solution)/shard_map/pallas_call | solution.py:78
  31.2 0.0 copy-start
  31.2 1.7 %copy-done = bf16[3072,512]{1,0:T(8,128)(2,1)} copy-done((bf16[3072,512]{1,0:T(8,128)(2,1)}, bf16[3072,512]{1,0:T(8,128)(2,1)S(1)}, u32[]{:S(2)}) %copy-start) | copy-done | bytes 3145752
  32.9 0.0 collective-permute-done.8.refs_9_
  32.9 0.0 collective-permute-done.13.refs_14_
  32.9 0.0 collective-permute-done.12.refs_13_
  32.9 0.0 copy-start.1
  32.9 4.9 %shard_map.104 = (bf16[128,3072]{1,0:T(8,128)(2,1)S(1)}, bf16[128,3072]{1,0:T(8,128)(2,1)S(1)}, bf16[128,512]{1,0:T(8,128)(2,1)S(1)}, bf16[128,256]{1,0:T(8,128)...) custom-call(s32[16]{0:T(128)S(1)} %copy-done.7, s32[1]{0:T(128)} %bitcast.me_ref, ...), custom_call_target="tpu_custom_call" | custom-call | tf_op jit(solution)/shard_map/pallas_call | solution.py:287
  37.9 0.6 collective-permute-start.15
  38.4 1.6 %shard_map.105.own_ref = f32[64,3200]{1,0:T(8,128)S(1)} custom-call(s32[16]{0:T(128)S(1)} %copy-done.7, s32[1]{0:T(128)} %bitcast.me_ref, bf16[128,512]{1,0:T(8,128)(2,1)S(1)} %get-tuple-element.18.pre_ref, bf16[3072,512]{1,0:T(8,128)(2,1)S(1)} %copy-done.1, f32[128,128]{1,0:T(8,128)S(1)} %get-tuple-element.19.gate_ref), custom_call_target="tpu_custom_call" | custom-call | tf_op jit(solution)/shard_map/pallas_call | solution.py:304
  40.0 0.0 collective-permute-done.15.got_ref
  40.0 0.2 shard_map.106
  40.2 0.9 %collective-permute-start.16 = (bf16[32,3200]{1,0:T(8,128)(2,1)S(1)}, bf16[32,3200]{1,0:T(8,128)(2,1)S(1)}, u32[]{:S(2)}, u32[]{:S(2)}) collective-permute-start(bf16[32,3200]{1,0:T(8,128)(2,1)S(1)} %get-tuple-element.22), channel_id=1, source_target_pairs={{0,2},{1,3},{2,0},{3,1},{4,6},{5,7},{6,4},{7,5},{8,10},{9,11},{10,... | collective-permute-start | bytes 614408 | tf_op jit(solution)/shard_map/ppermute | solution.py:26
  41.1 6.3 %collective-permute-done.16.got_ref = bf16[32,3200]{1,0:T(8,128)(2,1)S(1)} collective-permute-done((bf16[32,3200]{1,0:T(8,128)(2,1)S(1)}, bf16[32,3200]{1,0:T(8,128)(2,1)S(1)}, u32[]{:S(2)}, u32[]{:S(2)}) %collective-permute-start.16) | collective-permute-done | bytes 204832 | tf_op jit(solution)/shard_map/ppermute | solution.py:26
  47.4 0.1 shard_map.107
  47.5 1.3 %collective-permute-start.17 = (bf16[16,3200]{1,0:T(8,128)(2,1)S(1)}, bf16[16,3200]{1,0:T(8,128)(2,1)S(1)}, u32[]{:S(2)}, u32[]{:S(2)}) collective-permute-start(bf16[16,3200]{1,0:T(8,128)(2,1)S(1)} %get-tuple-element.24), channel_id=1, source_target_pairs={{0,4},{1,5},{2,6},{3,7},{4,0},{5,1},{6,2},{7,3},{8,12},{9,13},{10,... | collective-permute-start | bytes 307208 | tf_op jit(solution)/shard_map/ppermute | solution.py:26
  48.8 3.4 %collective-permute-done.17.got_ref = bf16[16,3200]{1,0:T(8,128)(2,1)S(1)} collective-permute-done((bf16[16,3200]{1,0:T(8,128)(2,1)S(1)}, bf16[16,3200]{1,0:T(8,128)(2,1)S(1)}, u32[]{:S(2)}, u32[]{:S(2)}) %collective-permute-start.17) | collective-permute-done | bytes 102432 | tf_op jit(solution)/shard_map/ppermute | solution.py:26
  52.2 0.1 shard_map.108
  52.4 2.8 %collective-permute-start.18 = (bf16[8,3200]{1,0:T(8,128)(2,1)S(1)}, bf16[8,3200]{1,0:T(8,128)(2,1)S(1)}, u32[]{:S(2)}, u32[]{:S(2)}) collective-permute-start(bf16[8,3200]{1,0:T(8,128)(2,1)S(1)} %get-tuple-element.26), channel_id=1, source_target_pairs={{0,8},{1,9},{2,10},{3,11},{4,12},{5,13},{6,14},{7,15},{8,0},{9,1},... | collective-permute-start | bytes 153608 | tf_op jit(solution)/shard_map/ppermute | solution.py:26
  55.2 2.4 %shard_map.111 = bf16[256,3072]{1,0:T(8,128)(2,1)} custom-call(bf16[128,256]{1,0:T(8,128)(2,1)S(1)} %get-tuple-element.30.hid_ref, bf16[128,3072]{1,0:T(8,128)(2,1)S(1)} %get-tuple-element.31.scaled_ref), custom_call_target="tpu_custom_call" | custom-call | flops 201326592 | bytes 3145728 | tf_op jit(solution)/shard_map/pallas_call | solution.py:244
  57.6 7.7 %shard_map.110 = bf16[3072,2,256]{2,1,0:T(2,128)(2,1)} custom-call(bf16[128,3072]{1,0:T(8,128)(2,1)S(1)} %get-tuple-element.29.tok_ref, bf16[128,512]{1,0:T(8,128)(2,1)S(1)} %get-tuple-element.18.pre_ref), custom_call_target="tpu_custom_call" | custom-call | flops 402653184 | bytes 23592960 | tf_op jit(solution)/shard_map/pallas_call | solution.py:219
  65.3 0.7 %shard_map.109 = (bf16[8,3072]{1,0:T(8,128)(2,1)}, f32[2,8]{1,0:T(2,128)}) custom-call(f32[8,3200]{1,0:T(8,128)S(1)} %get-tuple-element.25.own_ref, bf16[8,3200]{1,0:T(8,128)(2,1)S(1)} %collective-permute-done.18.got_ref, s32[2,8]{1,0:T(2,128)S(1)} %bitcast.5), custom_call_target="tpu_custom_call" | custom-call | tf_op jit(solution)/shard_map/pallas_call | solution.py:317
  (18 shorter events, 0.0 us)
Async XLA Ops:
  0.6 0.8 %copy-start.3 = (bf16[8,3072]{1,0:T(8,128)(2,1)S(1)}, bf16[8,3072]{1,0:T(8,128)(2,1)}, u32[]{:S(2)}) copy-start(bf16[8,3072]{1,0:T(8,128)(2,1)} %tok_ref.1) | copy-start | bytes 147460
  1.4 0.8 %copy-start.4 = (bf16[8,3072]{1,0:T(8,128)(2,1)S(1)}, bf16[8,3072]{1,0:T(8,128)(2,1)}, u32[]{:S(2)}) copy-start(bf16[8,3072]{1,0:T(8,128)(2,1)} %grad_ref.1) | copy-start | bytes 147460
  2.2 0.7 %copy-start.5 = (s32[8,2]{0,1:T(2,128)S(1)}, s32[8,2]{0,1:T(2,128)}, u32[]{:S(2)}) copy-start(s32[8,2]{0,1:T(2,128)} %param.9) | copy-start | bytes 196
  2.9 0.7 %copy-start.8 = (f32[8,2]{0,1:T(2,128)S(1)}, f32[8,2]{0,1:T(2,128)}, u32[]{:S(2)}) copy-start(f32[8,2]{0,1:T(2,128)} %param.10) | copy-start | bytes 196
  3.7 9.2 %collective-permute-start = (bf16[8,6272]{1,0:T(8,128)(2,1)S(1)}, bf16[8,6272]{1,0:T(8,128)(2,1)S(1)}, u32[]{:S(2)}, u32[]{:S(2)}) collective-permute-start(bf16[8,6272]{1,0:T(8,128)(2,1)S(1)} %shard_map.102.refs_0_), channel_id=1, source_target_pairs={{0,8},{1,9},{2,10},{3,11},{4,12},{5,13},{6,14},{7,15},{8,0},{9,1},... | collective-permute-start | bytes 301064 | tf_op jit(solution)/shard_map/ppermute | solution.py:26
  7.8 5.8 %collective-permute-start.3 = (bf16[8,6272]{1,0:T(8,128)(2,1)S(1)}, bf16[8,6272]{1,0:T(8,128)(2,1)S(1)}, u32[]{:S(2)}, u32[]{:S(2)}) collective-permute-start(bf16[8,6272]{1,0:T(8,128)(2,1)S(1)} %shard_map.102.refs_0_), channel_id=1, source_target_pairs={{0,2},{1,3},{2,0},{3,1},{4,6},{5,7},{6,4},{7,5},{8,10},{9,11},{10,... | collective-permute-start | bytes 301064 | tf_op jit(solution)/shard_map/ppermute | solution.py:26
  9.3 4.9 %collective-permute-start.1 = (bf16[8,6272]{1,0:T(8,128)(2,1)S(1)}, bf16[8,6272]{1,0:T(8,128)(2,1)S(1)}, u32[]{:S(2)}, u32[]{:S(2)}) collective-permute-start(bf16[8,6272]{1,0:T(8,128)(2,1)S(1)} %shard_map.102.refs_0_), channel_id=1, source_target_pairs={{0,4},{1,5},{2,6},{3,7},{4,0},{5,1},{6,2},{7,3},{8,12},{9,13},{10,... | collective-permute-start | bytes 301064 | tf_op jit(solution)/shard_map/ppermute | solution.py:26
  10.9 4.7 %collective-permute-start.7 = (bf16[8,6272]{1,0:T(8,128)(2,1)S(1)}, bf16[8,6272]{1,0:T(8,128)(2,1)S(1)}, u32[]{:S(2)}, u32[]{:S(2)}) collective-permute-start(bf16[8,6272]{1,0:T(8,128)(2,1)S(1)} %shard_map.102.refs_0_), channel_id=1, source_target_pairs={{0,1},{1,0},{2,3},{3,2},{4,5},{5,4},{6,7},{7,6},{8,9},{9,8},{10,11... | collective-permute-start | bytes 301064 | tf_op jit(solution)/shard_map/ppermute | solution.py:26
  12.9 4.6 %collective-permute-start.2 = (bf16[8,6272]{1,0:T(8,128)(2,1)S(1)}, bf16[8,6272]{1,0:T(8,128)(2,1)S(1)}, u32[]{:S(2)}, u32[]{:S(2)}) collective-permute-start(bf16[8,6272]{1,0:T(8,128)(2,1)S(1)} %collective-permute-done.refs_1_), channel_id=1, source_target_pairs={{0,4},{1,5},{2,6},{3,7},{4,0},{5,1},{6,2},{7,3},{8,12},{9,13},{10,... | collective-permute-start | bytes 301064 | tf_op jit(solution)/shard_map/ppermute | solution.py:26
  13.5 5.5 %collective-permute-start.11 = (bf16[8,6272]{1,0:T(8,128)(2,1)S(1)}, bf16[8,6272]{1,0:T(8,128)(2,1)S(1)}, u32[]{:S(2)}, u32[]{:S(2)}) collective-permute-start(bf16[8,6272]{1,0:T(8,128)(2,1)S(1)} %collective-permute-done.3.refs_4_), channel_id=1, source_target_pairs={{0,1},{1,0},{2,3},{3,2},{4,5},{5,4},{6,7},{7,6},{8,9},{9,8},{10,11... | collective-permute-start | bytes 301064 | tf_op jit(solution)/shard_map/ppermute | solution.py:26
  14.2 4.8 %collective-permute-start.9 = (bf16[8,6272]{1,0:T(8,128)(2,1)S(1)}, bf16[8,6272]{1,0:T(8,128)(2,1)S(1)}, u32[]{:S(2)}, u32[]{:S(2)}) collective-permute-start(bf16[8,6272]{1,0:T(8,128)(2,1)S(1)} %collective-permute-done.1.refs_2_), channel_id=1, source_target_pairs={{0,1},{1,0},{2,3},{3,2},{4,5},{5,4},{6,7},{7,6},{8,9},{9,8},{10,11... | collective-permute-start | bytes 301064 | tf_op jit(solution)/shard_map/ppermute | solution.py:26
  14.2 5.6 %collective-permute-start.5 = (bf16[8,6272]{1,0:T(8,128)(2,1)S(1)}, bf16[8,6272]{1,0:T(8,128)(2,1)S(1)}, u32[]{:S(2)}, u32[]{:S(2)}) collective-permute-start(bf16[8,6272]{1,0:T(8,128)(2,1)S(1)} %collective-permute-done.1.refs_2_), channel_id=1, source_target_pairs={{0,2},{1,3},{2,0},{3,1},{4,6},{5,7},{6,4},{7,5},{8,10},{9,11},{10,... | collective-permute-start | bytes 301064 | tf_op jit(solution)/shard_map/ppermute | solution.py:26
  15.5 6.5 %collective-permute-start.4 = (bf16[8,6272]{1,0:T(8,128)(2,1)S(1)}, bf16[8,6272]{1,0:T(8,128)(2,1)S(1)}, u32[]{:S(2)}, u32[]{:S(2)}) collective-permute-start(bf16[8,6272]{1,0:T(8,128)(2,1)S(1)} %collective-permute-done.refs_1_), channel_id=1, source_target_pairs={{0,2},{1,3},{2,0},{3,1},{4,6},{5,7},{6,4},{7,5},{8,10},{9,11},{10,... | collective-permute-start | bytes 301064 | tf_op jit(solution)/shard_map/ppermute | solution.py:26
  17.5 6.3 %collective-permute-start.6 = (bf16[8,6272]{1,0:T(8,128)(2,1)S(1)}, bf16[8,6272]{1,0:T(8,128)(2,1)S(1)}, u32[]{:S(2)}, u32[]{:S(2)}) collective-permute-start(bf16[8,6272]{1,0:T(8,128)(2,1)S(1)} %collective-permute-done.2.refs_3_), channel_id=1, source_target_pairs={{0,2},{1,3},{2,0},{3,1},{4,6},{5,7},{6,4},{7,5},{8,10},{9,11},{10,... | collective-permute-start | bytes 301064 | tf_op jit(solution)/shard_map/ppermute | solution.py:26
  19.1 13.8 %collective-permute-start.8 = (bf16[8,6272]{1,0:T(8,128)(2,1)S(1)}, bf16[8,6272]{1,0:T(8,128)(2,1)S(1)}, u32[]{:S(2)}, u32[]{:S(2)}) collective-permute-start(bf16[8,6272]{1,0:T(8,128)(2,1)S(1)} %collective-permute-done.refs_1_), channel_id=1, source_target_pairs={{0,1},{1,0},{2,3},{3,2},{4,5},{5,4},{6,7},{7,6},{8,9},{9,8},{10,11... | collective-permute-start | bytes 301064 | tf_op jit(solution)/shard_map/ppermute | solution.py:26
  19.1 13.8 %collective-permute-start.10 = (bf16[8,6272]{1,0:T(8,128)(2,1)S(1)}, bf16[8,6272]{1,0:T(8,128)(2,1)S(1)}, u32[]{:S(2)}, u32[]{:S(2)}) collective-permute-start(bf16[8,6272]{1,0:T(8,128)(2,1)S(1)} %collective-permute-done.2.refs_3_), channel_id=1, source_target_pairs={{0,1},{1,0},{2,3},{3,2},{4,5},{5,4},{6,7},{7,6},{8,9},{9,8},{10,11... | collective-permute-start | bytes 301064 | tf_op jit(solution)/shard_map/ppermute | solution.py:26
  19.9 13.0 %collective-permute-start.13 = (bf16[8,6272]{1,0:T(8,128)(2,1)S(1)}, bf16[8,6272]{1,0:T(8,128)(2,1)S(1)}, u32[]{:S(2)}, u32[]{:S(2)}) collective-permute-start(bf16[8,6272]{1,0:T(8,128)(2,1)S(1)} %collective-permute-done.5.refs_6_), channel_id=1, source_target_pairs={{0,1},{1,0},{2,3},{3,2},{4,5},{5,4},{6,7},{7,6},{8,9},{9,8},{10,11... | collective-permute-start | bytes 301064 | tf_op jit(solution)/shard_map/ppermute | solution.py:26
  22.0 10.8 %collective-permute-start.12 = (bf16[8,6272]{1,0:T(8,128)(2,1)S(1)}, bf16[8,6272]{1,0:T(8,128)(2,1)S(1)}, u32[]{:S(2)}, u32[]{:S(2)}) collective-permute-start(bf16[8,6272]{1,0:T(8,128)(2,1)S(1)} %collective-permute-done.4.refs_5_), channel_id=1, source_target_pairs={{0,1},{1,0},{2,3},{3,2},{4,5},{5,4},{6,7},{7,6},{8,9},{9,8},{10,11... | collective-permute-start | bytes 301064 | tf_op jit(solution)/shard_map/ppermute | solution.py:26
  23.8 9.1 %collective-permute-start.14 = (bf16[8,6272]{1,0:T(8,128)(2,1)S(1)}, bf16[8,6272]{1,0:T(8,128)(2,1)S(1)}, u32[]{:S(2)}, u32[]{:S(2)}) collective-permute-start(bf16[8,6272]{1,0:T(8,128)(2,1)S(1)} %collective-permute-done.6.refs_7_), channel_id=1, source_target_pairs={{0,1},{1,0},{2,3},{3,2},{4,5},{5,4},{6,7},{7,6},{8,9},{9,8},{10,11... | collective-permute-start | bytes 301064 | tf_op jit(solution)/shard_map/ppermute | solution.py:26
  23.8 9.1 %copy-start.2 = (bf16[256,3072]{1,0:T(8,128)(2,1)S(1)}, bf16[256,3072]{1,0:T(8,128)(2,1)}, u32[]{:S(2)}) copy-start(bf16[256,3072]{1,0:T(8,128)(2,1)} %refs_17_.1) | copy-start | bytes 4718596
  23.8 9.1 %copy-start.7 = (s32[16]{0:T(128)S(1)}, s32[16]{0:T(128)}, u32[]{:S(2)}) copy-start(s32[16]{0:T(128)} %owner_ref.3) | copy-start | bytes 196
  31.2 1.7 %copy-start = (bf16[3072,512]{1,0:T(8,128)(2,1)}, bf16[3072,512]{1,0:T(8,128)(2,1)S(1)}, u32[]{:S(2)}) copy-start(bf16[3072,512]{1,0:T(8,128)(2,1)S(1)} %shard_map.103.refs_16_.w_ref) | copy-start | bytes 9437188
  32.9 5.5 %copy-start.1 = (bf16[3072,512]{1,0:T(8,128)(2,1)S(1)}, bf16[3072,512]{1,0:T(8,128)(2,1)}, u32[]{:S(2)}) copy-start(bf16[3072,512]{1,0:T(8,128)(2,1)} %copy-done) | copy-start | bytes 9437188
  37.9 2.2 %collective-permute-start.15 = (bf16[64,3200]{1,0:T(8,128)(2,1)S(1)}, bf16[64,3200]{1,0:T(8,128)(2,1)S(1)}, u32[]{:S(2)}, u32[]{:S(2)}) collective-permute-start(bf16[64,3200]{1,0:T(8,128)(2,1)S(1)} %get-tuple-element.20), channel_id=1, source_target_pairs={{0,1},{1,0},{2,3},{3,2},{4,5},{5,4},{6,7},{7,6},{8,9},{9,8},{10,11... | collective-permute-start | bytes 1228808 | tf_op jit(solution)/shard_map/ppermute | solution.py:26
  40.2 7.2 %collective-permute-start.16 = (bf16[32,3200]{1,0:T(8,128)(2,1)S(1)}, bf16[32,3200]{1,0:T(8,128)(2,1)S(1)}, u32[]{:S(2)}, u32[]{:S(2)}) collective-permute-start(bf16[32,3200]{1,0:T(8,128)(2,1)S(1)} %get-tuple-element.22), channel_id=1, source_target_pairs={{0,2},{1,3},{2,0},{3,1},{4,6},{5,7},{6,4},{7,5},{8,10},{9,11},{10,... | collective-permute-start | bytes 614408 | tf_op jit(solution)/shard_map/ppermute | solution.py:26
  47.5 4.7 %collective-permute-start.17 = (bf16[16,3200]{1,0:T(8,128)(2,1)S(1)}, bf16[16,3200]{1,0:T(8,128)(2,1)S(1)}, u32[]{:S(2)}, u32[]{:S(2)}) collective-permute-start(bf16[16,3200]{1,0:T(8,128)(2,1)S(1)} %get-tuple-element.24), channel_id=1, source_target_pairs={{0,4},{1,5},{2,6},{3,7},{4,0},{5,1},{6,2},{7,3},{8,12},{9,13},{10,... | collective-permute-start | bytes 307208 | tf_op jit(solution)/shard_map/ppermute | solution.py:26
  52.4 12.9 %collective-permute-start.18 = (bf16[8,3200]{1,0:T(8,128)(2,1)S(1)}, bf16[8,3200]{1,0:T(8,128)(2,1)S(1)}, u32[]{:S(2)}, u32[]{:S(2)}) collective-permute-start(bf16[8,3200]{1,0:T(8,128)(2,1)S(1)} %get-tuple-element.26), channel_id=1, source_target_pairs={{0,8},{1,9},{2,10},{3,11},{4,12},{5,13},{6,14},{7,15},{8,0},{9,1},... | collective-permute-start | bytes 153608 | tf_op jit(solution)/shard_map/ppermute | solution.py:26
  55.2 10.1 %copy-start.6 = (s32[8,2]{0,1:T(2,128)S(1)}, s32[8,2]{0,1:T(2,128)}, u32[]{:S(2)}) copy-start(s32[8,2]{0,1:T(2,128)} %param.9) | copy-start | bytes 196

commit v2 on v1

--- a/solution.py
+++ b/solution.py
@@ -9,16 +9,19 @@
 
 EXP_WIN = 4
 META = 128
+LANES = 128
+SIDE = 256
 BF = jnp.bfloat16
 F32 = jnp.float32
 VMEM = pl.BlockSpec(memory_space=pltpu.VMEM)
+ANY = pl.BlockSpec(memory_space=pl.ANY)
 SMEM = pl.BlockSpec(memory_space=pltpu.SMEM)
 NT = (((1,), (1,)), ((), ()))
 TN = (((0,), (0,)), ((), ()))
 
 
-def params():
-    return pltpu.CompilerParams(vmem_limit_bytes=48 << 20)
+def params(mib=16):
+    return pltpu.CompilerParams(vmem_limit_bytes=mib << 20)
 
 
 def xor_swap(value, bit):
@@ -66,26 +69,51 @@
     out_ref[:, 2 * width :] = meta.astype(BF)
 
 
+def shuffle(group, inverse=False):
+    per = SIDE // group
+    row = lax.broadcasted_iota(jnp.int32, (SIDE, SIDE), 0)
+    col = lax.broadcasted_iota(jnp.int32, (SIDE, SIDE), 1)
+    if inverse:
+        row, col = col, row
+    return (col == (row % per) * group + row // per).astype(BF)
+
+
 def split_kernel(w_ref, out_ref):
-    hid = w_ref.shape[2]
-    block = w_ref[...]
-    out_ref[:, :hid] = block[:, 0, :]
-    out_ref[:, hid:] = block[:, 1, :]
+    d, wide = out_ref.shape
+    group = wide // LANES
+    per = SIDE // group
+    tiles = group // 2
+    take = shuffle(group)
+    for s in range(0, d // per, 2):
+        pair = jnp.concatenate(
+            [w_ref[s * SIDE : (s + 1) * SIDE, :], w_ref[(s + 1) * SIDE : (s + 2) * SIDE, :]], 1
+        )
+        rows = jnp.dot(take, pair, preferred_element_type=F32).astype(BF)
+        for q in range(group):
+            column = (q % 2 * tiles + q // 2) * LANES
+            for half in range(2):
+                here = (s + half) * per
+                out_ref[here : here + per, column : column + LANES] = rows[
+                    q * per : (q + 1) * per, half * LANES : (half + 1) * LANES
+                ]
 
 
 def split_weights(w_in, block=512):
     d, two, hid = w_in.shape
+    tiles = hid // LANES
+    group = two * tiles
+    view = w_in.reshape(d, two, tiles, LANES).transpose(0, 2, 1, 3).reshape(d * group, LANES)
     return pl.pallas_call(
         split_kernel,
         grid=(d // block,),
-        in_specs=[pl.BlockSpec((block, two, hid), lambda i: (i, 0, 0))],
+        in_specs=[pl.BlockSpec((block * group, LANES), lambda i: (i, 0))],
         out_specs=pl.BlockSpec((block, two * hid), lambda i: (i, 0)),
         out_shape=jax.ShapeDtypeStruct((d, two * hid), BF),
         compiler_params=params(),
         cost_estimate=pl.CostEstimate(
-            flops=0, bytes_accessed=30 * d * two * hid, transcendentals=0
-        ),
-    )(w_in)
+            flops=2 * d * group * SIDE * LANES, bytes_accessed=8 * d * hid, transcendentals=0
+        ),
+    )(view)
 
 
 def put_gate(out_ref, value, expert, width):
@@ -105,13 +133,13 @@
         ).astype(out_ref.dtype)
 
 
-def main_kernel(n, owner_ref, me_ref, *refs):
+def main_kernel(n, owner_ref, *refs):
     pieces, refs = refs[:n], refs[n:]
     w_ref, down_ref, tok_ref, scaled_ref, pre_ref, hid_ref, gate_ref, send_ref, grad_ref = refs
     rows = pieces[0].shape[0]
     width = down_ref.shape[1]
     hid = down_ref.shape[0]
-    expert = owner_ref[me_ref[0]]
+    expert = owner_ref[lax.axis_index("dev")]
     metas = []
     for i in range(0, n, 2):
         pair = [pieces[i][...].astype(F32), pieces[i + 1][...].astype(F32)]
@@ -145,35 +173,34 @@
     scaled_ref[...] = (prob * grad_ref[...].astype(F32)).astype(BF)
 
 
-def own_kernel(owner_ref, me_ref, pre_ref, w_ref, gate_ref, out_ref):
+def own_kernel(owner_ref, pre_ref, w_ref, gate_ref, out_ref):
     half = out_ref.shape[0]
     width = w_ref.shape[0]
-    put_gate(out_ref, gate_ref[:half, :1], owner_ref[me_ref[0]], width)
+    put_gate(out_ref, gate_ref[:half, :1], owner_ref[lax.axis_index("dev")], width)
     token_part(pre_ref[:half, :], w_ref, out_ref, width)
 
 
-def add_kernel(own_ref, got_ref, keep_ref, send_ref=None):
+def add_kernel(own_ref, got_ref, after_ref, keep_ref, send_ref):
     total = own_ref[...] + got_ref[...].astype(F32)
     half = keep_ref.shape[0]
     width = total.shape[1] - META
     keep_ref[...] = total[:half]
-    if send_ref is not None:
-        send_ref[:, :width] = total[half:, :width].astype(BF)
-        tail = total[half:, width:]
-        lane = lax.broadcasted_iota(jnp.int32, tail.shape, 1)
-        value = tail + pltpu.roll(tail, META - EXP_WIN, 1)
-        high = value.astype(BF).astype(F32)
-        low = pltpu.roll(value - high, EXP_WIN, 1)
-        pair = jnp.where(lane < EXP_WIN, high, jnp.where(lane < 2 * EXP_WIN, low, 0.0))
-        send_ref[:, width:] = pair.astype(BF)
-
-
-def add_step(own, got):
+    send_ref[:, :width] = total[half:, :width].astype(BF)
+    tail = total[half:, width:]
+    lane = lax.broadcasted_iota(jnp.int32, tail.shape, 1)
+    value = tail + pltpu.roll(tail, META - EXP_WIN, 1)
+    high = value.astype(BF).astype(F32)
+    low = pltpu.roll(value - high, EXP_WIN, 1)
+    pair = jnp.where(lane < EXP_WIN, high, jnp.where(lane < 2 * EXP_WIN, low, 0.0))
+    send_ref[:, width:] = pair.astype(BF)
+
+
+def add_step(own, got, after):
     rows, width = own.shape
     half = rows // 2
     return pl.pallas_call(
         add_kernel,
-        in_specs=[VMEM, VMEM],
+        in_specs=[VMEM, VMEM, ANY],
         out_specs=[VMEM, VMEM],
         out_shape=[
             jax.ShapeDtypeStruct((half, width), F32),
@@ -183,7 +210,7 @@
         cost_estimate=pl.CostEstimate(
             flops=rows * width, bytes_accessed=8 * rows * width, transcendentals=0
         ),
-    )(own, got)
+    )(own, got, after)
 
 
 def last_kernel(own_ref, got_ref, ids_ref, tok_ref, gates_ref):
@@ -206,33 +233,65 @@
         gates_ref[k : k + 1, :] = jnp.sum(square, 0, keepdims=True)
 
 
-def win_kernel(tok_ref, pre_ref, out_ref):
-    hid = out_ref.shape[2]
-    block = lax.dot_general(tok_ref[...], pre_ref[...], TN, preferred_element_type=F32)
-    out_ref[:, 0, :] = block[:, :hid].astype(BF)
-    out_ref[:, 1, :] = block[:, hid:].astype(BF)
-
-
-def grad_in(tok, pre, block=256):
+def win_kernel(tok_ref, pre_ref, out_ref, token_ref):
+    wide = pre_ref.shape[1]
+    group = wide // LANES
+    per = SIDE // group
+    tiles = group // 2
+    put = shuffle(group, inverse=True)
+    block = lax.dot_general(
+        tok_ref[...], pre_ref[...], TN, preferred_element_type=F32
+    ).astype(BF)
+    for s in range(0, tok_ref.shape[1] // per, 2):
+        sides = []
+        for half in range(2):
+            here = (s + half) * per
+            sides.append(
+                jnp.concatenate(
+                    [
+                        block[here : here + per, c * LANES : (c + 1) * LANES]
+                        for c in [q % 2 * tiles + q // 2 for q in range(group)]
+                    ],
+                    0,
+                )
+            )
+        rows = jnp.dot(put, jnp.concatenate(sides, 1), preferred_element_type=F32).astype(BF)
+        out_ref[s * SIDE : (s + 1) * SIDE, :] = rows[:, :LANES]
+        out_ref[(s + 1) * SIDE : (s + 2) * SIDE, :] = rows[:, LANES:]
+    token_ref[...] = jnp.zeros_like(token_ref)
+
+
+def grad_in(tok, pre, block=512):
     rows, d = tok.shape
     hid = pre.shape[1] // 2
-    return pl.pallas_call(
+    tiles = hid // LANES
+    group = 2 * tiles
+    out, token = pl.pallas_call(
         win_kernel,
         grid=(d // block,),
         in_specs=[
             pl.BlockSpec((rows, block), lambda i: (0, i)),
             pl.BlockSpec((rows, 2 * hid), lambda i: (0, 0)),
         ],
-        out_specs=pl.BlockSpec((block, 2, hid), lambda i: (i, 0, 0)),
-        out_shape=jax.ShapeDtypeStruct((d, 2, hid), BF),
+        out_specs=[
+            pl.BlockSpec((block * group, LANES), lambda i: (i, 0)),
+            pl.BlockSpec((8, LANES), lambda i: (0, 0)),
+        ],
+        out_shape=[
+            jax.ShapeDtypeStruct((d * group, LANES), BF),
+            jax.ShapeDtypeStruct((8, LANES), F32),
+        ],
         compiler_params=params(),
         cost_estimate=pl.CostEstimate(
-            flops=4 * rows * d * hid, bytes_accessed=30 * d * hid, transcendentals=0
+            flops=4 * rows * d * hid, bytes_accessed=8 * d * hid, transcendentals=0
         ),
     )(tok, pre)
-
-
-def down_kernel(hid_ref, scaled_ref, out_ref):
+    out = out.reshape(d, tiles, 2, LANES).transpose(0, 2, 1, 3).reshape(d, 2, hid)
+    return out, token
+
+
+def down_kernel(hid_ref, scaled_ref, out_ref, token_ref):
+    token_ref[...] = jnp.zeros_like(token_ref)
     out_ref[...] = lax.dot_general(
         hid_ref[...], scaled_ref[...], TN, preferred_element_type=F32
     ).astype(BF)
@@ -248,8 +307,14 @@
             pl.BlockSpec((rows, hid), lambda i: (0, 0)),
             pl.BlockSpec((rows, block), lambda i: (0, i)),
         ],
-        out_specs=pl.BlockSpec((hid, block), lambda i: (0, i)),
-        out_shape=jax.ShapeDtypeStruct((hid, d), BF),
+        out_specs=[
+            pl.BlockSpec((hid, block), lambda i: (0, i)),
+            pl.BlockSpec((8, LANES), lambda i: (0, 0)),
+        ],
+        out_shape=[
+            jax.ShapeDtypeStruct((hid, d), BF),
+            jax.ShapeDtypeStruct((8, LANES), F32),
+        ],
         compiler_params=params(),
         cost_estimate=pl.CostEstimate(
             flops=2 * rows * d * hid, bytes_accessed=4 * d * hid, transcendentals=0
@@ -259,7 +324,6 @@
 
 def shards(tokens, grad_out, expert_ids, gate_probs, device_expert, w_in, w_down):
     n = lax.axis_size("dev")
-    me = lax.axis_index("dev").astype(jnp.int32).reshape(1)
     rows, width = tokens.shape
     hid = w_down.shape[0]
     ids_t = expert_ids.T
@@ -271,22 +335,25 @@
         in_specs=[VMEM] * 4,
         out_specs=VMEM,
         out_shape=jax.ShapeDtypeStruct((rows, 2 * width + META), BF),
-        compiler_params=params(),
+        compiler_params=params(60),
     )(tokens, grad_out, ids_t, probs_t)
 
     held = {0: own}
     order = [0]
-    for bit in bits:
+    w_flat = split_weights(w_in)
+    for step, bit in enumerate(bits):
         for o in order:
             held[o ^ bit] = xor_swap(held[o], bit)
+        if bit == 2:
+            last = order[1] ^ bit
+            held[last], w_flat = lax.optimization_barrier((held[last], w_flat))
         order = order + [o ^ bit for o in order]
 
-    w_flat = split_weights(w_in)
     total = n * rows
     half = total // 2
     tok, scaled, pre, hidden, gate, send = pl.pallas_call(
         functools.partial(main_kernel, n),
-        in_specs=[SMEM, SMEM] + [VMEM] * (n + 2),
+        in_specs=[SMEM] + [VMEM] * (n + 2),
         out_specs=[VMEM] * 6,
         out_shape=[
             jax.ShapeDtypeStruct((total, width), BF),
@@ -298,22 +365,22 @@
         ],
         scratch_shapes=[pltpu.VMEM((total, width), BF)],
         compiler_params=params(),
-    )(device_expert, me, *[held[o] for o in order], w_flat, w_down)
+    )(device_expert, *[held[o] for o in order], w_flat, w_down)
 
     got = xor_swap(send, 1)
     mine = pl.pallas_call(
         own_kernel,
-        in_specs=[SMEM, SMEM] + [VMEM] * 3,
+        in_specs=[SMEM] + [VMEM] * 3,
         out_specs=VMEM,
         out_shape=jax.ShapeDtypeStruct((half, width + META), F32),
         compiler_params=params(),
-    )(device_expert, me, pre, w_flat, gate)
-    for bit in bits[-2::-1]:
-        mine, send = add_step(mine, got)
+    )(device_expert, pre, w_flat, gate)
+    grad_w_in, after_in = grad_in(tok, pre)
+    grad_w_down, after_down = grad_down(hidden, scaled)
+    for step, bit in enumerate(bits[-2::-1]):
+        mine, send = add_step(mine, got, (gate, after_in, after_down)[min(step, 2)])
         got = xor_swap(send, bit)
 
-    grad_w_down = grad_down(hidden, scaled)
-    grad_w_in = grad_in(tok, pre)
     grad_tokens, gates_t = pl.pallas_call(
         last_kernel,
         in_specs=[VMEM] * 3,

time: 66.4 us -> 48.2 us (0.73)
  Pallas kernels: 25.3 us -> 16.7 us
  waiting for transfers between devices: 17.8 us -> 11.4 us
  local copies, waits for them, and re-layouts: 4.62 us -> 1.91 us
    ppermute x19, waiting for transfers between devices: 17.8 us -> 11.4 us  [xor_swap(): return lax.ppermute(value, 'dev', [(i, i ^ bit) for i in range(n)])]
    pallas_call x1, Pallas kernels: 7.38 us -> 1.89 us  [split_weights(): pl.pallas_call(split_kernel, grid=(d // block,), in_specs=[pl.BlockSpec((...]
    pallas_call x1, Pallas kernels: 7.68 us -> 4.64 us  [grad_in(): pl.pallas_call(win_kernel, grid=(d // block,), in_specs=[pl.BlockSpec((ro...]
    unnamed x18 -> x10, local copies, waits for them, and re-layouts: 4.62 us -> 1.91 us
    pallas_call x5, Pallas kernels: 6.97 us -> 5.46 us  [the longest x1 3.42 us: shards(): pl.pallas_call(functools.partial(main_kernel, n), in_specs=[SMEM] + [VMEM...]
    pallas_call x1, Pallas kernels: 0.09 us -> 1.56 us  [shards(): pl.pallas_call(pack_kernel, in_specs=[VMEM] * 4, out_specs=VMEM, out_shap...]
  transfers between devices with their start and end apart: 19 -> 19, of which waited for: 8 -> 10; matrix products, arithmetic and copies ran while one was open for 0% -> 0% of each run, Pallas kernels for 29% -> 22%
where the time goes in v2:
time: 48.2 us; the launch traced here: 48 us
  starting transfers between devices  17.3 us (36%)
  Pallas kernels  16.7 us (35%)
  waiting for transfers between devices  11.4 us (24%)
  local copies, waits for them, and re-layouts  1.91 us (4%)
  between operations  0.7 us (1%)
    ppermute x19, starting transfers between devices, xor_swap(): return lax.ppermute(value, 'dev', [(i, i ^ bit) for i in range(n)])  17.3 us
    ppermute x19, waiting for transfers between devices, xor_swap(): return lax.ppermute(value, 'dev', [(i, i ^ bit) for i in range(n)])  11.4 us
    pallas_call x1, Pallas kernels, grad_in(): pl.pallas_call(win_kernel, grid=(d // block,), in_specs=[pl.BlockSpec((ro...  4.64 us
    pallas_call x1, Pallas kernels, shards(): pl.pallas_call(functools.partial(main_kernel, n), in_specs=[SMEM] + [VMEM...  3.42 us
    pallas_call x1, Pallas kernels, grad_down(): pl.pallas_call(down_kernel, grid=(d // block,), in_specs=[pl.BlockSpec((r...  2.41 us
    unnamed x10, local copies, waits for them, and re-layouts  1.91 us
    pallas_call x1, Pallas kernels, split_weights(): pl.pallas_call(split_kernel, grid=(d // block,), in_specs=[pl.BlockSpec((...  1.89 us
    pallas_call x1, Pallas kernels, shards(): pl.pallas_call(own_kernel, in_specs=[SMEM] + [VMEM] * 3, out_specs=VMEM,...  1.6 us
  transfers between devices with their start and end apart: 19, of which 10 were waited for; matrix products, arithmetic and copies ran while one was open for 0% of the time, Pallas kernels for 22%

profile of v2, /device:TPU:0, one launch (start us, length us, event | category | flops | bytes accessed | tf_op | source)
XLA Modules:
  0.0 48.0 jit_solution(10727691147663635708)
XLA Ops:
  0.6 1.6 %shard_map.102.refs_0_ = bf16[8,6272]{1,0:T(8,128)(2,1)} custom-call(bf16[8,3072]{1,0:T(8,128)(2,1)} %tok_ref.1, bf16[8,3072]{1,0:T(8,128)(2,1)} %grad_ref.1, s32[2,8]{1,0:T(2,128)} %bitcast.14, f32[2,8]{1,0:T(2,128)} %bitcast.16), custom_call_target="tpu_custom_call" | custom-call | tf_op jit(solution)/shard_map/pallas_call | solution.py:333
  2.2 4.0 %collective-permute-start = (bf16[8,6272]{1,0:T(8,128)(2,1)}, bf16[8,6272]{1,0:T(8,128)(2,1)S(1)}, u32[]{:S(2)}, u32[]{:S(2)}) collective-permute-start(bf16[8,6272]{1,0:T(8,128)(2,1)} %shard_map.102.refs_0_), channel_id=1, source_target_pairs={{0,8},{1,9},{2,10},{3,11},{4,12},{5,13},{6,14},{7,15},{8,0},{9,1},... | collective-permute-start | bytes 301064 | tf_op jit(solution)/shard_map/ppermute | solution.py:29
  6.2 1.5 %collective-permute-start.3 = (bf16[8,6272]{1,0:T(8,128)(2,1)}, bf16[8,6272]{1,0:T(8,128)(2,1)S(1)}, u32[]{:S(2)}, u32[]{:S(2)}) collective-permute-start(bf16[8,6272]{1,0:T(8,128)(2,1)} %shard_map.102.refs_0_), channel_id=1, source_target_pairs={{0,2},{1,3},{2,0},{3,1},{4,6},{5,7},{6,4},{7,5},{8,10},{9,11},{10,... | collective-permute-start | bytes 301064 | tf_op jit(solution)/shard_map/ppermute | solution.py:29
  7.7 1.6 %collective-permute-start.1 = (bf16[8,6272]{1,0:T(8,128)(2,1)}, bf16[8,6272]{1,0:T(8,128)(2,1)S(1)}, u32[]{:S(2)}, u32[]{:S(2)}) collective-permute-start(bf16[8,6272]{1,0:T(8,128)(2,1)} %shard_map.102.refs_0_), channel_id=1, source_target_pairs={{0,4},{1,5},{2,6},{3,7},{4,0},{5,1},{6,2},{7,3},{8,12},{9,13},{10,... | collective-permute-start | bytes 301064 | tf_op jit(solution)/shard_map/ppermute | solution.py:29
  9.3 2.2 %collective-permute-done.refs_1_ = bf16[8,6272]{1,0:T(8,128)(2,1)S(1)} collective-permute-done((bf16[8,6272]{1,0:T(8,128)(2,1)}, bf16[8,6272]{1,0:T(8,128)(2,1)S(1)}, u32[]{:S(2)}, u32[]{:S(2)}) %collective-permute-start) | collective-permute-done | bytes 100384 | tf_op jit(solution)/shard_map/ppermute | solution.py:29
  11.5 1.6 %collective-permute-start.4 = (bf16[8,6272]{1,0:T(8,128)(2,1)S(1)}, bf16[8,6272]{1,0:T(8,128)(2,1)S(1)}, u32[]{:S(2)}, u32[]{:S(2)}) collective-permute-start(bf16[8,6272]{1,0:T(8,128)(2,1)S(1)} %collective-permute-done.refs_1_), channel_id=1, source_target_pairs={{0,2},{1,3},{2,0},{3,1},{4,6},{5,7},{6,4},{7,5},{8,10},{9,11},{10,... | collective-permute-start | bytes 301064 | tf_op jit(solution)/shard_map/ppermute | solution.py:29
  13.1 0.7 %collective-permute-start.2 = (bf16[8,6272]{1,0:T(8,128)(2,1)S(1)}, bf16[8,6272]{1,0:T(8,128)(2,1)S(1)}, u32[]{:S(2)}, u32[]{:S(2)}) collective-permute-start(bf16[8,6272]{1,0:T(8,128)(2,1)S(1)} %collective-permute-done.refs_1_), channel_id=1, source_target_pairs={{0,4},{1,5},{2,6},{3,7},{4,0},{5,1},{6,2},{7,3},{8,12},{9,13},{10,... | collective-permute-start | bytes 301064 | tf_op jit(solution)/shard_map/ppermute | solution.py:29
  13.8 0.0 collective-permute-start.7
  13.8 0.0 collective-permute-done.3.refs_4_
  13.8 0.5 %collective-permute-start.11 = (bf16[8,6272]{1,0:T(8,128)(2,1)S(1)}, bf16[8,6272]{1,0:T(8,128)(2,1)S(1)}, u32[]{:S(2)}, u32[]{:S(2)}) collective-permute-start(bf16[8,6272]{1,0:T(8,128)(2,1)S(1)} %collective-permute-done.3.refs_4_), channel_id=1, source_target_pairs={{0,1},{1,0},{2,3},{3,2},{4,5},{5,4},{6,7},{7,6},{8,9},{9,8},{10,11... | collective-permute-start | bytes 301064 | tf_op jit(solution)/shard_map/ppermute | solution.py:29
  14.3 0.0 collective-permute-done.1.refs_2_
  14.3 0.6 %collective-permute-start.5 = (bf16[8,6272]{1,0:T(8,128)(2,1)S(1)}, bf16[8,6272]{1,0:T(8,128)(2,1)S(1)}, u32[]{:S(2)}, u32[]{:S(2)}) collective-permute-start(bf16[8,6272]{1,0:T(8,128)(2,1)S(1)} %collective-permute-done.1.refs_2_), channel_id=1, source_target_pairs={{0,2},{1,3},{2,0},{3,1},{4,6},{5,7},{6,4},{7,5},{8,10},{9,11},{10,... | collective-permute-start | bytes 301064 | tf_op jit(solution)/shard_map/ppermute | solution.py:29
  14.8 1.3 %collective-permute-done.4.refs_5_ = bf16[8,6272]{1,0:T(8,128)(2,1)S(1)} collective-permute-done((bf16[8,6272]{1,0:T(8,128)(2,1)S(1)}, bf16[8,6272]{1,0:T(8,128)(2,1)S(1)}, u32[]{:S(2)}, u32[]{:S(2)}) %collective-permute-start.4) | collective-permute-done | bytes 100384 | tf_op jit(solution)/shard_map/ppermute | solution.py:29
  16.2 0.0 collective-permute-start.9
  16.2 1.6 %collective-permute-done.2.refs_3_ = bf16[8,6272]{1,0:T(8,128)(2,1)S(1)} collective-permute-done((bf16[8,6272]{1,0:T(8,128)(2,1)S(1)}, bf16[8,6272]{1,0:T(8,128)(2,1)S(1)}, u32[]{:S(2)}, u32[]{:S(2)}) %collective-permute-start.2) | collective-permute-done | bytes 100384 | tf_op jit(solution)/shard_map/ppermute | solution.py:29
  17.7 0.5 collective-permute-start.6
  18.2 1.9 %copy-done = bf16[3072,2,256]{2,1,0:T(2,128)(2,1)S(1)} copy-done((bf16[3072,2,256]{2,1,0:T(2,128)(2,1)S(1)}, bf16[3072,2,256]{2,1,0:T(2,128)(2,1)}, u32[]{:S(2)}) %copy-start) | copy-done | bytes 3145752
  20.1 1.9 %shard_map.103.refs_16_.w_ref = bf16[3072,512]{1,0:T(8,128)(2,1)S(1)} custom-call(bf16[12288,128]{1,0:T(8,128)(2,1)S(1)} %bitcast.13), custom_call_target="tpu_custom_call" | custom-call | flops 805306368 | bytes 6291456 | tf_op jit(solution)/shard_map/pallas_call | solution.py:106
  22.0 0.0 collective-permute-done.7.refs_8_
  22.0 0.1 collective-permute-start.8
  22.1 0.5 %collective-permute-start.12 = (bf16[8,6272]{1,0:T(8,128)(2,1)S(1)}, bf16[8,6272]{1,0:T(8,128)(2,1)S(1)}, u32[]{:S(2)}, u32[]{:S(2)}) collective-permute-start(bf16[8,6272]{1,0:T(8,128)(2,1)S(1)} %collective-permute-done.4.refs_5_), channel_id=1, source_target_pairs={{0,1},{1,0},{2,3},{3,2},{4,5},{5,4},{6,7},{7,6},{8,9},{9,8},{10,11... | collective-permute-start | bytes 301064 | tf_op jit(solution)/shard_map/ppermute | solution.py:29
  22.6 0.0 collective-permute-done.5.refs_6_
  22.6 0.1 collective-permute-start.13
  22.7 0.4 collective-permute-start.10
  23.1 0.0 collective-permute-done.6.refs_7_
  23.1 0.1 collective-permute-start.14
  23.2 0.2 collective-permute-done.8.refs_9_
  23.4 0.5 %collective-permute-done.13.refs_14_ = bf16[8,6272]{1,0:T(8,128)(2,1)S(1)} collective-permute-done((bf16[8,6272]{1,0:T(8,128)(2,1)S(1)}, bf16[8,6272]{1,0:T(8,128)(2,1)S(1)}, u32[]{:S(2)}, u32[]{:S(2)}) %collective-permute-start.13) | collective-permute-done | bytes 100384 | tf_op jit(solution)/shard_map/ppermute | solution.py:29
  23.9 0.2 collective-permute-done.10.refs_11_
  24.0 0.0 collective-permute-done.12.refs_13_
  24.1 0.4 collective-permute-done.14.refs_15_
  24.4 3.4 %shard_map.104 = (bf16[128,3072]{1,0:T(8,128)(2,1)S(1)}, bf16[128,3072]{1,0:T(8,128)(2,1)S(1)}, bf16[128,512]{1,0:T(8,128)(2,1)S(1)}, bf16[128,256]{1,0:T(8,128)...) custom-call(s32[16]{0:T(128)S(1)} %copy-done.4, bf16[8,6272]{1,0:T(8,128)(2,1)S(1)} %copy-done.2, ...), custom_call_target="tpu_custom_call" | custom-call | tf_op jit(solution)/shard_map/pallas_call | solution.py:354
  27.8 0.2 collective-permute-start.15
  28.1 1.6 %shard_map.105.own_ref = f32[64,3200]{1,0:T(8,128)S(1)} custom-call(s32[16]{0:T(128)S(1)} %copy-done.4, bf16[128,512]{1,0:T(8,128)(2,1)S(1)} %get-tuple-element.26.pre_ref, bf16[3072,512]{1,0:T(8,128)(2,1)S(1)} %shard_map.103.refs_16_.w_ref, f32[128,128]{1,0:T(8,128)S(1)} %get-tuple-element.27.gate_ref.after_ref), custom_call_target="tpu_custom_call" | custom-call | tf_op jit(solution)/shard_map/pallas_call | solution.py:371
  29.7 0.0 copy-start.3
  29.7 0.0 collective-permute-done.15.got_ref
  29.7 0.2 shard_map.106
  29.8 1.6 %collective-permute-start.16 = (bf16[32,3200]{1,0:T(8,128)(2,1)S(1)}, bf16[32,3200]{1,0:T(8,128)(2,1)S(1)}, u32[]{:S(2)}, u32[]{:S(2)}) collective-permute-start(bf16[32,3200]{1,0:T(8,128)(2,1)S(1)} %get-tuple-element.30), channel_id=1, source_target_pairs={{0,2},{1,3},{2,0},{3,1},{4,6},{5,7},{6,4},{7,5},{8,10},{9,11},{10,... | collective-permute-start | bytes 614408 | tf_op jit(solution)/shard_map/ppermute | solution.py:29
  31.5 4.6 %shard_map.107 = (bf16[12288,128]{1,0:T(8,128)(2,1)}, f32[8,128]{1,0:T(8,128)S(1)}) custom-call(bf16[128,3072]{1,0:T(8,128)(2,1)S(1)} %get-tuple-element.31.tok_ref, bf16[128,512]{1,0:T(8,128)(2,1)S(1)} %get-tuple-element.26.pre_ref), custom_call_target="tpu_custom_call" | custom-call | flops 402653184 | bytes 6291456 | tf_op jit(solution)/shard_map/pallas_call | solution.py:269
  36.1 1.1 %collective-permute-done.16.got_ref = bf16[32,3200]{1,0:T(8,128)(2,1)S(1)} collective-permute-done((bf16[32,3200]{1,0:T(8,128)(2,1)S(1)}, bf16[32,3200]{1,0:T(8,128)(2,1)S(1)}, u32[]{:S(2)}, u32[]{:S(2)}) %collective-permute-start.16) | collective-permute-done | bytes 204832 | tf_op jit(solution)/shard_map/ppermute | solution.py:29
  37.2 0.1 shard_map.108
  37.4 0.8 %collective-permute-start.17 = (bf16[16,3200]{1,0:T(8,128)(2,1)S(1)}, bf16[16,3200]{1,0:T(8,128)(2,1)S(1)}, u32[]{:S(2)}, u32[]{:S(2)}) collective-permute-start(bf16[16,3200]{1,0:T(8,128)(2,1)S(1)} %get-tuple-element.34), channel_id=1, source_target_pairs={{0,4},{1,5},{2,6},{3,7},{4,0},{5,1},{6,2},{7,3},{8,12},{9,13},{10,... | collective-permute-start | bytes 307208 | tf_op jit(solution)/shard_map/ppermute | solution.py:29
  38.2 2.4 %shard_map.109 = (bf16[256,3072]{1,0:T(8,128)(2,1)}, f32[8,128]{1,0:T(8,128)S(1)}) custom-call(bf16[128,256]{1,0:T(8,128)(2,1)S(1)} %get-tuple-element.35.hid_ref, bf16[128,3072]{1,0:T(8,128)(2,1)S(1)} %get-tuple-element.36.scaled_ref), custom_call_target="tpu_custom_call" | custom-call | flops 201326592 | bytes 3145728 | tf_op jit(solution)/shard_map/pallas_call | solution.py:303
  40.6 1.5 %collective-permute-done.17.got_ref = bf16[16,3200]{1,0:T(8,128)(2,1)S(1)} collective-permute-done((bf16[16,3200]{1,0:T(8,128)(2,1)S(1)}, bf16[16,3200]{1,0:T(8,128)(2,1)S(1)}, u32[]{:S(2)}, u32[]{:S(2)}) %collective-permute-start.17) | collective-permute-done | bytes 102432 | tf_op jit(solution)/shard_map/ppermute | solution.py:29
  42.1 0.1 shard_map.110
  42.2 2.6 %collective-permute-start.18 = (bf16[8,3200]{1,0:T(8,128)(2,1)S(1)}, bf16[8,3200]{1,0:T(8,128)(2,1)S(1)}, u32[]{:S(2)}, u32[]{:S(2)}) collective-permute-start(bf16[8,3200]{1,0:T(8,128)(2,1)S(1)} %get-tuple-element.39), channel_id=1, source_target_pairs={{0,8},{1,9},{2,10},{3,11},{4,12},{5,13},{6,14},{7,15},{8,0},{9,1},... | collective-permute-start | bytes 153608 | tf_op jit(solution)/shard_map/ppermute | solution.py:29
  44.8 2.4 %collective-permute-done.18.got_ref = bf16[8,3200]{1,0:T(8,128)(2,1)S(1)} collective-permute-done((bf16[8,3200]{1,0:T(8,128)(2,1)S(1)}, bf16[8,3200]{1,0:T(8,128)(2,1)S(1)}, u32[]{:S(2)}, u32[]{:S(2)}) %collective-permute-start.18) | collective-permute-done | bytes 51232 | tf_op jit(solution)/shard_map/ppermute | solution.py:29
  47.3 0.7 %shard_map.111 = (bf16[8,3072]{1,0:T(8,128)(2,1)}, f32[2,8]{1,0:T(2,128)}) custom-call(f32[8,3200]{1,0:T(8,128)S(1)} %get-tuple-element.38.own_ref, bf16[8,3200]{1,0:T(8,128)(2,1)S(1)} %collective-permute-done.18.got_ref, s32[2,8]{1,0:T(2,128)S(1)} %bitcast.15), custom_call_target="tpu_custom_call" | custom-call | tf_op jit(solution)/shard_map/pallas_call | solution.py:384
  (10 shorter events, 0.0 us)
Async XLA Ops:
  2.2 9.3 %collective-permute-start = (bf16[8,6272]{1,0:T(8,128)(2,1)}, bf16[8,6272]{1,0:T(8,128)(2,1)S(1)}, u32[]{:S(2)}, u32[]{:S(2)}) collective-permute-start(bf16[8,6272]{1,0:T(8,128)(2,1)} %shard_map.102.refs_0_), channel_id=1, source_target_pairs={{0,8},{1,9},{2,10},{3,11},{4,12},{5,13},{6,14},{7,15},{8,0},{9,1},... | collective-permute-start | bytes 301064 | tf_op jit(solution)/shard_map/ppermute | solution.py:29
  6.2 7.6 %collective-permute-start.3 = (bf16[8,6272]{1,0:T(8,128)(2,1)}, bf16[8,6272]{1,0:T(8,128)(2,1)S(1)}, u32[]{:S(2)}, u32[]{:S(2)}) collective-permute-start(bf16[8,6272]{1,0:T(8,128)(2,1)} %shard_map.102.refs_0_), channel_id=1, source_target_pairs={{0,2},{1,3},{2,0},{3,1},{4,6},{5,7},{6,4},{7,5},{8,10},{9,11},{10,... | collective-permute-start | bytes 301064 | tf_op jit(solution)/shard_map/ppermute | solution.py:29
  7.7 6.5 %collective-permute-start.1 = (bf16[8,6272]{1,0:T(8,128)(2,1)}, bf16[8,6272]{1,0:T(8,128)(2,1)S(1)}, u32[]{:S(2)}, u32[]{:S(2)}) collective-permute-start(bf16[8,6272]{1,0:T(8,128)(2,1)} %shard_map.102.refs_0_), channel_id=1, source_target_pairs={{0,4},{1,5},{2,6},{3,7},{4,0},{5,1},{6,2},{7,3},{8,12},{9,13},{10,... | collective-permute-start | bytes 301064 | tf_op jit(solution)/shard_map/ppermute | solution.py:29
  11.5 4.6 %collective-permute-start.4 = (bf16[8,6272]{1,0:T(8,128)(2,1)S(1)}, bf16[8,6272]{1,0:T(8,128)(2,1)S(1)}, u32[]{:S(2)}, u32[]{:S(2)}) collective-permute-start(bf16[8,6272]{1,0:T(8,128)(2,1)S(1)} %collective-permute-done.refs_1_), channel_id=1, source_target_pairs={{0,2},{1,3},{2,0},{3,1},{4,6},{5,7},{6,4},{7,5},{8,10},{9,11},{10,... | collective-permute-start | bytes 301064 | tf_op jit(solution)/shard_map/ppermute | solution.py:29
  13.1 4.6 %collective-permute-start.2 = (bf16[8,6272]{1,0:T(8,128)(2,1)S(1)}, bf16[8,6272]{1,0:T(8,128)(2,1)S(1)}, u32[]{:S(2)}, u32[]{:S(2)}) collective-permute-start(bf16[8,6272]{1,0:T(8,128)(2,1)S(1)} %collective-permute-done.refs_1_), channel_id=1, source_target_pairs={{0,4},{1,5},{2,6},{3,7},{4,0},{5,1},{6,2},{7,3},{8,12},{9,13},{10,... | collective-permute-start | bytes 301064 | tf_op jit(solution)/shard_map/ppermute | solution.py:29
  13.8 8.2 %collective-permute-start.7 = (bf16[8,6272]{1,0:T(8,128)(2,1)}, bf16[8,6272]{1,0:T(8,128)(2,1)S(1)}, u32[]{:S(2)}, u32[]{:S(2)}) collective-permute-start(bf16[8,6272]{1,0:T(8,128)(2,1)} %shard_map.102.refs_0_), channel_id=1, source_target_pairs={{0,1},{1,0},{2,3},{3,2},{4,5},{5,4},{6,7},{7,6},{8,9},{9,8},{10,11... | collective-permute-start | bytes 301064 | tf_op jit(solution)/shard_map/ppermute | solution.py:29
  13.8 8.3 %collective-permute-start.11 = (bf16[8,6272]{1,0:T(8,128)(2,1)S(1)}, bf16[8,6272]{1,0:T(8,128)(2,1)S(1)}, u32[]{:S(2)}, u32[]{:S(2)}) collective-permute-start(bf16[8,6272]{1,0:T(8,128)(2,1)S(1)} %collective-permute-done.3.refs_4_), channel_id=1, source_target_pairs={{0,1},{1,0},{2,3},{3,2},{4,5},{5,4},{6,7},{7,6},{8,9},{9,8},{10,11... | collective-permute-start | bytes 301064 | tf_op jit(solution)/shard_map/ppermute | solution.py:29
  14.3 8.3 %collective-permute-start.5 = (bf16[8,6272]{1,0:T(8,128)(2,1)S(1)}, bf16[8,6272]{1,0:T(8,128)(2,1)S(1)}, u32[]{:S(2)}, u32[]{:S(2)}) collective-permute-start(bf16[8,6272]{1,0:T(8,128)(2,1)S(1)} %collective-permute-done.1.refs_2_), channel_id=1, source_target_pairs={{0,2},{1,3},{2,0},{3,1},{4,6},{5,7},{6,4},{7,5},{8,10},{9,11},{10,... | collective-permute-start | bytes 301064 | tf_op jit(solution)/shard_map/ppermute | solution.py:29
  16.2 6.5 %collective-permute-start.9 = (bf16[8,6272]{1,0:T(8,128)(2,1)S(1)}, bf16[8,6272]{1,0:T(8,128)(2,1)S(1)}, u32[]{:S(2)}, u32[]{:S(2)}) collective-permute-start(bf16[8,6272]{1,0:T(8,128)(2,1)S(1)} %collective-permute-done.1.refs_2_), channel_id=1, source_target_pairs={{0,1},{1,0},{2,3},{3,2},{4,5},{5,4},{6,7},{7,6},{8,9},{9,8},{10,11... | collective-permute-start | bytes 301064 | tf_op jit(solution)/shard_map/ppermute | solution.py:29
  17.7 5.4 %collective-permute-start.6 = (bf16[8,6272]{1,0:T(8,128)(2,1)S(1)}, bf16[8,6272]{1,0:T(8,128)(2,1)S(1)}, u32[]{:S(2)}, u32[]{:S(2)}) collective-permute-start(bf16[8,6272]{1,0:T(8,128)(2,1)S(1)} %collective-permute-done.2.refs_3_), channel_id=1, source_target_pairs={{0,2},{1,3},{2,0},{3,1},{4,6},{5,7},{6,4},{7,5},{8,10},{9,11},{10,... | collective-permute-start | bytes 301064 | tf_op jit(solution)/shard_map/ppermute | solution.py:29
  18.2 1.9 %copy-start = (bf16[3072,2,256]{2,1,0:T(2,128)(2,1)S(1)}, bf16[3072,2,256]{2,1,0:T(2,128)(2,1)}, u32[]{:S(2)}) copy-start(bf16[3072,2,256]{2,1,0:T(2,128)(2,1)} %param.12) | copy-start | bytes 9437188
  20.1 4.3 %copy-start.1 = (bf16[256,3072]{1,0:T(8,128)(2,1)S(1)}, bf16[256,3072]{1,0:T(8,128)(2,1)}, u32[]{:S(2)}) copy-start(bf16[256,3072]{1,0:T(8,128)(2,1)} %refs_17_.1) | copy-start | bytes 4718596
  20.1 4.3 %copy-start.2 = (bf16[8,6272]{1,0:T(8,128)(2,1)S(1)}, bf16[8,6272]{1,0:T(8,128)(2,1)}, u32[]{:S(2)}) copy-start(bf16[8,6272]{1,0:T(8,128)(2,1)} %shard_map.102.refs_0_) | copy-start | bytes 301060
  20.1 4.3 %copy-start.4 = (s32[16]{0:T(128)S(1)}, s32[16]{0:T(128)}, u32[]{:S(2)}) copy-start(s32[16]{0:T(128)} %owner_ref.3) | copy-start | bytes 196
  22.0 1.4 %collective-permute-start.8 = (bf16[8,6272]{1,0:T(8,128)(2,1)S(1)}, bf16[8,6272]{1,0:T(8,128)(2,1)S(1)}, u32[]{:S(2)}, u32[]{:S(2)}) collective-permute-start(bf16[8,6272]{1,0:T(8,128)(2,1)S(1)} %collective-permute-done.refs_1_), channel_id=1, source_target_pairs={{0,1},{1,0},{2,3},{3,2},{4,5},{5,4},{6,7},{7,6},{8,9},{9,8},{10,11... | collective-permute-start | bytes 301064 | tf_op jit(solution)/shard_map/ppermute | solution.py:29
  22.1 2.0 %collective-permute-start.12 = (bf16[8,6272]{1,0:T(8,128)(2,1)S(1)}, bf16[8,6272]{1,0:T(8,128)(2,1)S(1)}, u32[]{:S(2)}, u32[]{:S(2)}) collective-permute-start(bf16[8,6272]{1,0:T(8,128)(2,1)S(1)} %collective-permute-done.4.refs_5_), channel_id=1, source_target_pairs={{0,1},{1,0},{2,3},{3,2},{4,5},{5,4},{6,7},{7,6},{8,9},{9,8},{10,11... | collective-permute-start | bytes 301064 | tf_op jit(solution)/shard_map/ppermute | solution.py:29
  22.6 1.3 %collective-permute-start.13 = (bf16[8,6272]{1,0:T(8,128)(2,1)S(1)}, bf16[8,6272]{1,0:T(8,128)(2,1)S(1)}, u32[]{:S(2)}, u32[]{:S(2)}) collective-permute-start(bf16[8,6272]{1,0:T(8,128)(2,1)S(1)} %collective-permute-done.5.refs_6_), channel_id=1, source_target_pairs={{0,1},{1,0},{2,3},{3,2},{4,5},{5,4},{6,7},{7,6},{8,9},{9,8},{10,11... | collective-permute-start | bytes 301064 | tf_op jit(solution)/shard_map/ppermute | solution.py:29
  22.7 1.4 %collective-permute-start.10 = (bf16[8,6272]{1,0:T(8,128)(2,1)S(1)}, bf16[8,6272]{1,0:T(8,128)(2,1)S(1)}, u32[]{:S(2)}, u32[]{:S(2)}) collective-permute-start(bf16[8,6272]{1,0:T(8,128)(2,1)S(1)} %collective-permute-done.2.refs_3_), channel_id=1, source_target_pairs={{0,1},{1,0},{2,3},{3,2},{4,5},{5,4},{6,7},{7,6},{8,9},{9,8},{10,11... | collective-permute-start | bytes 301064 | tf_op jit(solution)/shard_map/ppermute | solution.py:29
  23.1 1.3 %collective-permute-start.14 = (bf16[8,6272]{1,0:T(8,128)(2,1)S(1)}, bf16[8,6272]{1,0:T(8,128)(2,1)S(1)}, u32[]{:S(2)}, u32[]{:S(2)}) collective-permute-start(bf16[8,6272]{1,0:T(8,128)(2,1)S(1)} %collective-permute-done.6.refs_7_), channel_id=1, source_target_pairs={{0,1},{1,0},{2,3},{3,2},{4,5},{5,4},{6,7},{7,6},{8,9},{9,8},{10,11... | collective-permute-start | bytes 301064 | tf_op jit(solution)/shard_map/ppermute | solution.py:29
  27.8 1.8 %collective-permute-start.15 = (bf16[64,3200]{1,0:T(8,128)(2,1)S(1)}, bf16[64,3200]{1,0:T(8,128)(2,1)S(1)}, u32[]{:S(2)}, u32[]{:S(2)}) collective-permute-start(bf16[64,3200]{1,0:T(8,128)(2,1)S(1)} %get-tuple-element.28), channel_id=1, source_target_pairs={{0,1},{1,0},{2,3},{3,2},{4,5},{5,4},{6,7},{7,6},{8,9},{9,8},{10,11... | collective-permute-start | bytes 1228808 | tf_op jit(solution)/shard_map/ppermute | solution.py:29
  29.7 17.6 %copy-start.3 = (s32[8,2]{0,1:T(2,128)S(1)}, s32[8,2]{0,1:T(2,128)}, u32[]{:S(2)}) copy-start(s32[8,2]{0,1:T(2,128)} %param.9) | copy-start | bytes 196
  29.8 7.4 %collective-permute-start.16 = (bf16[32,3200]{1,0:T(8,128)(2,1)S(1)}, bf16[32,3200]{1,0:T(8,128)(2,1)S(1)}, u32[]{:S(2)}, u32[]{:S(2)}) collective-permute-start(bf16[32,3200]{1,0:T(8,128)(2,1)S(1)} %get-tuple-element.30), channel_id=1, source_target_pairs={{0,2},{1,3},{2,0},{3,1},{4,6},{5,7},{6,4},{7,5},{8,10},{9,11},{10,... | collective-permute-start | bytes 614408 | tf_op jit(solution)/shard_map/ppermute | solution.py:29
  37.4 4.7 %collective-permute-start.17 = (bf16[16,3200]{1,0:T(8,128)(2,1)S(1)}, bf16[16,3200]{1,0:T(8,128)(2,1)S(1)}, u32[]{:S(2)}, u32[]{:S(2)}) collective-permute-start(bf16[16,3200]{1,0:T(8,128)(2,1)S(1)} %get-tuple-element.34), channel_id=1, source_target_pairs={{0,4},{1,5},{2,6},{3,7},{4,0},{5,1},{6,2},{7,3},{8,12},{9,13},{10,... | collective-permute-start | bytes 307208 | tf_op jit(solution)/shard_map/ppermute | solution.py:29
  42.2 5.0 %collective-permute-start.18 = (bf16[8,3200]{1,0:T(8,128)(2,1)S(1)}, bf16[8,3200]{1,0:T(8,128)(2,1)S(1)}, u32[]{:S(2)}, u32[]{:S(2)}) collective-permute-start(bf16[8,3200]{1,0:T(8,128)(2,1)S(1)} %get-tuple-element.39), channel_id=1, source_target_pairs={{0,8},{1,9},{2,10},{3,11},{4,12},{5,13},{6,14},{7,15},{8,0},{9,1},... | collective-permute-start | bytes 153608 | tf_op jit(solution)/shard_map/ppermute | solution.py:29

commit v3 on v2

--- a/solution.py
+++ b/solution.py
@@ -26,7 +26,8 @@
 
 def xor_swap(value, bit):
     n = lax.axis_size("dev")
-    return lax.ppermute(value, "dev", [(i, i ^ bit) for i in range(n)])
+    other = {2: 4, 4: 2}.get(bit, bit) if n >= 8 else bit
+    return lax.ppermute(value, "dev", [(i, i ^ (other if i & 1 else bit)) for i in range(n)])
 
 
 def xor_bits(n):
@@ -78,13 +79,27 @@
     return (col == (row % per) * group + row // per).astype(BF)
 
 
-def split_kernel(w_ref, out_ref):
+def split_kernel(part, w_hbm, out_ref, w_ref, sems):
     d, wide = out_ref.shape
     group = wide // LANES
     per = SIDE // group
     tiles = group // 2
     take = shuffle(group)
+    parts = sems.shape[0]
+    size = d * group // parts
+    copies = [
+        pltpu.make_async_copy(
+            w_hbm.at[pl.ds((part * parts + i) * size, size), :],
+            w_ref.at[pl.ds(i * size, size), :],
+            sems.at[i],
+        )
+        for i in range(parts)
+    ]
+    for copy in copies:
+        copy.start()
     for s in range(0, d // per, 2):
+        if s * SIDE % size == 0:
+            copies[s * SIDE // size].wait()
         pair = jnp.concatenate(
             [w_ref[s * SIDE : (s + 1) * SIDE, :], w_ref[(s + 1) * SIDE : (s + 2) * SIDE, :]], 1
         )
@@ -98,20 +113,23 @@
                 ]
 
 
-def split_weights(w_in, block=512):
+def lane_rows(w_in):
     d, two, hid = w_in.shape
     tiles = hid // LANES
-    group = two * tiles
-    view = w_in.reshape(d, two, tiles, LANES).transpose(0, 2, 1, 3).reshape(d * group, LANES)
+    return w_in.reshape(d, two, tiles, LANES).transpose(0, 2, 1, 3).reshape(-1, LANES)
+
+
+def split_weights(view, part, d, wide):
+    rows = view.shape[0] // 2
     return pl.pallas_call(
-        split_kernel,
-        grid=(d // block,),
-        in_specs=[pl.BlockSpec((block * group, LANES), lambda i: (i, 0))],
-        out_specs=pl.BlockSpec((block, two * hid), lambda i: (i, 0)),
-        out_shape=jax.ShapeDtypeStruct((d, two * hid), BF),
-        compiler_params=params(),
+        functools.partial(split_kernel, part),
+        in_specs=[ANY],
+        out_specs=VMEM,
+        out_shape=jax.ShapeDtypeStruct((d // 2, wide), BF),
+        scratch_shapes=[pltpu.VMEM((rows, LANES), BF), pltpu.SemaphoreType.DMA((3,))],
+        compiler_params=params(50),
         cost_estimate=pl.CostEstimate(
-            flops=2 * d * group * SIDE * LANES, bytes_accessed=8 * d * hid, transcendentals=0
+            flops=2 * rows * SIDE * LANES, bytes_accessed=4 * rows * LANES, transcendentals=0
         ),
     )(view)
 
@@ -126,19 +144,13 @@
     out_ref[:, width:] = pair.astype(out_ref.dtype)
 
 
-def token_part(pre, w_ref, out_ref, width, step=768):
-    for c in range(0, width, step):
-        out_ref[:, c : c + step] = lax.dot_general(
-            pre, w_ref[c : c + step, :], NT, preferred_element_type=F32
-        ).astype(out_ref.dtype)
-
-
 def main_kernel(n, owner_ref, *refs):
     pieces, refs = refs[:n], refs[n:]
-    w_ref, down_ref, tok_ref, scaled_ref, pre_ref, hid_ref, gate_ref, send_ref, grad_ref = refs
+    low_ref, high_ref, down_ref, tok_ref, grad_ref, pre_ref, hid_ref, prob_ref, own_ref, send_ref = refs
     rows = pieces[0].shape[0]
     width = down_ref.shape[1]
     hid = down_ref.shape[0]
+    cut = low_ref.shape[0]
     expert = owner_ref[lax.axis_index("dev")]
     metas = []
     for i in range(0, n, 2):
@@ -154,7 +166,9 @@
     prob = jnp.sum(
         jnp.where((lane >= EXP_WIN) & (lane % EXP_WIN == expert), meta, 0.0), 1, keepdims=True
     )
-    projected = jnp.dot(tok_ref[...], w_ref[...], preferred_element_type=F32)
+    prob_ref[...] = jnp.broadcast_to(prob, prob_ref.shape)
+    projected = jnp.dot(tok_ref[:, :cut], low_ref[...], preferred_element_type=F32)
+    projected += jnp.dot(tok_ref[:, cut:], high_ref[...], preferred_element_type=F32)
     gate, up = projected[:, :hid], projected[:, hid:]
     back = lax.dot_general(grad_ref[...], down_ref[...], NT, preferred_element_type=F32)
     logistic = jax.nn.sigmoid(gate)
@@ -166,54 +180,58 @@
     pre_gate = hidden_grad * up * logistic * (1.0 + gate * (1.0 - logistic))
     pre_ref[:, :hid] = pre_gate.astype(BF)
     pre_ref[:, hid:] = (hidden_grad * activated).astype(BF)
-    gate_ref[...] = jnp.broadcast_to(gate_sum, gate_ref.shape)
     half = n * rows // 2
+    put_gate(own_ref, gate_sum[:half], expert, width)
     put_gate(send_ref, gate_sum[half:], expert, width)
-    token_part(pre_ref[half:, :], w_ref, send_ref, width)
-    scaled_ref[...] = (prob * grad_ref[...].astype(F32)).astype(BF)
-
-
-def own_kernel(owner_ref, pre_ref, w_ref, gate_ref, out_ref):
-    half = out_ref.shape[0]
-    width = w_ref.shape[0]
-    put_gate(out_ref, gate_ref[:half, :1], owner_ref[lax.axis_index("dev")], width)
-    token_part(pre_ref[:half, :], w_ref, out_ref, width)
-
-
-def add_kernel(own_ref, got_ref, after_ref, keep_ref, send_ref):
-    total = own_ref[...] + got_ref[...].astype(F32)
-    half = keep_ref.shape[0]
+    step = cut // 2
+    for c in range(0, width, step):
+        weights = low_ref if c < cut else high_ref
+        start = c if c < cut else c - cut
+        part = lax.dot_general(
+            pre_ref[...], weights[start : start + step, :], NT, preferred_element_type=F32
+        )
+        own_ref[:, c : c + step] = part[:half]
+        send_ref[:, c : c + step] = part[half:].astype(BF)
+
+
+def add_kernel(parts, own_ref, *refs):
+    got, (keep_ref, *send_refs) = refs[: -parts - 1], refs[-parts:]
+    total = own_ref[...]
+    for got_ref in got:
+        total += got_ref[...].astype(F32)
+    rows = keep_ref.shape[0]
     width = total.shape[1] - META
-    keep_ref[...] = total[:half]
-    send_ref[:, :width] = total[half:, :width].astype(BF)
-    tail = total[half:, width:]
-    lane = lax.broadcasted_iota(jnp.int32, tail.shape, 1)
-    value = tail + pltpu.roll(tail, META - EXP_WIN, 1)
-    high = value.astype(BF).astype(F32)
-    low = pltpu.roll(value - high, EXP_WIN, 1)
-    pair = jnp.where(lane < EXP_WIN, high, jnp.where(lane < 2 * EXP_WIN, low, 0.0))
-    send_ref[:, width:] = pair.astype(BF)
-
-
-def add_step(own, got, after):
+    keep_ref[...] = total[:rows]
+    for i, send_ref in enumerate(send_refs, 1):
+        here = total[i * rows : (i + 1) * rows]
+        send_ref[:, :width] = here[:, :width].astype(BF)
+        tail = here[:, width:]
+        lane = lax.broadcasted_iota(jnp.int32, tail.shape, 1)
+        value = tail + pltpu.roll(tail, META - EXP_WIN, 1)
+        high = value.astype(BF).astype(F32)
+        low = pltpu.roll(value - high, EXP_WIN, 1)
+        pair = jnp.where(lane < EXP_WIN, high, jnp.where(lane < 2 * EXP_WIN, low, 0.0))
+        send_ref[:, width:] = pair.astype(BF)
+
+
+def add_step(own, got, after, parts):
     rows, width = own.shape
-    half = rows // 2
-    return pl.pallas_call(
-        add_kernel,
-        in_specs=[VMEM, VMEM, ANY],
-        out_specs=[VMEM, VMEM],
-        out_shape=[
-            jax.ShapeDtypeStruct((half, width), F32),
-            jax.ShapeDtypeStruct((half, width), BF),
-        ],
+    part = rows // parts
+    keep, *send = pl.pallas_call(
+        functools.partial(add_kernel, parts),
+        in_specs=[VMEM] * (1 + len(got)) + [ANY],
+        out_specs=[VMEM] * parts,
+        out_shape=[jax.ShapeDtypeStruct((part, width), F32)]
+        + [jax.ShapeDtypeStruct((part, width), BF)] * (parts - 1),
         compiler_params=params(),
         cost_estimate=pl.CostEstimate(
             flops=rows * width, bytes_accessed=8 * rows * width, transcendentals=0
         ),
-    )(own, got, after)
-
-
-def last_kernel(own_ref, got_ref, ids_ref, tok_ref, gates_ref):
+    )(own, *got, after)
+    return keep, send
+
+
+def last_kernel(own_ref, got_ref, ids_ref, after_ref, tok_ref, gates_ref):
     total = own_ref[...] + got_ref[...].astype(F32)
     rows = total.shape[0]
     width = total.shape[1] - META
@@ -261,44 +279,48 @@
     token_ref[...] = jnp.zeros_like(token_ref)
 
 
-def grad_in(tok, pre, block=512):
+def grad_in(tok, pre, after, first, count, out=None, block=512):
     rows, d = tok.shape
-    hid = pre.shape[1] // 2
-    tiles = hid // LANES
-    group = 2 * tiles
-    out, token = pl.pallas_call(
-        win_kernel,
-        grid=(d // block,),
+    wide = pre.shape[1]
+    group = wide // LANES
+    kernel = lambda t, p, *refs: win_kernel(t, p, refs[-2], refs[-1])
+    return pl.pallas_call(
+        kernel,
+        grid=(count,),
         in_specs=[
-            pl.BlockSpec((rows, block), lambda i: (0, i)),
-            pl.BlockSpec((rows, 2 * hid), lambda i: (0, 0)),
-        ],
+            pl.BlockSpec((rows, block), lambda i: (0, i + first)),
+            pl.BlockSpec((rows, wide), lambda i: (0, 0)),
+            ANY,
+        ]
+        + ([] if out is None else [ANY]),
         out_specs=[
-            pl.BlockSpec((block * group, LANES), lambda i: (i, 0)),
+            pl.BlockSpec((block * group, LANES), lambda i: (i + first, 0)),
             pl.BlockSpec((8, LANES), lambda i: (0, 0)),
         ],
         out_shape=[
             jax.ShapeDtypeStruct((d * group, LANES), BF),
             jax.ShapeDtypeStruct((8, LANES), F32),
         ],
+        input_output_aliases={} if out is None else {3: 0},
         compiler_params=params(),
         cost_estimate=pl.CostEstimate(
-            flops=4 * rows * d * hid, bytes_accessed=8 * d * hid, transcendentals=0
-        ),
-    )(tok, pre)
-    out = out.reshape(d, tiles, 2, LANES).transpose(0, 2, 1, 3).reshape(d, 2, hid)
-    return out, token
-
-
-def down_kernel(hid_ref, scaled_ref, out_ref, token_ref):
+            flops=2 * rows * count * block * wide,
+            bytes_accessed=4 * count * block * wide,
+            transcendentals=0,
+        ),
+    )(tok, pre, after, *([] if out is None else [out]))
+
+
+def down_kernel(hid_ref, grad_ref, prob_ref, after_ref, out_ref, token_ref):
     token_ref[...] = jnp.zeros_like(token_ref)
+    scaled = (prob_ref[:, :1] * grad_ref[...].astype(F32)).astype(BF)
     out_ref[...] = lax.dot_general(
-        hid_ref[...], scaled_ref[...], TN, preferred_element_type=F32
+        hid_ref[...], scaled, TN, preferred_element_type=F32
     ).astype(BF)
 
 
-def grad_down(hidden, scaled, block=768):
-    rows, d = scaled.shape
+def grad_down(hidden, grads, prob, after, block=768):
+    rows, d = grads.shape
     hid = hidden.shape[1]
     return pl.pallas_call(
         down_kernel,
@@ -306,6 +328,8 @@
         in_specs=[
             pl.BlockSpec((rows, hid), lambda i: (0, 0)),
             pl.BlockSpec((rows, block), lambda i: (0, i)),
+            pl.BlockSpec((rows, META), lambda i: (0, 0)),
+            ANY,
         ],
         out_specs=[
             pl.BlockSpec((hid, block), lambda i: (0, i)),
@@ -319,7 +343,7 @@
         cost_estimate=pl.CostEstimate(
             flops=2 * rows * d * hid, bytes_accessed=4 * d * hid, transcendentals=0
         ),
-    )(hidden, scaled)
+    )(hidden, grads, prob, after)
 
 
 def shards(tokens, grad_out, expert_ids, gate_probs, device_expert, w_in, w_down):
@@ -338,59 +362,71 @@
         compiler_params=params(60),
     )(tokens, grad_out, ids_t, probs_t)
 
+    order = [0]
+    for bit in bits:
+        order = order + [o ^ bit for o in order]
+    view = lane_rows(w_in)
     held = {0: own}
-    order = [0]
-    w_flat = split_weights(w_in)
-    for step, bit in enumerate(bits):
-        for o in order:
-            held[o ^ bit] = xor_swap(held[o], bit)
-        if bit == 2:
-            last = order[1] ^ bit
-            held[last], w_flat = lax.optimization_barrier((held[last], w_flat))
-        order = order + [o ^ bit for o in order]
+    far, near = n // 2, n // 4
+    cross = near + 2
+
+    def piece(o):
+        if o not in held:
+            bit = near if o == cross else o & -o
+            held[o] = xor_swap(piece(o ^ bit), bit)
+        return held[o]
+
+    weights = []
+    for part, o in enumerate((far, far + near)):
+        half_split = split_weights(view, part, width, 2 * hid)
+        held[o], half_split = lax.optimization_barrier((piece(o), half_split))
+        weights.append(half_split)
+    for o in order:
+        piece(o)
 
     total = n * rows
     half = total // 2
-    tok, scaled, pre, hidden, gate, send = pl.pallas_call(
+    tok, grads, pre, hidden, prob, mine, send = pl.pallas_call(
         functools.partial(main_kernel, n),
-        in_specs=[SMEM] + [VMEM] * (n + 2),
-        out_specs=[VMEM] * 6,
+        in_specs=[SMEM] + [VMEM] * (n + 3),
+        out_specs=[VMEM] * 7,
         out_shape=[
             jax.ShapeDtypeStruct((total, width), BF),
             jax.ShapeDtypeStruct((total, width), BF),
             jax.ShapeDtypeStruct((total, 2 * hid), BF),
             jax.ShapeDtypeStruct((total, hid), BF),
             jax.ShapeDtypeStruct((total, META), F32),
+            jax.ShapeDtypeStruct((half, width + META), F32),
             jax.ShapeDtypeStruct((half, width + META), BF),
         ],
-        scratch_shapes=[pltpu.VMEM((total, width), BF)],
         compiler_params=params(),
-    )(device_expert, *[held[o] for o in order], w_flat, w_down)
-
-    got = xor_swap(send, 1)
-    mine = pl.pallas_call(
-        own_kernel,
-        in_specs=[SMEM] + [VMEM] * 3,
-        out_specs=VMEM,
-        out_shape=jax.ShapeDtypeStruct((half, width + META), F32),
-        compiler_params=params(),
-    )(device_expert, pre, w_flat, gate)
-    grad_w_in, after_in = grad_in(tok, pre)
-    grad_w_down, after_down = grad_down(hidden, scaled)
-    for step, bit in enumerate(bits[-2::-1]):
-        mine, send = add_step(mine, got, (gate, after_in, after_down)[min(step, 2)])
-        got = xor_swap(send, bit)
-
+    )(device_expert, *[held[o] for o in order], *weights, w_down)
+
+    steps = width // 512
+    first = 2
+    got = [xor_swap(send, 1)]
+    grad_w_in, after = grad_in(tok, pre, prob, 0, first)
+    mine, (by_near, by_side, by_both) = add_step(mine, got, after, 4)
+    got = [xor_swap(by_both, 6), xor_swap(by_side, 2), xor_swap(by_near, 4)]
+    grad_w_down, after = grad_down(hidden, grads, prob, mine)
+    for bit in bits[-4::-1]:
+        mine, (send,) = add_step(mine, got, after, 2)
+        got = [xor_swap(send, bit)]
+        if bit == 8:
+            grad_w_in, after = grad_in(tok, pre, mine, first, steps - first, grad_w_in)
+    tiles = hid // LANES
+    grad_w_in = grad_w_in.reshape(width, tiles, 2, LANES).transpose(0, 2, 1, 3)
+    grad_w_in = grad_w_in.reshape(width, 2, hid)
     grad_tokens, gates_t = pl.pallas_call(
         last_kernel,
-        in_specs=[VMEM] * 3,
+        in_specs=[VMEM] * 3 + [ANY],
         out_specs=[VMEM] * 2,
         out_shape=[
             jax.ShapeDtypeStruct((rows, width), BF),
             jax.ShapeDtypeStruct((expert_ids.shape[1], rows), F32),
         ],
         compiler_params=params(),
-    )(mine, got, ids_t)
+    )(mine, *got, ids_t, after)
     return grad_tokens, gates_t.T, grad_w_in, grad_w_down
 
 

time: 48.2 us -> 45 us (0.934)
  waiting for transfers between devices: 11.4 us -> 6.88 us
  starting transfers between devices: 17.3 us -> 19.5 us
  local copies, waits for them, and re-layouts: 1.91 us -> 0.02 us
  Pallas kernels: 16.7 us -> 17.7 us
    ppermute x19 -> x20, waiting for transfers between devices: 11.4 us -> 6.88 us  [xor_swap(): lax.ppermute(value, 'dev', [(i, i ^ (other if i & 1 else bit)) for i in r...]
    ppermute x19 -> x20, starting transfers between devices: 17.3 us -> 19.5 us  [xor_swap(): lax.ppermute(value, 'dev', [(i, i ^ (other if i & 1 else bit)) for i in r...]
    unnamed x10 -> x8, local copies, waits for them, and re-layouts: 1.91 us -> 0.02 us
    pallas_call x7, Pallas kernels: 9.3 us -> 10.2 us  [the longest x2 5.22 us: grad_in(): pl.pallas_call(kernel, grid=(count,), in_specs=[pl.BlockSpec((rows, block...]
  transfers between devices with their start and end apart: 19 -> 20, of which waited for: 10 -> 8; matrix products, arithmetic and copies ran while one was open for 0% -> 0% of each run, Pallas kernels for 22% -> 26%
where the time goes in v3:
time: 45 us; the launch traced here: 44.8 us
  starting transfers between devices  19.5 us (43%)
  Pallas kernels  17.7 us (39%)
  waiting for transfers between devices  6.88 us (15%)
  between operations  0.71 us (2%)
    ppermute x20, starting transfers between devices, xor_swap(): lax.ppermute(value, 'dev', [(i, i ^ (other if i & 1 else bit)) for i in r...  19.5 us
    ppermute x20, waiting for transfers between devices, xor_swap(): lax.ppermute(value, 'dev', [(i, i ^ (other if i & 1 else bit)) for i in r...  6.88 us
    pallas_call x2, Pallas kernels, grad_in(): pl.pallas_call(kernel, grid=(count,), in_specs=[pl.BlockSpec((rows, block...  5.22 us
    pallas_call x2, Pallas kernels, split_weights(): pl.pallas_call(functools.partial(split_kernel, part), in_specs=[ANY], out...  4 us
    pallas_call x1, Pallas kernels, shards(): pl.pallas_call(functools.partial(main_kernel, n), in_specs=[SMEM] + [VMEM...  3.39 us
    pallas_call x1, Pallas kernels, grad_down(): pl.pallas_call(down_kernel, grid=(d // block,), in_specs=[pl.BlockSpec((r...  2.52 us
    pallas_call x1, Pallas kernels, shards(): pl.pallas_call(pack_kernel, in_specs=[VMEM] * 4, out_specs=VMEM, out_shap...  1.56 us
  transfers between devices with their start and end apart: 20, of which 8 were waited for; matrix products, arithmetic and copies ran while one was open for 0% of the time, Pallas kernels for 26%

profile of v3, /device:TPU:0, one launch (start us, length us, event | category | flops | bytes accessed | tf_op | source)
XLA Modules:
  0.0 44.8 jit_solution(2444441263088274352)
XLA Ops:
  0.6 1.6 %shard_map.102.refs_0_ = bf16[8,6272]{1,0:T(8,128)(2,1)} custom-call(bf16[8,3072]{1,0:T(8,128)(2,1)} %tok_ref.1, bf16[8,3072]{1,0:T(8,128)(2,1)} %grad_ref.1, s32[2,8]{1,0:T(2,128)} %bitcast.13, f32[2,8]{1,0:T(2,128)} %bitcast.18), custom_call_target="tpu_custom_call" | custom-call | tf_op jit(solution)/shard_map/pallas_call | solution.py:357
  2.2 4.0 %collective-permute-start = (bf16[8,6272]{1,0:T(8,128)(2,1)}, bf16[8,6272]{1,0:T(8,128)(2,1)S(1)}, u32[]{:S(2)}, u32[]{:S(2)}) collective-permute-start(bf16[8,6272]{1,0:T(8,128)(2,1)} %shard_map.102.refs_0_), channel_id=1, source_target_pairs={{0,8},{1,9},{2,10},{3,11},{4,12},{5,13},{6,14},{7,15},{8,0},{9,1},... | collective-permute-start | bytes 301064 | tf_op jit(solution)/shard_map/ppermute | solution.py:30
  6.2 1.5 %collective-permute-start.3 = (bf16[8,6272]{1,0:T(8,128)(2,1)}, bf16[8,6272]{1,0:T(8,128)(2,1)S(1)}, u32[]{:S(2)}, u32[]{:S(2)}) collective-permute-start(bf16[8,6272]{1,0:T(8,128)(2,1)} %shard_map.102.refs_0_), channel_id=1, source_target_pairs={{0,2},{1,5},{2,0},{3,7},{4,6},{5,1},{6,4},{7,3},{8,10},{9,13},{10,... | collective-permute-start | bytes 301064 | tf_op jit(solution)/shard_map/ppermute | solution.py:30
  7.7 1.6 %collective-permute-start.1 = (bf16[8,6272]{1,0:T(8,128)(2,1)}, bf16[8,6272]{1,0:T(8,128)(2,1)S(1)}, u32[]{:S(2)}, u32[]{:S(2)}) collective-permute-start(bf16[8,6272]{1,0:T(8,128)(2,1)} %shard_map.102.refs_0_), channel_id=1, source_target_pairs={{0,4},{1,3},{2,6},{3,1},{4,0},{5,7},{6,2},{7,5},{8,12},{9,11},{10,... | collective-permute-start | bytes 301064 | tf_op jit(solution)/shard_map/ppermute | solution.py:30
  9.3 2.0 %shard_map.103.refs_16_ = bf16[1536,512]{1,0:T(8,128)(2,1)S(1)} custom-call(bf16[12288,128]{1,0:T(8,128)(2,1)} %bitcast.15), custom_call_target="tpu_custom_call" | custom-call | flops 402653184 | bytes 3145728 | tf_op jit(solution)/shard_map/pallas_call | solution.py:124
  11.4 0.0 copy-start
  11.4 0.0 copy-start.3
  11.4 0.0 collective-permute-done.refs_1_
  11.4 0.9 %collective-permute-start.2 = (bf16[8,6272]{1,0:T(8,128)(2,1)S(1)}, bf16[8,6272]{1,0:T(8,128)(2,1)S(1)}, u32[]{:S(2)}, u32[]{:S(2)}) collective-permute-start(bf16[8,6272]{1,0:T(8,128)(2,1)S(1)} %collective-permute-done.refs_1_), channel_id=1, source_target_pairs={{0,4},{1,3},{2,6},{3,1},{4,0},{5,7},{6,2},{7,5},{8,12},{9,11},{10,... | collective-permute-start | bytes 301064 | tf_op jit(solution)/shard_map/ppermute | solution.py:30
  12.3 0.0 collective-permute-start.7
  12.3 2.0 %shard_map.104.refs_17_ = bf16[1536,512]{1,0:T(8,128)(2,1)S(1)} custom-call(bf16[12288,128]{1,0:T(8,128)(2,1)} %bitcast.16), custom_call_target="tpu_custom_call" | custom-call | flops 402653184 | bytes 3145728 | tf_op jit(solution)/shard_map/pallas_call | solution.py:124
  14.3 1.5 %collective-permute-start.4 = (bf16[8,6272]{1,0:T(8,128)(2,1)S(1)}, bf16[8,6272]{1,0:T(8,128)(2,1)S(1)}, u32[]{:S(2)}, u32[]{:S(2)}) collective-permute-start(bf16[8,6272]{1,0:T(8,128)(2,1)S(1)} %collective-permute-done.refs_1_), channel_id=1, source_target_pairs={{0,2},{1,5},{2,0},{3,7},{4,6},{5,1},{6,4},{7,3},{8,10},{9,13},{10,... | collective-permute-start | bytes 301064 | tf_op jit(solution)/shard_map/ppermute | solution.py:30
  15.8 0.0 collective-permute-done.3.refs_4_
  15.8 0.0 collective-permute-start.11
  15.8 0.0 collective-permute-done.1.refs_2_
  15.8 1.4 %collective-permute-start.5 = (bf16[8,6272]{1,0:T(8,128)(2,1)S(1)}, bf16[8,6272]{1,0:T(8,128)(2,1)S(1)}, u32[]{:S(2)}, u32[]{:S(2)}) collective-permute-start(bf16[8,6272]{1,0:T(8,128)(2,1)S(1)} %collective-permute-done.3.refs_4_), channel_id=1, source_target_pairs={{0,4},{1,3},{2,6},{3,1},{4,0},{5,7},{6,2},{7,5},{8,12},{9,11},{10,... | collective-permute-start | bytes 301064 | tf_op jit(solution)/shard_map/ppermute | solution.py:30
  17.3 0.0 collective-permute-done.2.refs_3_
  17.3 0.0 collective-permute-start.9
  17.3 0.0 collective-permute-done.7.refs_8_
  17.3 0.9 %collective-permute-start.6 = (bf16[8,6272]{1,0:T(8,128)(2,1)S(1)}, bf16[8,6272]{1,0:T(8,128)(2,1)S(1)}, u32[]{:S(2)}, u32[]{:S(2)}) collective-permute-start(bf16[8,6272]{1,0:T(8,128)(2,1)S(1)} %collective-permute-done.2.refs_3_), channel_id=1, source_target_pairs={{0,2},{1,5},{2,0},{3,7},{4,6},{5,1},{6,4},{7,3},{8,10},{9,13},{10,... | collective-permute-start | bytes 301064 | tf_op jit(solution)/shard_map/ppermute | solution.py:30
  18.2 0.0 collective-permute-done.11.refs_12_
  18.2 0.0 collective-permute-start.8
  18.2 2.6 %collective-permute-done.5.refs_6_ = bf16[8,6272]{1,0:T(8,128)(2,1)S(1)} collective-permute-done((bf16[8,6272]{1,0:T(8,128)(2,1)S(1)}, bf16[8,6272]{1,0:T(8,128)(2,1)S(1)}, u32[]{:S(2)}, u32[]{:S(2)}) %collective-permute-start.5) | collective-permute-done | bytes 100384 | tf_op jit(solution)/shard_map/ppermute | solution.py:30
  20.7 0.0 collective-permute-start.10
  20.8 0.5 %collective-permute-start.13 = (bf16[8,6272]{1,0:T(8,128)(2,1)S(1)}, bf16[8,6272]{1,0:T(8,128)(2,1)S(1)}, u32[]{:S(2)}, u32[]{:S(2)}) collective-permute-start(bf16[8,6272]{1,0:T(8,128)(2,1)S(1)} %collective-permute-done.5.refs_6_), channel_id=1, source_target_pairs={{0,1},{1,0},{2,3},{3,2},{4,5},{5,4},{6,7},{7,6},{8,9},{9,8},{10,11... | collective-permute-start | bytes 301064 | tf_op jit(solution)/shard_map/ppermute | solution.py:30
  21.3 0.1 collective-permute-start.12
  21.3 0.6 %collective-permute-done.6.refs_7_ = bf16[8,6272]{1,0:T(8,128)(2,1)S(1)} collective-permute-done((bf16[8,6272]{1,0:T(8,128)(2,1)S(1)}, bf16[8,6272]{1,0:T(8,128)(2,1)S(1)}, u32[]{:S(2)}, u32[]{:S(2)}) %collective-permute-start.6) | collective-permute-done | bytes 100384 | tf_op jit(solution)/shard_map/ppermute | solution.py:30
  22.0 0.0 collective-permute-start.14
  22.0 0.0 collective-permute-done.8.refs_9_
  22.0 0.2 collective-permute-done.13.refs_14_
  22.2 0.4 collective-permute-done.12.refs_13_
  22.6 0.7 %collective-permute-done.14.refs_15_ = bf16[8,6272]{1,0:T(8,128)(2,1)S(1)} collective-permute-done((bf16[8,6272]{1,0:T(8,128)(2,1)S(1)}, bf16[8,6272]{1,0:T(8,128)(2,1)S(1)}, u32[]{:S(2)}, u32[]{:S(2)}) %collective-permute-start.14) | collective-permute-done | bytes 100384 | tf_op jit(solution)/shard_map/ppermute | solution.py:30
  23.3 3.4 %shard_map.105 = (bf16[128,3072]{1,0:T(8,128)(2,1)S(1)}, bf16[128,3072]{1,0:T(8,128)(2,1)S(1)}, bf16[128,512]{1,0:T(8,128)(2,1)S(1)}, bf16[128,256]{1,0:T(8,128)...) custom-call(s32[16]{0:T(128)S(1)} %copy-done.3, ...), custom_call_target="tpu_custom_call" | custom-call | tf_op jit(solution)/shard_map/pallas_call | solution.py:389
  26.7 0.2 collective-permute-start.15
  26.9 1.9 %shard_map.106 = (bf16[12288,128]{1,0:T(8,128)(2,1)}, f32[8,128]{1,0:T(8,128)S(1)}) custom-call(bf16[128,3072]{1,0:T(8,128)(2,1)S(1)} %get-tuple-element.35.t, bf16[128,512]{1,0:T(8,128)(2,1)S(1)} %get-tuple-element.36.p, f32[128,128]{1,0:T(8,128)S(1)} %get-tuple-element.37.refs_0_.prob_ref), custom_call_target="tpu_custom_call" | custom-call | flops 134217728 | bytes 2097152 | tf_op jit(solution)/shard_map/pallas_call | solution.py:287
  28.8 0.2 shard_map.107
  29.0 1.7 %collective-permute-start.16 = (bf16[16,3200]{1,0:T(8,128)(2,1)S(1)}, bf16[16,3200]{1,0:T(8,128)(2,1)S(1)}, u32[]{:S(2)}, u32[]{:S(2)}) collective-permute-start(bf16[16,3200]{1,0:T(8,128)(2,1)S(1)} %get-tuple-element.40), channel_id=1, source_target_pairs={{0,6},{1,7},{2,4},{3,5},{4,2},{5,3},{6,0},{7,1},{8,14},{9,15},{10,... | collective-permute-start | bytes 307208 | tf_op jit(solution)/shard_map/ppermute | solution.py:30
  30.7 1.5 %collective-permute-start.17 = (bf16[16,3200]{1,0:T(8,128)(2,1)S(1)}, bf16[16,3200]{1,0:T(8,128)(2,1)S(1)}, u32[]{:S(2)}, u32[]{:S(2)}) collective-permute-start(bf16[16,3200]{1,0:T(8,128)(2,1)S(1)} %get-tuple-element.41), channel_id=1, source_target_pairs={{0,2},{1,5},{2,0},{3,7},{4,6},{5,1},{6,4},{7,3},{8,10},{9,13},{10,... | collective-permute-start | bytes 307208 | tf_op jit(solution)/shard_map/ppermute | solution.py:30
  32.2 0.4 collective-permute-start.18
  32.6 2.5 %shard_map.108 = (bf16[256,3072]{1,0:T(8,128)(2,1)}, f32[8,128]{1,0:T(8,128)S(1)}) custom-call(bf16[128,256]{1,0:T(8,128)(2,1)S(1)} %get-tuple-element.43.hid_ref, bf16[128,3072]{1,0:T(8,128)(2,1)S(1)} %get-tuple-element.44.grad_ref, f32[128,128]{1,0:T(8,128)S(1)} %get-tuple-element.37.refs_0_.prob_ref, f32[16,3200]{1,0:T(8,128)S(1)} %get-tuple-element.39.after_ref.own_ref), custom_call_target="tpu_custom_call" | custom-call | flops 201326592 | bytes 3145728 | tf_op jit(solution)/shard_map/pallas_call | solution.py:325
  35.1 0.6 %collective-permute-done.16.refs_0_ = bf16[16,3200]{1,0:T(8,128)(2,1)S(1)} collective-permute-done((bf16[16,3200]{1,0:T(8,128)(2,1)S(1)}, bf16[16,3200]{1,0:T(8,128)(2,1)S(1)}, u32[]{:S(2)}, u32[]{:S(2)}) %collective-permute-start.16) | collective-permute-done | bytes 102432 | tf_op jit(solution)/shard_map/ppermute | solution.py:30
  35.7 1.6 %collective-permute-done.17.refs_1_ = bf16[16,3200]{1,0:T(8,128)(2,1)S(1)} collective-permute-done((bf16[16,3200]{1,0:T(8,128)(2,1)S(1)}, bf16[16,3200]{1,0:T(8,128)(2,1)S(1)}, u32[]{:S(2)}, u32[]{:S(2)}) %collective-permute-start.17) | collective-permute-done | bytes 102432 | tf_op jit(solution)/shard_map/ppermute | solution.py:30
  37.3 0.2 collective-permute-done.18.refs_2_
  37.4 0.1 shard_map.109
  37.6 3.2 %collective-permute-start.19 = (bf16[8,3200]{1,0:T(8,128)(2,1)S(1)}, bf16[8,3200]{1,0:T(8,128)(2,1)S(1)}, u32[]{:S(2)}, u32[]{:S(2)}) collective-permute-start(bf16[8,3200]{1,0:T(8,128)(2,1)S(1)} %get-tuple-element.47), channel_id=1, source_target_pairs={{0,8},{1,9},{2,10},{3,11},{4,12},{5,13},{6,14},{7,15},{8,0},{9,1},... | collective-permute-start | bytes 153608 | tf_op jit(solution)/shard_map/ppermute | solution.py:30
  40.8 3.3 %shard_map.110 = (bf16[12288,128]{1,0:T(8,128)(2,1)}, f32[8,128]{1,0:T(8,128)S(1)}) custom-call(bf16[128,3072]{1,0:T(8,128)(2,1)S(1)} %get-tuple-element.35.t, bf16[128,512]{1,0:T(8,128)(2,1)S(1)} %get-tuple-element.36.p, f32[8,3200]{1,0:T(8,128)S(1)} %get-tuple-element.46.refs_0_.own_ref, ...), custom_call_target="tpu_custom_call", output_to_operand_aliasing={{0}: (3, {})} | custom-call | flops 268435456 | bytes 4194304 | tf_op jit(solution)/shard_map/pallas_call | solution.py:287
  44.1 0.0 collective-permute-done.19.got_ref
  44.1 0.7 %shard_map.111 = (bf16[8,3072]{1,0:T(8,128)(2,1)}, f32[2,8]{1,0:T(2,128)}) custom-call(f32[8,3200]{1,0:T(8,128)S(1)} %get-tuple-element.46.refs_0_.own_ref, bf16[8,3200]{1,0:T(8,128)(2,1)S(1)} %collective-permute-done.19.got_ref, s32[2,8]{1,0:T(2,128)S(1)} %bitcast.14, f32[8,128]{1,0:T(8,128)S(1)} %get-tuple-element.49.after_ref), custom_call_target="tpu_custom_call" | custom-call | tf_op jit(solution)/shard_map/pallas_call | solution.py:420
  (10 shorter events, 0.0 us)
Async XLA Ops:
  2.2 9.2 %collective-permute-start = (bf16[8,6272]{1,0:T(8,128)(2,1)}, bf16[8,6272]{1,0:T(8,128)(2,1)S(1)}, u32[]{:S(2)}, u32[]{:S(2)}) collective-permute-start(bf16[8,6272]{1,0:T(8,128)(2,1)} %shard_map.102.refs_0_), channel_id=1, source_target_pairs={{0,8},{1,9},{2,10},{3,11},{4,12},{5,13},{6,14},{7,15},{8,0},{9,1},... | collective-permute-start | bytes 301064 | tf_op jit(solution)/shard_map/ppermute | solution.py:30
  6.2 9.6 %collective-permute-start.3 = (bf16[8,6272]{1,0:T(8,128)(2,1)}, bf16[8,6272]{1,0:T(8,128)(2,1)S(1)}, u32[]{:S(2)}, u32[]{:S(2)}) collective-permute-start(bf16[8,6272]{1,0:T(8,128)(2,1)} %shard_map.102.refs_0_), channel_id=1, source_target_pairs={{0,2},{1,5},{2,0},{3,7},{4,6},{5,1},{6,4},{7,3},{8,10},{9,13},{10,... | collective-permute-start | bytes 301064 | tf_op jit(solution)/shard_map/ppermute | solution.py:30
  7.7 8.1 %collective-permute-start.1 = (bf16[8,6272]{1,0:T(8,128)(2,1)}, bf16[8,6272]{1,0:T(8,128)(2,1)S(1)}, u32[]{:S(2)}, u32[]{:S(2)}) collective-permute-start(bf16[8,6272]{1,0:T(8,128)(2,1)} %shard_map.102.refs_0_), channel_id=1, source_target_pairs={{0,4},{1,3},{2,6},{3,1},{4,0},{5,7},{6,2},{7,5},{8,12},{9,11},{10,... | collective-permute-start | bytes 301064 | tf_op jit(solution)/shard_map/ppermute | solution.py:30
  9.3 3.0 %copy-start.1 = (bf16[8,6272]{1,0:T(8,128)(2,1)S(1)}, bf16[8,6272]{1,0:T(8,128)(2,1)}, u32[]{:S(2)}) copy-start(bf16[8,6272]{1,0:T(8,128)(2,1)} %shard_map.102.refs_0_) | copy-start | bytes 301060
  11.4 11.9 %copy-start = (bf16[256,3072]{1,0:T(8,128)(2,1)S(1)}, bf16[256,3072]{1,0:T(8,128)(2,1)}, u32[]{:S(2)}) copy-start(bf16[256,3072]{1,0:T(8,128)(2,1)} %refs_18_.1) | copy-start | bytes 4718596
  11.4 11.9 %copy-start.3 = (s32[16]{0:T(128)S(1)}, s32[16]{0:T(128)}, u32[]{:S(2)}) copy-start(s32[16]{0:T(128)} %owner_ref.1) | copy-start | bytes 196
  11.4 5.9 %collective-permute-start.2 = (bf16[8,6272]{1,0:T(8,128)(2,1)S(1)}, bf16[8,6272]{1,0:T(8,128)(2,1)S(1)}, u32[]{:S(2)}, u32[]{:S(2)}) collective-permute-start(bf16[8,6272]{1,0:T(8,128)(2,1)S(1)} %collective-permute-done.refs_1_), channel_id=1, source_target_pairs={{0,4},{1,3},{2,6},{3,1},{4,0},{5,7},{6,2},{7,5},{8,12},{9,11},{10,... | collective-permute-start | bytes 301064 | tf_op jit(solution)/shard_map/ppermute | solution.py:30
  12.3 5.0 %collective-permute-start.7 = (bf16[8,6272]{1,0:T(8,128)(2,1)S(1)}, bf16[8,6272]{1,0:T(8,128)(2,1)S(1)}, u32[]{:S(2)}, u32[]{:S(2)}) collective-permute-start(bf16[8,6272]{1,0:T(8,128)(2,1)S(1)} %copy-done.1), channel_id=1, source_target_pairs={{0,1},{1,0},{2,3},{3,2},{4,5},{5,4},{6,7},{7,6},{8,9},{9,8},{10,11... | collective-permute-start | bytes 301064 | tf_op jit(solution)/shard_map/ppermute | solution.py:30
  14.3 7.0 %collective-permute-start.4 = (bf16[8,6272]{1,0:T(8,128)(2,1)S(1)}, bf16[8,6272]{1,0:T(8,128)(2,1)S(1)}, u32[]{:S(2)}, u32[]{:S(2)}) collective-permute-start(bf16[8,6272]{1,0:T(8,128)(2,1)S(1)} %collective-permute-done.refs_1_), channel_id=1, source_target_pairs={{0,2},{1,5},{2,0},{3,7},{4,6},{5,1},{6,4},{7,3},{8,10},{9,13},{10,... | collective-permute-start | bytes 301064 | tf_op jit(solution)/shard_map/ppermute | solution.py:30
  15.8 2.3 %collective-permute-start.11 = (bf16[8,6272]{1,0:T(8,128)(2,1)S(1)}, bf16[8,6272]{1,0:T(8,128)(2,1)S(1)}, u32[]{:S(2)}, u32[]{:S(2)}) collective-permute-start(bf16[8,6272]{1,0:T(8,128)(2,1)S(1)} %collective-permute-done.3.refs_4_), channel_id=1, source_target_pairs={{0,1},{1,0},{2,3},{3,2},{4,5},{5,4},{6,7},{7,6},{8,9},{9,8},{10,11... | collective-permute-start | bytes 301064 | tf_op jit(solution)/shard_map/ppermute | solution.py:30
  15.8 4.9 %collective-permute-start.5 = (bf16[8,6272]{1,0:T(8,128)(2,1)S(1)}, bf16[8,6272]{1,0:T(8,128)(2,1)S(1)}, u32[]{:S(2)}, u32[]{:S(2)}) collective-permute-start(bf16[8,6272]{1,0:T(8,128)(2,1)S(1)} %collective-permute-done.3.refs_4_), channel_id=1, source_target_pairs={{0,4},{1,3},{2,6},{3,1},{4,0},{5,7},{6,2},{7,5},{8,12},{9,11},{10,... | collective-permute-start | bytes 301064 | tf_op jit(solution)/shard_map/ppermute | solution.py:30
  17.3 3.5 %collective-permute-start.9 = (bf16[8,6272]{1,0:T(8,128)(2,1)S(1)}, bf16[8,6272]{1,0:T(8,128)(2,1)S(1)}, u32[]{:S(2)}, u32[]{:S(2)}) collective-permute-start(bf16[8,6272]{1,0:T(8,128)(2,1)S(1)} %collective-permute-done.1.refs_2_), channel_id=1, source_target_pairs={{0,1},{1,0},{2,3},{3,2},{4,5},{5,4},{6,7},{7,6},{8,9},{9,8},{10,11... | collective-permute-start | bytes 301064 | tf_op jit(solution)/shard_map/ppermute | solution.py:30
  17.3 4.7 %collective-permute-start.6 = (bf16[8,6272]{1,0:T(8,128)(2,1)S(1)}, bf16[8,6272]{1,0:T(8,128)(2,1)S(1)}, u32[]{:S(2)}, u32[]{:S(2)}) collective-permute-start(bf16[8,6272]{1,0:T(8,128)(2,1)S(1)} %collective-permute-done.2.refs_3_), channel_id=1, source_target_pairs={{0,2},{1,5},{2,0},{3,7},{4,6},{5,1},{6,4},{7,3},{8,10},{9,13},{10,... | collective-permute-start | bytes 301064 | tf_op jit(solution)/shard_map/ppermute | solution.py:30
  18.2 3.8 %collective-permute-start.8 = (bf16[8,6272]{1,0:T(8,128)(2,1)S(1)}, bf16[8,6272]{1,0:T(8,128)(2,1)S(1)}, u32[]{:S(2)}, u32[]{:S(2)}) collective-permute-start(bf16[8,6272]{1,0:T(8,128)(2,1)S(1)} %collective-permute-done.refs_1_), channel_id=1, source_target_pairs={{0,1},{1,0},{2,3},{3,2},{4,5},{5,4},{6,7},{7,6},{8,9},{9,8},{10,11... | collective-permute-start | bytes 301064 | tf_op jit(solution)/shard_map/ppermute | solution.py:30
  20.7 1.8 %collective-permute-start.10 = (bf16[8,6272]{1,0:T(8,128)(2,1)S(1)}, bf16[8,6272]{1,0:T(8,128)(2,1)S(1)}, u32[]{:S(2)}, u32[]{:S(2)}) collective-permute-start(bf16[8,6272]{1,0:T(8,128)(2,1)S(1)} %collective-permute-done.2.refs_3_), channel_id=1, source_target_pairs={{0,1},{1,0},{2,3},{3,2},{4,5},{5,4},{6,7},{7,6},{8,9},{9,8},{10,11... | collective-permute-start | bytes 301064 | tf_op jit(solution)/shard_map/ppermute | solution.py:30
  20.8 1.5 %collective-permute-start.13 = (bf16[8,6272]{1,0:T(8,128)(2,1)S(1)}, bf16[8,6272]{1,0:T(8,128)(2,1)S(1)}, u32[]{:S(2)}, u32[]{:S(2)}) collective-permute-start(bf16[8,6272]{1,0:T(8,128)(2,1)S(1)} %collective-permute-done.5.refs_6_), channel_id=1, source_target_pairs={{0,1},{1,0},{2,3},{3,2},{4,5},{5,4},{6,7},{7,6},{8,9},{9,8},{10,11... | collective-permute-start | bytes 301064 | tf_op jit(solution)/shard_map/ppermute | solution.py:30
  21.3 1.3 %collective-permute-start.12 = (bf16[8,6272]{1,0:T(8,128)(2,1)S(1)}, bf16[8,6272]{1,0:T(8,128)(2,1)S(1)}, u32[]{:S(2)}, u32[]{:S(2)}) collective-permute-start(bf16[8,6272]{1,0:T(8,128)(2,1)S(1)} %collective-permute-done.4.refs_5_), channel_id=1, source_target_pairs={{0,1},{1,0},{2,3},{3,2},{4,5},{5,4},{6,7},{7,6},{8,9},{9,8},{10,11... | collective-permute-start | bytes 301064 | tf_op jit(solution)/shard_map/ppermute | solution.py:30
  22.0 1.3 %collective-permute-start.14 = (bf16[8,6272]{1,0:T(8,128)(2,1)S(1)}, bf16[8,6272]{1,0:T(8,128)(2,1)S(1)}, u32[]{:S(2)}, u32[]{:S(2)}) collective-permute-start(bf16[8,6272]{1,0:T(8,128)(2,1)S(1)} %collective-permute-done.6.refs_7_), channel_id=1, source_target_pairs={{0,1},{1,0},{2,3},{3,2},{4,5},{5,4},{6,7},{7,6},{8,9},{9,8},{10,11... | collective-permute-start | bytes 301064 | tf_op jit(solution)/shard_map/ppermute | solution.py:30
  26.7 2.1 %collective-permute-start.15 = (bf16[64,3200]{1,0:T(8,128)(2,1)S(1)}, bf16[64,3200]{1,0:T(8,128)(2,1)S(1)}, u32[]{:S(2)}, u32[]{:S(2)}) collective-permute-start(bf16[64,3200]{1,0:T(8,128)(2,1)S(1)} %get-tuple-element.34), channel_id=1, source_target_pairs={{0,1},{1,0},{2,3},{3,2},{4,5},{5,4},{6,7},{7,6},{8,9},{9,8},{10,11... | collective-permute-start | bytes 1228808 | tf_op jit(solution)/shard_map/ppermute | solution.py:30
  29.0 6.7 %collective-permute-start.16 = (bf16[16,3200]{1,0:T(8,128)(2,1)S(1)}, bf16[16,3200]{1,0:T(8,128)(2,1)S(1)}, u32[]{:S(2)}, u32[]{:S(2)}) collective-permute-start(bf16[16,3200]{1,0:T(8,128)(2,1)S(1)} %get-tuple-element.40), channel_id=1, source_target_pairs={{0,6},{1,7},{2,4},{3,5},{4,2},{5,3},{6,0},{7,1},{8,14},{9,15},{10,... | collective-permute-start | bytes 307208 | tf_op jit(solution)/shard_map/ppermute | solution.py:30
  30.7 6.6 %collective-permute-start.17 = (bf16[16,3200]{1,0:T(8,128)(2,1)S(1)}, bf16[16,3200]{1,0:T(8,128)(2,1)S(1)}, u32[]{:S(2)}, u32[]{:S(2)}) collective-permute-start(bf16[16,3200]{1,0:T(8,128)(2,1)S(1)} %get-tuple-element.41), channel_id=1, source_target_pairs={{0,2},{1,5},{2,0},{3,7},{4,6},{5,1},{6,4},{7,3},{8,10},{9,13},{10,... | collective-permute-start | bytes 307208 | tf_op jit(solution)/shard_map/ppermute | solution.py:30
  32.2 5.3 %collective-permute-start.18 = (bf16[16,3200]{1,0:T(8,128)(2,1)S(1)}, bf16[16,3200]{1,0:T(8,128)(2,1)S(1)}, u32[]{:S(2)}, u32[]{:S(2)}) collective-permute-start(bf16[16,3200]{1,0:T(8,128)(2,1)S(1)} %get-tuple-element.42), channel_id=1, source_target_pairs={{0,4},{1,3},{2,6},{3,1},{4,0},{5,7},{6,2},{7,5},{8,12},{9,11},{10,... | collective-permute-start | bytes 307208 | tf_op jit(solution)/shard_map/ppermute | solution.py:30
  37.6 6.5 %collective-permute-start.19 = (bf16[8,3200]{1,0:T(8,128)(2,1)S(1)}, bf16[8,3200]{1,0:T(8,128)(2,1)S(1)}, u32[]{:S(2)}, u32[]{:S(2)}) collective-permute-start(bf16[8,3200]{1,0:T(8,128)(2,1)S(1)} %get-tuple-element.47), channel_id=1, source_target_pairs={{0,8},{1,9},{2,10},{3,11},{4,12},{5,13},{6,14},{7,15},{8,0},{9,1},... | collective-permute-start | bytes 153608 | tf_op jit(solution)/shard_map/ppermute | solution.py:30
  40.8 3.3 %copy-start.2 = (s32[8,2]{0,1:T(2,128)S(1)}, s32[8,2]{0,1:T(2,128)}, u32[]{:S(2)}) copy-start(s32[8,2]{0,1:T(2,128)} %param.9) | copy-start | bytes 196

commit v4 on v3

--- a/solution.py
+++ b/solution.py
@@ -79,7 +79,7 @@
     return (col == (row % per) * group + row // per).astype(BF)
 
 
-def split_kernel(part, w_hbm, out_ref, w_ref, sems):
+def split_rows(part, w_hbm, out_ref, w_ref, sems):
     d, wide = out_ref.shape
     group = wide // LANES
     per = SIDE // group
@@ -113,17 +113,35 @@
                 ]
 
 
+def split_kernel(part, when, w_hbm, *refs):
+    done_ref, (out_ref, w_ref, sems) = refs[:-3], refs[-3:]
+    if when is None:
+        split_rows(part, w_hbm, out_ref, w_ref, sems)
+        return
+    mine = lax.axis_index("dev") % 2 == when
+
+    @pl.when(mine)
+    def _():
+        split_rows(part, w_hbm, out_ref, w_ref, sems)
+
+    if done_ref:
+
+        @pl.when(jnp.logical_not(mine))
+        def _():
+            out_ref[...] = done_ref[0][...]
+
+
 def lane_rows(w_in):
     d, two, hid = w_in.shape
     tiles = hid // LANES
     return w_in.reshape(d, two, tiles, LANES).transpose(0, 2, 1, 3).reshape(-1, LANES)
 
 
-def split_weights(view, part, d, wide):
+def split_weights(view, part, d, wide, when=None, *done):
     rows = view.shape[0] // 2
     return pl.pallas_call(
-        functools.partial(split_kernel, part),
-        in_specs=[ANY],
+        functools.partial(split_kernel, part, when),
+        in_specs=[ANY] + [VMEM] * len(done),
         out_specs=VMEM,
         out_shape=jax.ShapeDtypeStruct((d // 2, wide), BF),
         scratch_shapes=[pltpu.VMEM((rows, LANES), BF), pltpu.SemaphoreType.DMA((3,))],
@@ -131,7 +149,7 @@
         cost_estimate=pl.CostEstimate(
             flops=2 * rows * SIDE * LANES, bytes_accessed=4 * rows * LANES, transcendentals=0
         ),
-    )(view)
+    )(view, *done)
 
 
 def put_gate(out_ref, value, expert, width):
@@ -376,11 +394,13 @@
             held[o] = xor_swap(piece(o ^ bit), bit)
         return held[o]
 
-    weights = []
-    for part, o in enumerate((far, far + near)):
-        half_split = split_weights(view, part, width, 2 * hid)
-        held[o], half_split = lax.optimization_barrier((piece(o), half_split))
-        weights.append(half_split)
+    early = split_weights(view, 0, width, 2 * hid, 1)
+    held[0], early = lax.optimization_barrier((own, early))
+    low = split_weights(view, 0, width, 2 * hid, 0, early)
+    high = split_weights(view, 1, width, 2 * hid)
+    held[far], low = lax.optimization_barrier((piece(far), low))
+    held[far + 2], high = lax.optimization_barrier((piece(far + 2), high))
+    weights = [low, high]
     for o in order:
         piece(o)
 
@@ -403,17 +423,17 @@
     )(device_expert, *[held[o] for o in order], *weights, w_down)
 
     steps = width // 512
-    first = 2
     got = [xor_swap(send, 1)]
-    grad_w_in, after = grad_in(tok, pre, prob, 0, first)
+    grad_w_in, after = grad_in(tok, pre, prob, 0, 1)
     mine, (by_near, by_side, by_both) = add_step(mine, got, after, 4)
     got = [xor_swap(by_both, 6), xor_swap(by_side, 2), xor_swap(by_near, 4)]
-    grad_w_down, after = grad_down(hidden, grads, prob, mine)
+    grad_w_in, after = grad_in(tok, pre, mine, 1, 2, grad_w_in)
+    grad_w_down, after = grad_down(hidden, grads, prob, after)
     for bit in bits[-4::-1]:
         mine, (send,) = add_step(mine, got, after, 2)
         got = [xor_swap(send, bit)]
         if bit == 8:
-            grad_w_in, after = grad_in(tok, pre, mine, first, steps - first, grad_w_in)
+            grad_w_in, after = grad_in(tok, pre, mine, 3, steps - 3, grad_w_in)
     tiles = hid // LANES
     grad_w_in = grad_w_in.reshape(width, tiles, 2, LANES).transpose(0, 2, 1, 3)
     grad_w_in = grad_w_in.reshape(width, 2, hid)

time: 45 us -> 44.3 us (0.984)
  waiting for transfers between devices: 6.88 us -> 3.7 us
  starting transfers between devices: 19.5 us -> 21.1 us
  Pallas kernels: 17.7 us -> 18.5 us
    ppermute x20, waiting for transfers between devices: 6.88 us -> 3.7 us  [xor_swap(): lax.ppermute(value, 'dev', [(i, i ^ (other if i & 1 else bit)) for i in r...]
    ppermute x20, starting transfers between devices: 19.5 us -> 21.1 us  [xor_swap(): lax.ppermute(value, 'dev', [(i, i ^ (other if i & 1 else bit)) for i in r...]
    pallas_call x2 -> x3, Pallas kernels: 5.22 us -> 5.99 us  [grad_in(): pl.pallas_call(kernel, grid=(count,), in_specs=[pl.BlockSpec((rows, block...]
    pallas_call x2 -> x3, Pallas kernels: 4 us -> 4.01 us  [split_weights(): pl.pallas_call(functools.partial(split_kernel, part, when), in_specs=[ANY...]
  transfers between devices with their start and end apart: 20 -> 20, of which waited for: 8 -> 9; matrix products, arithmetic and copies ran while one was open for 0% -> 0% of each run, Pallas kernels for 26% -> 28%
where the time goes in v4:
time: 44.3 us; the launch traced here: 44.1 us
  starting transfers between devices  21.1 us (48%)
  Pallas kernels  18.5 us (42%)
  waiting for transfers between devices  3.7 us (8%)
  between operations  0.72 us (2%)
    ppermute x20, starting transfers between devices, xor_swap(): lax.ppermute(value, 'dev', [(i, i ^ (other if i & 1 else bit)) for i in r...  21.1 us
    pallas_call x3, Pallas kernels, grad_in(): pl.pallas_call(kernel, grid=(count,), in_specs=[pl.BlockSpec((rows, block...  5.99 us
    pallas_call x3, Pallas kernels, split_weights(): pl.pallas_call(functools.partial(split_kernel, part, when), in_specs=[ANY...  4.01 us
    ppermute x20, waiting for transfers between devices, xor_swap(): lax.ppermute(value, 'dev', [(i, i ^ (other if i & 1 else bit)) for i in r...  3.7 us
    pallas_call x1, Pallas kernels, shards(): pl.pallas_call(functools.partial(main_kernel, n), in_specs=[SMEM] + [VMEM...  3.39 us
    pallas_call x1, Pallas kernels, grad_down(): pl.pallas_call(down_kernel, grid=(d // block,), in_specs=[pl.BlockSpec((r...  2.53 us
    pallas_call x1, Pallas kernels, shards(): pl.pallas_call(pack_kernel, in_specs=[VMEM] * 4, out_specs=VMEM, out_shap...  1.56 us
  transfers between devices with their start and end apart: 20, of which 9 were waited for; matrix products, arithmetic and copies ran while one was open for 0% of the time, Pallas kernels for 28%

profile of v4, /device:TPU:0, one launch (start us, length us, event | category | flops | bytes accessed | tf_op | source)
XLA Modules:
  0.0 44.1 jit_solution(16285658608143375798)
XLA Ops:
  0.7 1.6 %shard_map.102.refs_0_ = bf16[8,6272]{1,0:T(8,128)(2,1)} custom-call(bf16[8,3072]{1,0:T(8,128)(2,1)} %tok_ref.1, bf16[8,3072]{1,0:T(8,128)(2,1)} %grad_ref.1, s32[2,8]{1,0:T(2,128)} %bitcast.13, f32[2,8]{1,0:T(2,128)} %bitcast.19), custom_call_target="tpu_custom_call" | custom-call | tf_op jit(solution)/shard_map/pallas_call | solution.py:375
  2.2 4.0 %collective-permute-start = (bf16[8,6272]{1,0:T(8,128)(2,1)}, bf16[8,6272]{1,0:T(8,128)(2,1)S(1)}, u32[]{:S(2)}, u32[]{:S(2)}) collective-permute-start(bf16[8,6272]{1,0:T(8,128)(2,1)} %shard_map.102.refs_0_), channel_id=1, source_target_pairs={{0,8},{1,9},{2,10},{3,11},{4,12},{5,13},{6,14},{7,15},{8,0},{9,1},... | collective-permute-start | bytes 301064 | tf_op jit(solution)/shard_map/ppermute | solution.py:30
  6.3 1.5 %collective-permute-start.3 = (bf16[8,6272]{1,0:T(8,128)(2,1)}, bf16[8,6272]{1,0:T(8,128)(2,1)S(1)}, u32[]{:S(2)}, u32[]{:S(2)}) collective-permute-start(bf16[8,6272]{1,0:T(8,128)(2,1)} %shard_map.102.refs_0_), channel_id=1, source_target_pairs={{0,2},{1,5},{2,0},{3,7},{4,6},{5,1},{6,4},{7,3},{8,10},{9,13},{10,... | collective-permute-start | bytes 301064 | tf_op jit(solution)/shard_map/ppermute | solution.py:30
  7.8 1.6 %collective-permute-start.1 = (bf16[8,6272]{1,0:T(8,128)(2,1)}, bf16[8,6272]{1,0:T(8,128)(2,1)S(1)}, u32[]{:S(2)}, u32[]{:S(2)}) collective-permute-start(bf16[8,6272]{1,0:T(8,128)(2,1)} %shard_map.102.refs_0_), channel_id=1, source_target_pairs={{0,4},{1,3},{2,6},{3,1},{4,0},{5,7},{6,2},{7,5},{8,12},{9,11},{10,... | collective-permute-start | bytes 301064 | tf_op jit(solution)/shard_map/ppermute | solution.py:30
  9.4 2.0 %shard_map.104.refs_16_ = bf16[1536,512]{1,0:T(8,128)(2,1)S(1)} custom-call(bf16[12288,128]{1,0:T(8,128)(2,1)} %bitcast.16, bf16[1536,512]{1,0:T(8,128)(2,1)S(1)} %shard_map.103.refs_0_), custom_call_target="tpu_custom_call" | custom-call | flops 402653184 | bytes 3145728 | tf_op jit(solution)/shard_map/pallas_call | solution.py:142
  11.4 0.0 copy-start
  11.4 0.0 copy-start.3
  11.4 0.0 collective-permute-done.refs_1_
  11.4 1.4 %collective-permute-start.4 = (bf16[8,6272]{1,0:T(8,128)(2,1)S(1)}, bf16[8,6272]{1,0:T(8,128)(2,1)S(1)}, u32[]{:S(2)}, u32[]{:S(2)}) collective-permute-start(bf16[8,6272]{1,0:T(8,128)(2,1)S(1)} %collective-permute-done.refs_1_), channel_id=1, source_target_pairs={{0,2},{1,5},{2,0},{3,7},{4,6},{5,1},{6,4},{7,3},{8,10},{9,13},{10,... | collective-permute-start | bytes 301064 | tf_op jit(solution)/shard_map/ppermute | solution.py:30
  12.8 2.0 %collective-permute-start.2 = (bf16[8,6272]{1,0:T(8,128)(2,1)S(1)}, bf16[8,6272]{1,0:T(8,128)(2,1)S(1)}, u32[]{:S(2)}, u32[]{:S(2)}) collective-permute-start(bf16[8,6272]{1,0:T(8,128)(2,1)S(1)} %collective-permute-done.refs_1_), channel_id=1, source_target_pairs={{0,4},{1,3},{2,6},{3,1},{4,0},{5,7},{6,2},{7,5},{8,12},{9,11},{10,... | collective-permute-start | bytes 301064 | tf_op jit(solution)/shard_map/ppermute | solution.py:30
  14.9 0.0 collective-permute-start.7
  14.9 0.0 collective-permute-done.3.refs_4_
  14.9 0.5 %collective-permute-start.11 = (bf16[8,6272]{1,0:T(8,128)(2,1)S(1)}, bf16[8,6272]{1,0:T(8,128)(2,1)S(1)}, u32[]{:S(2)}, u32[]{:S(2)}) collective-permute-start(bf16[8,6272]{1,0:T(8,128)(2,1)S(1)} %collective-permute-done.3.refs_4_), channel_id=1, source_target_pairs={{0,1},{1,0},{2,3},{3,2},{4,5},{5,4},{6,7},{7,6},{8,9},{9,8},{10,11... | collective-permute-start | bytes 301064 | tf_op jit(solution)/shard_map/ppermute | solution.py:30
  15.4 0.0 collective-permute-done.1.refs_2_
  15.4 0.3 collective-permute-start.5
  15.7 0.6 %collective-permute-done.4.refs_5_ = bf16[8,6272]{1,0:T(8,128)(2,1)S(1)} collective-permute-done((bf16[8,6272]{1,0:T(8,128)(2,1)S(1)}, bf16[8,6272]{1,0:T(8,128)(2,1)S(1)}, u32[]{:S(2)}, u32[]{:S(2)}) %collective-permute-start.4) | collective-permute-done | bytes 100384 | tf_op jit(solution)/shard_map/ppermute | solution.py:30
  16.3 0.0 collective-permute-start.9
  16.3 1.2 %collective-permute-done.2.refs_3_ = bf16[8,6272]{1,0:T(8,128)(2,1)S(1)} collective-permute-done((bf16[8,6272]{1,0:T(8,128)(2,1)S(1)}, bf16[8,6272]{1,0:T(8,128)(2,1)S(1)}, u32[]{:S(2)}, u32[]{:S(2)}) %collective-permute-start.2) | collective-permute-done | bytes 100384 | tf_op jit(solution)/shard_map/ppermute | solution.py:30
  17.5 1.4 %collective-permute-start.6 = (bf16[8,6272]{1,0:T(8,128)(2,1)S(1)}, bf16[8,6272]{1,0:T(8,128)(2,1)S(1)}, u32[]{:S(2)}, u32[]{:S(2)}) collective-permute-start(bf16[8,6272]{1,0:T(8,128)(2,1)S(1)} %collective-permute-done.2.refs_3_), channel_id=1, source_target_pairs={{0,2},{1,5},{2,0},{3,7},{4,6},{5,1},{6,4},{7,3},{8,10},{9,13},{10,... | collective-permute-start | bytes 301064 | tf_op jit(solution)/shard_map/ppermute | solution.py:30
  18.9 2.0 %shard_map.105.refs_17_ = bf16[1536,512]{1,0:T(8,128)(2,1)S(1)} custom-call(bf16[12288,128]{1,0:T(8,128)(2,1)} %bitcast.17), custom_call_target="tpu_custom_call" | custom-call | flops 402653184 | bytes 3145728 | tf_op jit(solution)/shard_map/pallas_call | solution.py:142
  20.9 0.0 collective-permute-done.7.refs_8_
  20.9 0.4 collective-permute-start.8
  21.3 0.2 collective-permute-start.12
  21.4 0.3 collective-permute-start.13
  21.8 0.0 collective-permute-done.9.refs_10_
  21.8 0.2 collective-permute-start.10
  22.0 0.2 collective-permute-done.6.refs_7_
  22.1 0.2 collective-permute-start.14
  22.3 0.0 collective-permute-done.8.refs_9_
  22.3 0.4 %collective-permute-done.13.refs_14_ = bf16[8,6272]{1,0:T(8,128)(2,1)S(1)} collective-permute-done((bf16[8,6272]{1,0:T(8,128)(2,1)S(1)}, bf16[8,6272]{1,0:T(8,128)(2,1)S(1)}, u32[]{:S(2)}, u32[]{:S(2)}) %collective-permute-start.13) | collective-permute-done | bytes 100384 | tf_op jit(solution)/shard_map/ppermute | solution.py:30
  22.8 0.3 collective-permute-done.10.refs_11_
  23.1 0.4 collective-permute-done.14.refs_15_
  23.5 3.4 %shard_map.106 = (bf16[128,3072]{1,0:T(8,128)(2,1)S(1)}, bf16[128,3072]{1,0:T(8,128)(2,1)S(1)}, bf16[128,512]{1,0:T(8,128)(2,1)S(1)}, bf16[128,256]{1,0:T(8,128)...) custom-call(s32[16]{0:T(128)S(1)} %copy-done.3, ...), custom_call_target="tpu_custom_call" | custom-call | tf_op jit(solution)/shard_map/pallas_call | solution.py:409
  26.9 0.2 collective-permute-start.15
  27.1 1.3 %shard_map.107 = (bf16[12288,128]{1,0:T(8,128)(2,1)}, f32[8,128]{1,0:T(8,128)S(1)}) custom-call(bf16[128,3072]{1,0:T(8,128)(2,1)S(1)} %get-tuple-element.41.t, bf16[128,512]{1,0:T(8,128)(2,1)S(1)} %get-tuple-element.42.p, f32[128,128]{1,0:T(8,128)S(1)} %get-tuple-element.43.refs_0_.prob_ref), custom_call_target="tpu_custom_call" | custom-call | flops 67108864 | bytes 1048576 | tf_op jit(solution)/shard_map/pallas_call | solution.py:305
  28.4 0.2 collective-permute-done.15.refs_0_
  28.7 0.2 shard_map.108
  28.8 2.6 %collective-permute-start.16 = (bf16[16,3200]{1,0:T(8,128)(2,1)S(1)}, bf16[16,3200]{1,0:T(8,128)(2,1)S(1)}, u32[]{:S(2)}, u32[]{:S(2)}) collective-permute-start(bf16[16,3200]{1,0:T(8,128)(2,1)S(1)} %get-tuple-element.46), channel_id=1, source_target_pairs={{0,6},{1,7},{2,4},{3,5},{4,2},{5,3},{6,0},{7,1},{8,14},{9,15},{10,... | collective-permute-start | bytes 307208 | tf_op jit(solution)/shard_map/ppermute | solution.py:30
  31.4 1.0 %collective-permute-start.17 = (bf16[16,3200]{1,0:T(8,128)(2,1)S(1)}, bf16[16,3200]{1,0:T(8,128)(2,1)S(1)}, u32[]{:S(2)}, u32[]{:S(2)}) collective-permute-start(bf16[16,3200]{1,0:T(8,128)(2,1)S(1)} %get-tuple-element.47), channel_id=1, source_target_pairs={{0,2},{1,5},{2,0},{3,7},{4,6},{5,1},{6,4},{7,3},{8,10},{9,13},{10,... | collective-permute-start | bytes 307208 | tf_op jit(solution)/shard_map/ppermute | solution.py:30
  32.4 1.9 %shard_map.109 = (bf16[12288,128]{1,0:T(8,128)(2,1)}, f32[8,128]{1,0:T(8,128)S(1)}) custom-call(bf16[128,3072]{1,0:T(8,128)(2,1)S(1)} %get-tuple-element.41.t, bf16[128,512]{1,0:T(8,128)(2,1)S(1)} %get-tuple-element.42.p, f32[16,3200]{1,0:T(8,128)S(1)} %get-tuple-element.45.refs_0_.own_ref, ...), custom_call_target="tpu_custom_call", output_to_operand_aliasing={{0}: (3, {})} | custom-call | flops 134217728 | bytes 2097152 | tf_op jit(solution)/shard_map/pallas_call | solution.py:305
  34.3 2.5 %shard_map.110 = (bf16[256,3072]{1,0:T(8,128)(2,1)}, f32[8,128]{1,0:T(8,128)S(1)}) custom-call(bf16[128,256]{1,0:T(8,128)(2,1)S(1)} %get-tuple-element.49.hid_ref, bf16[128,3072]{1,0:T(8,128)(2,1)S(1)} %get-tuple-element.50.grad_ref, f32[128,128]{1,0:T(8,128)S(1)} %get-tuple-element.43.refs_0_.prob_ref, f32[8,128]{1,0:T(8,128)S(1)} %get-tuple-element.52.after_ref), custom_call_target="tpu_custom_call" | custom-call | flops 201326592 | bytes 3145728 | tf_op jit(solution)/shard_map/pallas_call | solution.py:343
  36.8 0.1 collective-permute-done.17.refs_1_
  36.9 0.2 collective-permute-done.18.refs_2_
  37.1 0.1 shard_map.111
  37.2 3.4 %collective-permute-start.19 = (bf16[8,3200]{1,0:T(8,128)(2,1)S(1)}, bf16[8,3200]{1,0:T(8,128)(2,1)S(1)}, u32[]{:S(2)}, u32[]{:S(2)}) collective-permute-start(bf16[8,3200]{1,0:T(8,128)(2,1)S(1)} %get-tuple-element.55), channel_id=1, source_target_pairs={{0,8},{1,9},{2,10},{3,11},{4,12},{5,13},{6,14},{7,15},{8,0},{9,1},... | collective-permute-start | bytes 153608 | tf_op jit(solution)/shard_map/ppermute | solution.py:30
  40.6 2.7 %shard_map.112 = (bf16[12288,128]{1,0:T(8,128)(2,1)}, f32[8,128]{1,0:T(8,128)S(1)}) custom-call(bf16[128,3072]{1,0:T(8,128)(2,1)S(1)} %get-tuple-element.41.t, bf16[128,512]{1,0:T(8,128)(2,1)S(1)} %get-tuple-element.42.p, f32[8,3200]{1,0:T(8,128)S(1)} %get-tuple-element.54.refs_0_.own_ref, ...), custom_call_target="tpu_custom_call", output_to_operand_aliasing={{0}: (3, {})} | custom-call | flops 201326592 | bytes 3145728 | tf_op jit(solution)/shard_map/pallas_call | solution.py:305
  43.3 0.0 collective-permute-done.19.got_ref
  43.3 0.7 %shard_map.113 = (bf16[8,3072]{1,0:T(8,128)(2,1)}, f32[2,8]{1,0:T(2,128)}) custom-call(f32[8,3200]{1,0:T(8,128)S(1)} %get-tuple-element.54.refs_0_.own_ref, bf16[8,3200]{1,0:T(8,128)(2,1)S(1)} %collective-permute-done.19.got_ref, s32[2,8]{1,0:T(2,128)S(1)} %bitcast.14, f32[8,128]{1,0:T(8,128)S(1)} %get-tuple-element.57.after_ref), custom_call_target="tpu_custom_call" | custom-call | tf_op jit(solution)/shard_map/pallas_call | solution.py:440
  (12 shorter events, 0.1 us)
Async XLA Ops:
  2.2 12.6 %copy-start.1 = (bf16[8,6272]{1,0:T(8,128)(2,1)S(1)}, bf16[8,6272]{1,0:T(8,128)(2,1)}, u32[]{:S(2)}) copy-start(bf16[8,6272]{1,0:T(8,128)(2,1)} %shard_map.102.refs_0_) | copy-start | bytes 301060
  2.2 9.2 %collective-permute-start = (bf16[8,6272]{1,0:T(8,128)(2,1)}, bf16[8,6272]{1,0:T(8,128)(2,1)S(1)}, u32[]{:S(2)}, u32[]{:S(2)}) collective-permute-start(bf16[8,6272]{1,0:T(8,128)(2,1)} %shard_map.102.refs_0_), channel_id=1, source_target_pairs={{0,8},{1,9},{2,10},{3,11},{4,12},{5,13},{6,14},{7,15},{8,0},{9,1},... | collective-permute-start | bytes 301064 | tf_op jit(solution)/shard_map/ppermute | solution.py:30
  6.3 8.6 %collective-permute-start.3 = (bf16[8,6272]{1,0:T(8,128)(2,1)}, bf16[8,6272]{1,0:T(8,128)(2,1)S(1)}, u32[]{:S(2)}, u32[]{:S(2)}) collective-permute-start(bf16[8,6272]{1,0:T(8,128)(2,1)} %shard_map.102.refs_0_), channel_id=1, source_target_pairs={{0,2},{1,5},{2,0},{3,7},{4,6},{5,1},{6,4},{7,3},{8,10},{9,13},{10,... | collective-permute-start | bytes 301064 | tf_op jit(solution)/shard_map/ppermute | solution.py:30
  7.8 7.6 %collective-permute-start.1 = (bf16[8,6272]{1,0:T(8,128)(2,1)}, bf16[8,6272]{1,0:T(8,128)(2,1)S(1)}, u32[]{:S(2)}, u32[]{:S(2)}) collective-permute-start(bf16[8,6272]{1,0:T(8,128)(2,1)} %shard_map.102.refs_0_), channel_id=1, source_target_pairs={{0,4},{1,3},{2,6},{3,1},{4,0},{5,7},{6,2},{7,5},{8,12},{9,11},{10,... | collective-permute-start | bytes 301064 | tf_op jit(solution)/shard_map/ppermute | solution.py:30
  11.4 12.1 %copy-start = (bf16[256,3072]{1,0:T(8,128)(2,1)S(1)}, bf16[256,3072]{1,0:T(8,128)(2,1)}, u32[]{:S(2)}) copy-start(bf16[256,3072]{1,0:T(8,128)(2,1)} %refs_18_.1) | copy-start | bytes 4718596
  11.4 12.1 %copy-start.3 = (s32[16]{0:T(128)S(1)}, s32[16]{0:T(128)}, u32[]{:S(2)}) copy-start(s32[16]{0:T(128)} %owner_ref.1) | copy-start | bytes 196
  11.4 4.9 %collective-permute-start.4 = (bf16[8,6272]{1,0:T(8,128)(2,1)S(1)}, bf16[8,6272]{1,0:T(8,128)(2,1)S(1)}, u32[]{:S(2)}, u32[]{:S(2)}) collective-permute-start(bf16[8,6272]{1,0:T(8,128)(2,1)S(1)} %collective-permute-done.refs_1_), channel_id=1, source_target_pairs={{0,2},{1,5},{2,0},{3,7},{4,6},{5,1},{6,4},{7,3},{8,10},{9,13},{10,... | collective-permute-start | bytes 301064 | tf_op jit(solution)/shard_map/ppermute | solution.py:30
  12.8 4.7 %collective-permute-start.2 = (bf16[8,6272]{1,0:T(8,128)(2,1)S(1)}, bf16[8,6272]{1,0:T(8,128)(2,1)S(1)}, u32[]{:S(2)}, u32[]{:S(2)}) collective-permute-start(bf16[8,6272]{1,0:T(8,128)(2,1)S(1)} %collective-permute-done.refs_1_), channel_id=1, source_target_pairs={{0,4},{1,3},{2,6},{3,1},{4,0},{5,7},{6,2},{7,5},{8,12},{9,11},{10,... | collective-permute-start | bytes 301064 | tf_op jit(solution)/shard_map/ppermute | solution.py:30
  14.9 6.0 %collective-permute-start.7 = (bf16[8,6272]{1,0:T(8,128)(2,1)S(1)}, bf16[8,6272]{1,0:T(8,128)(2,1)S(1)}, u32[]{:S(2)}, u32[]{:S(2)}) collective-permute-start(bf16[8,6272]{1,0:T(8,128)(2,1)S(1)} %copy-done.1), channel_id=1, source_target_pairs={{0,1},{1,0},{2,3},{3,2},{4,5},{5,4},{6,7},{7,6},{8,9},{9,8},{10,11... | collective-permute-start | bytes 301064 | tf_op jit(solution)/shard_map/ppermute | solution.py:30
  14.9 6.4 %collective-permute-start.11 = (bf16[8,6272]{1,0:T(8,128)(2,1)S(1)}, bf16[8,6272]{1,0:T(8,128)(2,1)S(1)}, u32[]{:S(2)}, u32[]{:S(2)}) collective-permute-start(bf16[8,6272]{1,0:T(8,128)(2,1)S(1)} %collective-permute-done.3.refs_4_), channel_id=1, source_target_pairs={{0,1},{1,0},{2,3},{3,2},{4,5},{5,4},{6,7},{7,6},{8,9},{9,8},{10,11... | collective-permute-start | bytes 301064 | tf_op jit(solution)/shard_map/ppermute | solution.py:30
  15.4 6.0 %collective-permute-start.5 = (bf16[8,6272]{1,0:T(8,128)(2,1)S(1)}, bf16[8,6272]{1,0:T(8,128)(2,1)S(1)}, u32[]{:S(2)}, u32[]{:S(2)}) collective-permute-start(bf16[8,6272]{1,0:T(8,128)(2,1)S(1)} %collective-permute-done.3.refs_4_), channel_id=1, source_target_pairs={{0,4},{1,3},{2,6},{3,1},{4,0},{5,7},{6,2},{7,5},{8,12},{9,11},{10,... | collective-permute-start | bytes 301064 | tf_op jit(solution)/shard_map/ppermute | solution.py:30
  16.3 5.5 %collective-permute-start.9 = (bf16[8,6272]{1,0:T(8,128)(2,1)S(1)}, bf16[8,6272]{1,0:T(8,128)(2,1)S(1)}, u32[]{:S(2)}, u32[]{:S(2)}) collective-permute-start(bf16[8,6272]{1,0:T(8,128)(2,1)S(1)} %collective-permute-done.1.refs_2_), channel_id=1, source_target_pairs={{0,1},{1,0},{2,3},{3,2},{4,5},{5,4},{6,7},{7,6},{8,9},{9,8},{10,11... | collective-permute-start | bytes 301064 | tf_op jit(solution)/shard_map/ppermute | solution.py:30
  17.5 4.6 %collective-permute-start.6 = (bf16[8,6272]{1,0:T(8,128)(2,1)S(1)}, bf16[8,6272]{1,0:T(8,128)(2,1)S(1)}, u32[]{:S(2)}, u32[]{:S(2)}) collective-permute-start(bf16[8,6272]{1,0:T(8,128)(2,1)S(1)} %collective-permute-done.2.refs_3_), channel_id=1, source_target_pairs={{0,2},{1,5},{2,0},{3,7},{4,6},{5,1},{6,4},{7,3},{8,10},{9,13},{10,... | collective-permute-start | bytes 301064 | tf_op jit(solution)/shard_map/ppermute | solution.py:30
  20.9 1.4 %collective-permute-start.8 = (bf16[8,6272]{1,0:T(8,128)(2,1)S(1)}, bf16[8,6272]{1,0:T(8,128)(2,1)S(1)}, u32[]{:S(2)}, u32[]{:S(2)}) collective-permute-start(bf16[8,6272]{1,0:T(8,128)(2,1)S(1)} %collective-permute-done.refs_1_), channel_id=1, source_target_pairs={{0,1},{1,0},{2,3},{3,2},{4,5},{5,4},{6,7},{7,6},{8,9},{9,8},{10,11... | collective-permute-start | bytes 301064 | tf_op jit(solution)/shard_map/ppermute | solution.py:30
  21.3 1.5 %collective-permute-start.12 = (bf16[8,6272]{1,0:T(8,128)(2,1)S(1)}, bf16[8,6272]{1,0:T(8,128)(2,1)S(1)}, u32[]{:S(2)}, u32[]{:S(2)}) collective-permute-start(bf16[8,6272]{1,0:T(8,128)(2,1)S(1)} %collective-permute-done.4.refs_5_), channel_id=1, source_target_pairs={{0,1},{1,0},{2,3},{3,2},{4,5},{5,4},{6,7},{7,6},{8,9},{9,8},{10,11... | collective-permute-start | bytes 301064 | tf_op jit(solution)/shard_map/ppermute | solution.py:30
  21.4 1.3 %collective-permute-start.13 = (bf16[8,6272]{1,0:T(8,128)(2,1)S(1)}, bf16[8,6272]{1,0:T(8,128)(2,1)S(1)}, u32[]{:S(2)}, u32[]{:S(2)}) collective-permute-start(bf16[8,6272]{1,0:T(8,128)(2,1)S(1)} %collective-permute-done.5.refs_6_), channel_id=1, source_target_pairs={{0,1},{1,0},{2,3},{3,2},{4,5},{5,4},{6,7},{7,6},{8,9},{9,8},{10,11... | collective-permute-start | bytes 301064 | tf_op jit(solution)/shard_map/ppermute | solution.py:30
  21.8 1.3 %collective-permute-start.10 = (bf16[8,6272]{1,0:T(8,128)(2,1)S(1)}, bf16[8,6272]{1,0:T(8,128)(2,1)S(1)}, u32[]{:S(2)}, u32[]{:S(2)}) collective-permute-start(bf16[8,6272]{1,0:T(8,128)(2,1)S(1)} %collective-permute-done.2.refs_3_), channel_id=1, source_target_pairs={{0,1},{1,0},{2,3},{3,2},{4,5},{5,4},{6,7},{7,6},{8,9},{9,8},{10,11... | collective-permute-start | bytes 301064 | tf_op jit(solution)/shard_map/ppermute | solution.py:30
  22.1 1.3 %collective-permute-start.14 = (bf16[8,6272]{1,0:T(8,128)(2,1)S(1)}, bf16[8,6272]{1,0:T(8,128)(2,1)S(1)}, u32[]{:S(2)}, u32[]{:S(2)}) collective-permute-start(bf16[8,6272]{1,0:T(8,128)(2,1)S(1)} %collective-permute-done.6.refs_7_), channel_id=1, source_target_pairs={{0,1},{1,0},{2,3},{3,2},{4,5},{5,4},{6,7},{7,6},{8,9},{9,8},{10,11... | collective-permute-start | bytes 301064 | tf_op jit(solution)/shard_map/ppermute | solution.py:30
  26.9 1.8 %collective-permute-start.15 = (bf16[64,3200]{1,0:T(8,128)(2,1)S(1)}, bf16[64,3200]{1,0:T(8,128)(2,1)S(1)}, u32[]{:S(2)}, u32[]{:S(2)}) collective-permute-start(bf16[64,3200]{1,0:T(8,128)(2,1)S(1)} %get-tuple-element.40), channel_id=1, source_target_pairs={{0,1},{1,0},{2,3},{3,2},{4,5},{5,4},{6,7},{7,6},{8,9},{9,8},{10,11... | collective-permute-start | bytes 1228808 | tf_op jit(solution)/shard_map/ppermute | solution.py:30
  28.8 8.0 %collective-permute-start.16 = (bf16[16,3200]{1,0:T(8,128)(2,1)S(1)}, bf16[16,3200]{1,0:T(8,128)(2,1)S(1)}, u32[]{:S(2)}, u32[]{:S(2)}) collective-permute-start(bf16[16,3200]{1,0:T(8,128)(2,1)S(1)} %get-tuple-element.46), channel_id=1, source_target_pairs={{0,6},{1,7},{2,4},{3,5},{4,2},{5,3},{6,0},{7,1},{8,14},{9,15},{10,... | collective-permute-start | bytes 307208 | tf_op jit(solution)/shard_map/ppermute | solution.py:30
  31.4 5.5 %collective-permute-start.17 = (bf16[16,3200]{1,0:T(8,128)(2,1)S(1)}, bf16[16,3200]{1,0:T(8,128)(2,1)S(1)}, u32[]{:S(2)}, u32[]{:S(2)}) collective-permute-start(bf16[16,3200]{1,0:T(8,128)(2,1)S(1)} %get-tuple-element.47), channel_id=1, source_target_pairs={{0,2},{1,5},{2,0},{3,7},{4,6},{5,1},{6,4},{7,3},{8,10},{9,13},{10,... | collective-permute-start | bytes 307208 | tf_op jit(solution)/shard_map/ppermute | solution.py:30
  32.4 4.7 %collective-permute-start.18 = (bf16[16,3200]{1,0:T(8,128)(2,1)S(1)}, bf16[16,3200]{1,0:T(8,128)(2,1)S(1)}, u32[]{:S(2)}, u32[]{:S(2)}) collective-permute-start(bf16[16,3200]{1,0:T(8,128)(2,1)S(1)} %get-tuple-element.48), channel_id=1, source_target_pairs={{0,4},{1,3},{2,6},{3,1},{4,0},{5,7},{6,2},{7,5},{8,12},{9,11},{10,... | collective-permute-start | bytes 307208 | tf_op jit(solution)/shard_map/ppermute | solution.py:30
  37.2 6.1 %collective-permute-start.19 = (bf16[8,3200]{1,0:T(8,128)(2,1)S(1)}, bf16[8,3200]{1,0:T(8,128)(2,1)S(1)}, u32[]{:S(2)}, u32[]{:S(2)}) collective-permute-start(bf16[8,3200]{1,0:T(8,128)(2,1)S(1)} %get-tuple-element.55), channel_id=1, source_target_pairs={{0,8},{1,9},{2,10},{3,11},{4,12},{5,13},{6,14},{7,15},{8,0},{9,1},... | collective-permute-start | bytes 153608 | tf_op jit(solution)/shard_map/ppermute | solution.py:30
  40.6 2.7 %copy-start.2 = (s32[8,2]{0,1:T(2,128)S(1)}, s32[8,2]{0,1:T(2,128)}, u32[]{:S(2)}) copy-start(s32[8,2]{0,1:T(2,128)} %param.9) | copy-start | bytes 196

commit v5 on v4

--- a/solution.py
+++ b/solution.py
@@ -269,16 +269,17 @@
         gates_ref[k : k + 1, :] = jnp.sum(square, 0, keepdims=True)
 
 
-def win_kernel(tok_ref, pre_ref, out_ref, token_ref):
+def win_block(tok_ref, pre_ref, column, out_ref):
     wide = pre_ref.shape[1]
     group = wide // LANES
     per = SIDE // group
     tiles = group // 2
+    rows = out_ref.shape[0] // group
     put = shuffle(group, inverse=True)
     block = lax.dot_general(
-        tok_ref[...], pre_ref[...], TN, preferred_element_type=F32
+        tok_ref[:, column : column + rows], pre_ref[...], TN, preferred_element_type=F32
     ).astype(BF)
-    for s in range(0, tok_ref.shape[1] // per, 2):
+    for s in range(0, rows // per, 2):
         sides = []
         for half in range(2):
             here = (s + half) * per
@@ -291,33 +292,58 @@
                     0,
                 )
             )
-        rows = jnp.dot(put, jnp.concatenate(sides, 1), preferred_element_type=F32).astype(BF)
-        out_ref[s * SIDE : (s + 1) * SIDE, :] = rows[:, :LANES]
-        out_ref[(s + 1) * SIDE : (s + 2) * SIDE, :] = rows[:, LANES:]
+        both = jnp.dot(put, jnp.concatenate(sides, 1), preferred_element_type=F32).astype(BF)
+        out_ref[s * SIDE : (s + 1) * SIDE, :] = both[:, :LANES]
+        out_ref[(s + 1) * SIDE : (s + 2) * SIDE, :] = both[:, LANES:]
+
+
+def win_kernel(blocks, parity, tok_ref, pre_ref, *refs):
+    out_hbm, token_ref, near_ref, sems = refs[-4:]
+    size = near_ref.shape[1]
+    columns = size * LANES // pre_ref.shape[1]
     token_ref[...] = jnp.zeros_like(token_ref)
 
-
-def grad_in(tok, pre, after, first, count, out=None, block=512):
+    def run(blocks):
+        copies = []
+        for j, block in enumerate(blocks):
+            if j >= 2:
+                copies[j - 2].wait()
+            win_block(tok_ref, pre_ref, block * columns, near_ref.at[j % 2])
+            copies.append(
+                pltpu.make_async_copy(
+                    near_ref.at[j % 2],
+                    out_hbm.at[pl.ds(block * size, size), :],
+                    sems.at[j % 2],
+                )
+            )
+            copies[j].start()
+        for copy in copies[-2:]:
+            copy.wait()
+
+    if parity is None:
+        run(blocks)
+        return
+    odd = lax.axis_index("dev") % 2 == 1
+    pl.when(odd)(lambda: run(blocks[1]))
+    pl.when(jnp.logical_not(odd))(lambda: run(blocks[0]))
+
+
+def grad_in(tok, pre, after, blocks, out=None, parity=None, block=512):
     rows, d = tok.shape
     wide = pre.shape[1]
     group = wide // LANES
-    kernel = lambda t, p, *refs: win_kernel(t, p, refs[-2], refs[-1])
+    count = len(blocks) if parity is None else max(len(b) for b in blocks)
     return pl.pallas_call(
-        kernel,
-        grid=(count,),
-        in_specs=[
-            pl.BlockSpec((rows, block), lambda i: (0, i + first)),
-            pl.BlockSpec((rows, wide), lambda i: (0, 0)),
-            ANY,
-        ]
-        + ([] if out is None else [ANY]),
-        out_specs=[
-            pl.BlockSpec((block * group, LANES), lambda i: (i + first, 0)),
-            pl.BlockSpec((8, LANES), lambda i: (0, 0)),
-        ],
+        functools.partial(win_kernel, blocks, parity),
+        in_specs=[VMEM, VMEM, ANY] + ([] if out is None else [ANY]),
+        out_specs=[ANY, VMEM],
         out_shape=[
             jax.ShapeDtypeStruct((d * group, LANES), BF),
             jax.ShapeDtypeStruct((8, LANES), F32),
+        ],
+        scratch_shapes=[
+            pltpu.VMEM((2, block * group, LANES), BF),
+            pltpu.SemaphoreType.DMA((2,)),
         ],
         input_output_aliases={} if out is None else {3: 0},
         compiler_params=params(),
@@ -329,33 +355,41 @@
     )(tok, pre, after, *([] if out is None else [out]))
 
 
-def down_kernel(hid_ref, grad_ref, prob_ref, after_ref, out_ref, token_ref):
+def down_kernel(hid_ref, grad_ref, prob_ref, after_ref, out_hbm, token_ref, scaled_ref, near_ref, sems):
     token_ref[...] = jnp.zeros_like(token_ref)
-    scaled = (prob_ref[:, :1] * grad_ref[...].astype(F32)).astype(BF)
-    out_ref[...] = lax.dot_general(
-        hid_ref[...], scaled, TN, preferred_element_type=F32
-    ).astype(BF)
-
-
-def grad_down(hidden, grads, prob, after, block=768):
+    scaled_ref[...] = (prob_ref[:, :1] * grad_ref[...].astype(F32)).astype(BF)
+    count, rows, _ = near_ref.shape
+    copies = []
+    for j in range(count):
+        here = slice(j * rows, (j + 1) * rows)
+        near_ref[j] = lax.dot_general(
+            hid_ref[:, here], scaled_ref[...], TN, preferred_element_type=F32
+        ).astype(BF)
+        copies.append(
+            pltpu.make_async_copy(
+                near_ref.at[j], out_hbm.at[pl.ds(j * rows, rows), :], sems.at[j]
+            )
+        )
+        copies[j].start()
+    for copy in copies:
+        copy.wait()
+
+
+def grad_down(hidden, grads, prob, after):
     rows, d = grads.shape
     hid = hidden.shape[1]
     return pl.pallas_call(
         down_kernel,
-        grid=(d // block,),
-        in_specs=[
-            pl.BlockSpec((rows, hid), lambda i: (0, 0)),
-            pl.BlockSpec((rows, block), lambda i: (0, i)),
-            pl.BlockSpec((rows, META), lambda i: (0, 0)),
-            ANY,
-        ],
-        out_specs=[
-            pl.BlockSpec((hid, block), lambda i: (0, i)),
-            pl.BlockSpec((8, LANES), lambda i: (0, 0)),
-        ],
+        in_specs=[VMEM] * 3 + [ANY],
+        out_specs=[ANY, VMEM],
         out_shape=[
             jax.ShapeDtypeStruct((hid, d), BF),
             jax.ShapeDtypeStruct((8, LANES), F32),
+        ],
+        scratch_shapes=[
+            pltpu.VMEM((rows, d), BF),
+            pltpu.VMEM((hid // LANES, LANES, d), BF),
+            pltpu.SemaphoreType.DMA((hid // LANES,)),
         ],
         compiler_params=params(),
         cost_estimate=pl.CostEstimate(
@@ -422,18 +456,21 @@
         compiler_params=params(),
     )(device_expert, *[held[o] for o in order], *weights, w_down)
 
-    steps = width // 512
+    steps = list(range(width // 512))
     got = [xor_swap(send, 1)]
-    grad_w_in, after = grad_in(tok, pre, prob, 0, 1)
+    grad_w_in, after = grad_in(tok, pre, prob, steps[:1])
     mine, (by_near, by_side, by_both) = add_step(mine, got, after, 4)
     got = [xor_swap(by_both, 6), xor_swap(by_side, 2), xor_swap(by_near, 4)]
-    grad_w_in, after = grad_in(tok, pre, mine, 1, 2, grad_w_in)
+    grad_w_in, after = grad_in(tok, pre, mine, steps[1:4], grad_w_in)
     grad_w_down, after = grad_down(hidden, grads, prob, after)
     for bit in bits[-4::-1]:
         mine, (send,) = add_step(mine, got, after, 2)
+        if bit == 8:
+            rest = steps[4:]
+            got = [xor_swap(send, bit)]
+            grad_w_in, after = grad_in(tok, pre, mine, rest, grad_w_in)
+            continue
         got = [xor_swap(send, bit)]
-        if bit == 8:
-            grad_w_in, after = grad_in(tok, pre, mine, 3, steps - 3, grad_w_in)
     tiles = hid // LANES
     grad_w_in = grad_w_in.reshape(width, tiles, 2, LANES).transpose(0, 2, 1, 3)
     grad_w_in = grad_w_in.reshape(width, 2, hid)

time: 44.3 us -> 43.6 us (0.984)
  Pallas kernels: 18.5 us -> 17.4 us
  waiting for transfers between devices: 3.7 us -> 4.16 us
    pallas_call x4, Pallas kernels: 8.52 us -> 7.38 us  [the longest x3 5.78 us: grad_in(): pl.pallas_call(functools.partial(win_kernel, blocks, parity), in_specs=[V...]
    ppermute x20, waiting for transfers between devices: 3.7 us -> 4.16 us  [xor_swap(): lax.ppermute(value, 'dev', [(i, i ^ (other if i & 1 else bit)) for i in r...]
  transfers between devices with their start and end apart: 20 -> 20, of which waited for: 9 -> 10; matrix products, arithmetic and copies ran while one was open for 0% -> 0% of each run, Pallas kernels for 28% -> 26%
where the time goes in v5:
time: 43.6 us; the launch traced here: 43.4 us
  starting transfers between devices  21.1 us (48%)
  Pallas kernels  17.4 us (40%)
  waiting for transfers between devices  4.16 us (10%)
  between operations  0.76 us (2%)
    ppermute x20, starting transfers between devices, xor_swap(): lax.ppermute(value, 'dev', [(i, i ^ (other if i & 1 else bit)) for i in r...  21.1 us
    pallas_call x3, Pallas kernels, grad_in(): pl.pallas_call(functools.partial(win_kernel, blocks, parity), in_specs=[V...  5.78 us
    ppermute x20, waiting for transfers between devices, xor_swap(): lax.ppermute(value, 'dev', [(i, i ^ (other if i & 1 else bit)) for i in r...  4.16 us
    pallas_call x3, Pallas kernels, split_weights(): pl.pallas_call(functools.partial(split_kernel, part, when), in_specs=[ANY...  4.01 us
    pallas_call x1, Pallas kernels, shards(): pl.pallas_call(functools.partial(main_kernel, n), in_specs=[SMEM] + [VMEM...  3.39 us
    pallas_call x1, Pallas kernels, grad_down(): pl.pallas_call(down_kernel, in_specs=[VMEM] * 3 + [ANY], out_specs=[ANY,...  1.61 us
    pallas_call x1, Pallas kernels, shards(): pl.pallas_call(pack_kernel, in_specs=[VMEM] * 4, out_specs=VMEM, out_shap...  1.56 us
  transfers between devices with their start and end apart: 20, of which 10 were waited for; matrix products, arithmetic and copies ran while one was open for 0% of the time, Pallas kernels for 26%

profile of v5, /device:TPU:0, one launch (start us, length us, event | category | flops | bytes accessed | tf_op | source)
XLA Modules:
  0.0 43.4 jit_solution(9743978626310320393)
XLA Ops:
  0.7 1.6 %shard_map.102.refs_0_ = bf16[8,6272]{1,0:T(8,128)(2,1)} custom-call(bf16[8,3072]{1,0:T(8,128)(2,1)} %tok_ref.1, bf16[8,3072]{1,0:T(8,128)(2,1)} %grad_ref.1, s32[2,8]{1,0:T(2,128)} %bitcast.13, f32[2,8]{1,0:T(2,128)} %bitcast.19), custom_call_target="tpu_custom_call" | custom-call | tf_op jit(solution)/shard_map/pallas_call | solution.py:409
  2.2 4.0 %collective-permute-start = (bf16[8,6272]{1,0:T(8,128)(2,1)}, bf16[8,6272]{1,0:T(8,128)(2,1)S(1)}, u32[]{:S(2)}, u32[]{:S(2)}) collective-permute-start(bf16[8,6272]{1,0:T(8,128)(2,1)} %shard_map.102.refs_0_), channel_id=1, source_target_pairs={{0,8},{1,9},{2,10},{3,11},{4,12},{5,13},{6,14},{7,15},{8,0},{9,1},... | collective-permute-start | bytes 301064 | tf_op jit(solution)/shard_map/ppermute | solution.py:30
  6.3 1.5 %collective-permute-start.3 = (bf16[8,6272]{1,0:T(8,128)(2,1)}, bf16[8,6272]{1,0:T(8,128)(2,1)S(1)}, u32[]{:S(2)}, u32[]{:S(2)}) collective-permute-start(bf16[8,6272]{1,0:T(8,128)(2,1)} %shard_map.102.refs_0_), channel_id=1, source_target_pairs={{0,2},{1,5},{2,0},{3,7},{4,6},{5,1},{6,4},{7,3},{8,10},{9,13},{10,... | collective-permute-start | bytes 301064 | tf_op jit(solution)/shard_map/ppermute | solution.py:30
  7.8 1.6 %collective-permute-start.1 = (bf16[8,6272]{1,0:T(8,128)(2,1)}, bf16[8,6272]{1,0:T(8,128)(2,1)S(1)}, u32[]{:S(2)}, u32[]{:S(2)}) collective-permute-start(bf16[8,6272]{1,0:T(8,128)(2,1)} %shard_map.102.refs_0_), channel_id=1, source_target_pairs={{0,4},{1,3},{2,6},{3,1},{4,0},{5,7},{6,2},{7,5},{8,12},{9,11},{10,... | collective-permute-start | bytes 301064 | tf_op jit(solution)/shard_map/ppermute | solution.py:30
  9.4 2.0 %shard_map.104.refs_16_ = bf16[1536,512]{1,0:T(8,128)(2,1)S(1)} custom-call(bf16[12288,128]{1,0:T(8,128)(2,1)} %bitcast.16, bf16[1536,512]{1,0:T(8,128)(2,1)S(1)} %shard_map.103.refs_0_), custom_call_target="tpu_custom_call" | custom-call | flops 402653184 | bytes 3145728 | tf_op jit(solution)/shard_map/pallas_call | solution.py:142
  11.4 0.0 copy-start
  11.4 0.0 copy-start.3
  11.4 0.0 collective-permute-done.refs_1_
  11.4 1.4 %collective-permute-start.4 = (bf16[8,6272]{1,0:T(8,128)(2,1)S(1)}, bf16[8,6272]{1,0:T(8,128)(2,1)S(1)}, u32[]{:S(2)}, u32[]{:S(2)}) collective-permute-start(bf16[8,6272]{1,0:T(8,128)(2,1)S(1)} %collective-permute-done.refs_1_), channel_id=1, source_target_pairs={{0,2},{1,5},{2,0},{3,7},{4,6},{5,1},{6,4},{7,3},{8,10},{9,13},{10,... | collective-permute-start | bytes 301064 | tf_op jit(solution)/shard_map/ppermute | solution.py:30
  12.8 2.0 %collective-permute-start.2 = (bf16[8,6272]{1,0:T(8,128)(2,1)S(1)}, bf16[8,6272]{1,0:T(8,128)(2,1)S(1)}, u32[]{:S(2)}, u32[]{:S(2)}) collective-permute-start(bf16[8,6272]{1,0:T(8,128)(2,1)S(1)} %collective-permute-done.refs_1_), channel_id=1, source_target_pairs={{0,4},{1,3},{2,6},{3,1},{4,0},{5,7},{6,2},{7,5},{8,12},{9,11},{10,... | collective-permute-start | bytes 301064 | tf_op jit(solution)/shard_map/ppermute | solution.py:30
  14.9 0.0 collective-permute-start.7
  14.9 0.5 %collective-permute-start.11 = (bf16[8,6272]{1,0:T(8,128)(2,1)S(1)}, bf16[8,6272]{1,0:T(8,128)(2,1)S(1)}, u32[]{:S(2)}, u32[]{:S(2)}) collective-permute-start(bf16[8,6272]{1,0:T(8,128)(2,1)S(1)} %collective-permute-done.3.refs_4_), channel_id=1, source_target_pairs={{0,1},{1,0},{2,3},{3,2},{4,5},{5,4},{6,7},{7,6},{8,9},{9,8},{10,11... | collective-permute-start | bytes 301064 | tf_op jit(solution)/shard_map/ppermute | solution.py:30
  15.4 0.3 collective-permute-start.5
  15.7 0.6 %collective-permute-done.4.refs_5_ = bf16[8,6272]{1,0:T(8,128)(2,1)S(1)} collective-permute-done((bf16[8,6272]{1,0:T(8,128)(2,1)S(1)}, bf16[8,6272]{1,0:T(8,128)(2,1)S(1)}, u32[]{:S(2)}, u32[]{:S(2)}) %collective-permute-start.4) | collective-permute-done | bytes 100384 | tf_op jit(solution)/shard_map/ppermute | solution.py:30
  16.3 1.2 %collective-permute-done.2.refs_3_ = bf16[8,6272]{1,0:T(8,128)(2,1)S(1)} collective-permute-done((bf16[8,6272]{1,0:T(8,128)(2,1)S(1)}, bf16[8,6272]{1,0:T(8,128)(2,1)S(1)}, u32[]{:S(2)}, u32[]{:S(2)}) %collective-permute-start.2) | collective-permute-done | bytes 100384 | tf_op jit(solution)/shard_map/ppermute | solution.py:30
  17.5 1.4 %collective-permute-start.6 = (bf16[8,6272]{1,0:T(8,128)(2,1)S(1)}, bf16[8,6272]{1,0:T(8,128)(2,1)S(1)}, u32[]{:S(2)}, u32[]{:S(2)}) collective-permute-start(bf16[8,6272]{1,0:T(8,128)(2,1)S(1)} %collective-permute-done.2.refs_3_), channel_id=1, source_target_pairs={{0,2},{1,5},{2,0},{3,7},{4,6},{5,1},{6,4},{7,3},{8,10},{9,13},{10,... | collective-permute-start | bytes 301064 | tf_op jit(solution)/shard_map/ppermute | solution.py:30
  18.9 2.0 %shard_map.105.refs_17_ = bf16[1536,512]{1,0:T(8,128)(2,1)S(1)} custom-call(bf16[12288,128]{1,0:T(8,128)(2,1)} %bitcast.17), custom_call_target="tpu_custom_call" | custom-call | flops 402653184 | bytes 3145728 | tf_op jit(solution)/shard_map/pallas_call | solution.py:142
  20.9 0.4 collective-permute-start.8
  21.3 0.0 collective-permute-done.11.refs_12_
  21.3 0.2 collective-permute-start.12
  21.4 0.0 collective-permute-done.5.refs_6_
  21.4 0.3 collective-permute-start.13
  21.8 0.0 collective-permute-done.9.refs_10_
  21.8 0.2 collective-permute-start.10
  22.0 0.2 collective-permute-done.6.refs_7_
  22.1 0.2 collective-permute-start.14
  22.3 0.0 collective-permute-done.8.refs_9_
  22.3 0.4 %collective-permute-done.13.refs_14_ = bf16[8,6272]{1,0:T(8,128)(2,1)S(1)} collective-permute-done((bf16[8,6272]{1,0:T(8,128)(2,1)S(1)}, bf16[8,6272]{1,0:T(8,128)(2,1)S(1)}, u32[]{:S(2)}, u32[]{:S(2)}) %collective-permute-start.13) | collective-permute-done | bytes 100384 | tf_op jit(solution)/shard_map/ppermute | solution.py:30
  22.7 0.0 collective-permute-done.12.refs_13_
  22.8 0.3 collective-permute-done.10.refs_11_
  23.1 0.4 collective-permute-done.14.refs_15_
  23.5 3.4 %shard_map.106 = (bf16[128,3072]{1,0:T(8,128)(2,1)S(1)}, bf16[128,3072]{1,0:T(8,128)(2,1)S(1)}, bf16[128,512]{1,0:T(8,128)(2,1)S(1)}, bf16[128,256]{1,0:T(8,128)...) custom-call(s32[16]{0:T(128)S(1)} %copy-done.3, ...), custom_call_target="tpu_custom_call" | custom-call | tf_op jit(solution)/shard_map/pallas_call | solution.py:443
  26.9 0.2 collective-permute-start.15
  27.1 1.4 %shard_map.107 = (bf16[12288,128]{1,0:T(8,128)(2,1)}, f32[8,128]{1,0:T(8,128)S(1)}) custom-call(bf16[128,3072]{1,0:T(8,128)(2,1)S(1)} %get-tuple-element.41.tok_ref, bf16[128,512]{1,0:T(8,128)(2,1)S(1)} %get-tuple-element.42.pre_ref, f32[128,128]{1,0:T(8,128)S(1)} %get-tuple-element.43.refs_0_.prob_ref), custom_call_target="tpu_custom_call" | custom-call | flops 67108864 | bytes 1048576 | tf_op jit(solution)/shard_map/pallas_call | solution.py:336
  28.4 0.2 collective-permute-done.15.refs_0_
  28.7 0.2 shard_map.108
  28.8 2.6 %collective-permute-start.16 = (bf16[16,3200]{1,0:T(8,128)(2,1)S(1)}, bf16[16,3200]{1,0:T(8,128)(2,1)S(1)}, u32[]{:S(2)}, u32[]{:S(2)}) collective-permute-start(bf16[16,3200]{1,0:T(8,128)(2,1)S(1)} %get-tuple-element.46), channel_id=1, source_target_pairs={{0,6},{1,7},{2,4},{3,5},{4,2},{5,3},{6,0},{7,1},{8,14},{9,15},{10,... | collective-permute-start | bytes 307208 | tf_op jit(solution)/shard_map/ppermute | solution.py:30
  31.4 1.0 %collective-permute-start.17 = (bf16[16,3200]{1,0:T(8,128)(2,1)S(1)}, bf16[16,3200]{1,0:T(8,128)(2,1)S(1)}, u32[]{:S(2)}, u32[]{:S(2)}) collective-permute-start(bf16[16,3200]{1,0:T(8,128)(2,1)S(1)} %get-tuple-element.47), channel_id=1, source_target_pairs={{0,2},{1,5},{2,0},{3,7},{4,6},{5,1},{6,4},{7,3},{8,10},{9,13},{10,... | collective-permute-start | bytes 307208 | tf_op jit(solution)/shard_map/ppermute | solution.py:30
  32.4 0.0 collective-permute-start.18
  32.4 2.7 %shard_map.109 = (bf16[12288,128]{1,0:T(8,128)(2,1)}, f32[8,128]{1,0:T(8,128)S(1)}) custom-call(bf16[128,3072]{1,0:T(8,128)(2,1)S(1)} %get-tuple-element.41.tok_ref, bf16[128,512]{1,0:T(8,128)(2,1)S(1)} %get-tuple-element.42.pre_ref, f32[16,3200]{1,0:T(8,128)S(1)} %get-tuple-element.45.refs_0_.own_ref, ...), custom_call_target="tpu_custom_call", output_to_operand_aliasing={{0}: (3, {})} | custom-call | flops 201326592 | bytes 3145728 | tf_op jit(solution)/shard_map/pallas_call | solution.py:336
  35.1 1.6 %shard_map.110 = (bf16[256,3072]{1,0:T(8,128)(2,1)}, f32[8,128]{1,0:T(8,128)S(1)}) custom-call(bf16[128,256]{1,0:T(8,128)(2,1)S(1)} %get-tuple-element.49.hid_ref, bf16[128,3072]{1,0:T(8,128)(2,1)S(1)} %get-tuple-element.50.grad_ref, f32[128,128]{1,0:T(8,128)S(1)} %get-tuple-element.43.refs_0_.prob_ref, f32[8,128]{1,0:T(8,128)S(1)} %get-tuple-element.52.after_ref), custom_call_target="tpu_custom_call" | custom-call | flops 201326592 | bytes 3145728 | tf_op jit(solution)/shard_map/pallas_call | solution.py:381
  36.7 0.2 collective-permute-done.17.refs_1_
  36.9 0.2 collective-permute-done.18.refs_2_
  37.1 0.1 shard_map.111
  37.2 3.4 %collective-permute-start.19 = (bf16[8,3200]{1,0:T(8,128)(2,1)S(1)}, bf16[8,3200]{1,0:T(8,128)(2,1)S(1)}, u32[]{:S(2)}, u32[]{:S(2)}) collective-permute-start(bf16[8,3200]{1,0:T(8,128)(2,1)S(1)} %get-tuple-element.55), channel_id=1, source_target_pairs={{0,8},{1,9},{2,10},{3,11},{4,12},{5,13},{6,14},{7,15},{8,0},{9,1},... | collective-permute-start | bytes 153608 | tf_op jit(solution)/shard_map/ppermute | solution.py:30
  40.6 1.7 %shard_map.112 = (bf16[12288,128]{1,0:T(8,128)(2,1)}, f32[8,128]{1,0:T(8,128)S(1)}) custom-call(bf16[128,3072]{1,0:T(8,128)(2,1)S(1)} %get-tuple-element.41.tok_ref, bf16[128,512]{1,0:T(8,128)(2,1)S(1)} %get-tuple-element.42.pre_ref, f32[8,3200]{1,0:T(8,128)S(1)} %get-tuple-element.54.refs_0_.own_ref, ...), custom_call_target="tpu_custom_call", output_to_operand_aliasing={{0}: (3, {})} | custom-call | flops 134217728 | bytes 2097152 | tf_op jit(solution)/shard_map/pallas_call | solution.py:336
  42.3 0.4 collective-permute-done.19.got_ref
  42.7 0.7 %shard_map.113 = (bf16[8,3072]{1,0:T(8,128)(2,1)}, f32[2,8]{1,0:T(2,128)}) custom-call(f32[8,3200]{1,0:T(8,128)S(1)} %get-tuple-element.54.refs_0_.own_ref, bf16[8,3200]{1,0:T(8,128)(2,1)S(1)} %collective-permute-done.19.got_ref, s32[2,8]{1,0:T(2,128)S(1)} %bitcast.14, f32[8,128]{1,0:T(8,128)S(1)} %get-tuple-element.57.after_ref), custom_call_target="tpu_custom_call" | custom-call | tf_op jit(solution)/shard_map/pallas_call | solution.py:477
  (12 shorter events, 0.1 us)
Async XLA Ops:
  2.2 12.6 %copy-start.1 = (bf16[8,6272]{1,0:T(8,128)(2,1)S(1)}, bf16[8,6272]{1,0:T(8,128)(2,1)}, u32[]{:S(2)}) copy-start(bf16[8,6272]{1,0:T(8,128)(2,1)} %shard_map.102.refs_0_) | copy-start | bytes 301060
  2.2 9.2 %collective-permute-start = (bf16[8,6272]{1,0:T(8,128)(2,1)}, bf16[8,6272]{1,0:T(8,128)(2,1)S(1)}, u32[]{:S(2)}, u32[]{:S(2)}) collective-permute-start(bf16[8,6272]{1,0:T(8,128)(2,1)} %shard_map.102.refs_0_), channel_id=1, source_target_pairs={{0,8},{1,9},{2,10},{3,11},{4,12},{5,13},{6,14},{7,15},{8,0},{9,1},... | collective-permute-start | bytes 301064 | tf_op jit(solution)/shard_map/ppermute | solution.py:30
  6.3 8.6 %collective-permute-start.3 = (bf16[8,6272]{1,0:T(8,128)(2,1)}, bf16[8,6272]{1,0:T(8,128)(2,1)S(1)}, u32[]{:S(2)}, u32[]{:S(2)}) collective-permute-start(bf16[8,6272]{1,0:T(8,128)(2,1)} %shard_map.102.refs_0_), channel_id=1, source_target_pairs={{0,2},{1,5},{2,0},{3,7},{4,6},{5,1},{6,4},{7,3},{8,10},{9,13},{10,... | collective-permute-start | bytes 301064 | tf_op jit(solution)/shard_map/ppermute | solution.py:30
  7.8 7.6 %collective-permute-start.1 = (bf16[8,6272]{1,0:T(8,128)(2,1)}, bf16[8,6272]{1,0:T(8,128)(2,1)S(1)}, u32[]{:S(2)}, u32[]{:S(2)}) collective-permute-start(bf16[8,6272]{1,0:T(8,128)(2,1)} %shard_map.102.refs_0_), channel_id=1, source_target_pairs={{0,4},{1,3},{2,6},{3,1},{4,0},{5,7},{6,2},{7,5},{8,12},{9,11},{10,... | collective-permute-start | bytes 301064 | tf_op jit(solution)/shard_map/ppermute | solution.py:30
  11.4 12.1 %copy-start = (bf16[256,3072]{1,0:T(8,128)(2,1)S(1)}, bf16[256,3072]{1,0:T(8,128)(2,1)}, u32[]{:S(2)}) copy-start(bf16[256,3072]{1,0:T(8,128)(2,1)} %refs_18_.1) | copy-start | bytes 4718596
  11.4 12.1 %copy-start.3 = (s32[16]{0:T(128)S(1)}, s32[16]{0:T(128)}, u32[]{:S(2)}) copy-start(s32[16]{0:T(128)} %owner_ref.1) | copy-start | bytes 196
  11.4 4.9 %collective-permute-start.4 = (bf16[8,6272]{1,0:T(8,128)(2,1)S(1)}, bf16[8,6272]{1,0:T(8,128)(2,1)S(1)}, u32[]{:S(2)}, u32[]{:S(2)}) collective-permute-start(bf16[8,6272]{1,0:T(8,128)(2,1)S(1)} %collective-permute-done.refs_1_), channel_id=1, source_target_pairs={{0,2},{1,5},{2,0},{3,7},{4,6},{5,1},{6,4},{7,3},{8,10},{9,13},{10,... | collective-permute-start | bytes 301064 | tf_op jit(solution)/shard_map/ppermute | solution.py:30
  12.8 4.7 %collective-permute-start.2 = (bf16[8,6272]{1,0:T(8,128)(2,1)S(1)}, bf16[8,6272]{1,0:T(8,128)(2,1)S(1)}, u32[]{:S(2)}, u32[]{:S(2)}) collective-permute-start(bf16[8,6272]{1,0:T(8,128)(2,1)S(1)} %collective-permute-done.refs_1_), channel_id=1, source_target_pairs={{0,4},{1,3},{2,6},{3,1},{4,0},{5,7},{6,2},{7,5},{8,12},{9,11},{10,... | collective-permute-start | bytes 301064 | tf_op jit(solution)/shard_map/ppermute | solution.py:30
  14.9 6.0 %collective-permute-start.7 = (bf16[8,6272]{1,0:T(8,128)(2,1)S(1)}, bf16[8,6272]{1,0:T(8,128)(2,1)S(1)}, u32[]{:S(2)}, u32[]{:S(2)}) collective-permute-start(bf16[8,6272]{1,0:T(8,128)(2,1)S(1)} %copy-done.1), channel_id=1, source_target_pairs={{0,1},{1,0},{2,3},{3,2},{4,5},{5,4},{6,7},{7,6},{8,9},{9,8},{10,11... | collective-permute-start | bytes 301064 | tf_op jit(solution)/shard_map/ppermute | solution.py:30
  14.9 6.4 %collective-permute-start.11 = (bf16[8,6272]{1,0:T(8,128)(2,1)S(1)}, bf16[8,6272]{1,0:T(8,128)(2,1)S(1)}, u32[]{:S(2)}, u32[]{:S(2)}) collective-permute-start(bf16[8,6272]{1,0:T(8,128)(2,1)S(1)} %collective-permute-done.3.refs_4_), channel_id=1, source_target_pairs={{0,1},{1,0},{2,3},{3,2},{4,5},{5,4},{6,7},{7,6},{8,9},{9,8},{10,11... | collective-permute-start | bytes 301064 | tf_op jit(solution)/shard_map/ppermute | solution.py:30
  15.4 6.0 %collective-permute-start.5 = (bf16[8,6272]{1,0:T(8,128)(2,1)S(1)}, bf16[8,6272]{1,0:T(8,128)(2,1)S(1)}, u32[]{:S(2)}, u32[]{:S(2)}) collective-permute-start(bf16[8,6272]{1,0:T(8,128)(2,1)S(1)} %collective-permute-done.3.refs_4_), channel_id=1, source_target_pairs={{0,4},{1,3},{2,6},{3,1},{4,0},{5,7},{6,2},{7,5},{8,12},{9,11},{10,... | collective-permute-start | bytes 301064 | tf_op jit(solution)/shard_map/ppermute | solution.py:30
  16.3 5.5 %collective-permute-start.9 = (bf16[8,6272]{1,0:T(8,128)(2,1)S(1)}, bf16[8,6272]{1,0:T(8,128)(2,1)S(1)}, u32[]{:S(2)}, u32[]{:S(2)}) collective-permute-start(bf16[8,6272]{1,0:T(8,128)(2,1)S(1)} %collective-permute-done.1.refs_2_), channel_id=1, source_target_pairs={{0,1},{1,0},{2,3},{3,2},{4,5},{5,4},{6,7},{7,6},{8,9},{9,8},{10,11... | collective-permute-start | bytes 301064 | tf_op jit(solution)/shard_map/ppermute | solution.py:30
  17.5 4.6 %collective-permute-start.6 = (bf16[8,6272]{1,0:T(8,128)(2,1)S(1)}, bf16[8,6272]{1,0:T(8,128)(2,1)S(1)}, u32[]{:S(2)}, u32[]{:S(2)}) collective-permute-start(bf16[8,6272]{1,0:T(8,128)(2,1)S(1)} %collective-permute-done.2.refs_3_), channel_id=1, source_target_pairs={{0,2},{1,5},{2,0},{3,7},{4,6},{5,1},{6,4},{7,3},{8,10},{9,13},{10,... | collective-permute-start | bytes 301064 | tf_op jit(solution)/shard_map/ppermute | solution.py:30
  20.9 1.4 %collective-permute-start.8 = (bf16[8,6272]{1,0:T(8,128)(2,1)S(1)}, bf16[8,6272]{1,0:T(8,128)(2,1)S(1)}, u32[]{:S(2)}, u32[]{:S(2)}) collective-permute-start(bf16[8,6272]{1,0:T(8,128)(2,1)S(1)} %collective-permute-done.refs_1_), channel_id=1, source_target_pairs={{0,1},{1,0},{2,3},{3,2},{4,5},{5,4},{6,7},{7,6},{8,9},{9,8},{10,11... | collective-permute-start | bytes 301064 | tf_op jit(solution)/shard_map/ppermute | solution.py:30
  21.3 1.5 %collective-permute-start.12 = (bf16[8,6272]{1,0:T(8,128)(2,1)S(1)}, bf16[8,6272]{1,0:T(8,128)(2,1)S(1)}, u32[]{:S(2)}, u32[]{:S(2)}) collective-permute-start(bf16[8,6272]{1,0:T(8,128)(2,1)S(1)} %collective-permute-done.4.refs_5_), channel_id=1, source_target_pairs={{0,1},{1,0},{2,3},{3,2},{4,5},{5,4},{6,7},{7,6},{8,9},{9,8},{10,11... | collective-permute-start | bytes 301064 | tf_op jit(solution)/shard_map/ppermute | solution.py:30
  21.4 1.3 %collective-permute-start.13 = (bf16[8,6272]{1,0:T(8,128)(2,1)S(1)}, bf16[8,6272]{1,0:T(8,128)(2,1)S(1)}, u32[]{:S(2)}, u32[]{:S(2)}) collective-permute-start(bf16[8,6272]{1,0:T(8,128)(2,1)S(1)} %collective-permute-done.5.refs_6_), channel_id=1, source_target_pairs={{0,1},{1,0},{2,3},{3,2},{4,5},{5,4},{6,7},{7,6},{8,9},{9,8},{10,11... | collective-permute-start | bytes 301064 | tf_op jit(solution)/shard_map/ppermute | solution.py:30
  21.8 1.3 %collective-permute-start.10 = (bf16[8,6272]{1,0:T(8,128)(2,1)S(1)}, bf16[8,6272]{1,0:T(8,128)(2,1)S(1)}, u32[]{:S(2)}, u32[]{:S(2)}) collective-permute-start(bf16[8,6272]{1,0:T(8,128)(2,1)S(1)} %collective-permute-done.2.refs_3_), channel_id=1, source_target_pairs={{0,1},{1,0},{2,3},{3,2},{4,5},{5,4},{6,7},{7,6},{8,9},{9,8},{10,11... | collective-permute-start | bytes 301064 | tf_op jit(solution)/shard_map/ppermute | solution.py:30
  22.1 1.3 %collective-permute-start.14 = (bf16[8,6272]{1,0:T(8,128)(2,1)S(1)}, bf16[8,6272]{1,0:T(8,128)(2,1)S(1)}, u32[]{:S(2)}, u32[]{:S(2)}) collective-permute-start(bf16[8,6272]{1,0:T(8,128)(2,1)S(1)} %collective-permute-done.6.refs_7_), channel_id=1, source_target_pairs={{0,1},{1,0},{2,3},{3,2},{4,5},{5,4},{6,7},{7,6},{8,9},{9,8},{10,11... | collective-permute-start | bytes 301064 | tf_op jit(solution)/shard_map/ppermute | solution.py:30
  26.9 1.8 %collective-permute-start.15 = (bf16[64,3200]{1,0:T(8,128)(2,1)S(1)}, bf16[64,3200]{1,0:T(8,128)(2,1)S(1)}, u32[]{:S(2)}, u32[]{:S(2)}) collective-permute-start(bf16[64,3200]{1,0:T(8,128)(2,1)S(1)} %get-tuple-element.40), channel_id=1, source_target_pairs={{0,1},{1,0},{2,3},{3,2},{4,5},{5,4},{6,7},{7,6},{8,9},{9,8},{10,11... | collective-permute-start | bytes 1228808 | tf_op jit(solution)/shard_map/ppermute | solution.py:30
  28.8 7.9 %collective-permute-start.16 = (bf16[16,3200]{1,0:T(8,128)(2,1)S(1)}, bf16[16,3200]{1,0:T(8,128)(2,1)S(1)}, u32[]{:S(2)}, u32[]{:S(2)}) collective-permute-start(bf16[16,3200]{1,0:T(8,128)(2,1)S(1)} %get-tuple-element.46), channel_id=1, source_target_pairs={{0,6},{1,7},{2,4},{3,5},{4,2},{5,3},{6,0},{7,1},{8,14},{9,15},{10,... | collective-permute-start | bytes 307208 | tf_op jit(solution)/shard_map/ppermute | solution.py:30
  31.4 5.5 %collective-permute-start.17 = (bf16[16,3200]{1,0:T(8,128)(2,1)S(1)}, bf16[16,3200]{1,0:T(8,128)(2,1)S(1)}, u32[]{:S(2)}, u32[]{:S(2)}) collective-permute-start(bf16[16,3200]{1,0:T(8,128)(2,1)S(1)} %get-tuple-element.47), channel_id=1, source_target_pairs={{0,2},{1,5},{2,0},{3,7},{4,6},{5,1},{6,4},{7,3},{8,10},{9,13},{10,... | collective-permute-start | bytes 307208 | tf_op jit(solution)/shard_map/ppermute | solution.py:30
  32.4 4.7 %collective-permute-start.18 = (bf16[16,3200]{1,0:T(8,128)(2,1)S(1)}, bf16[16,3200]{1,0:T(8,128)(2,1)S(1)}, u32[]{:S(2)}, u32[]{:S(2)}) collective-permute-start(bf16[16,3200]{1,0:T(8,128)(2,1)S(1)} %get-tuple-element.48), channel_id=1, source_target_pairs={{0,4},{1,3},{2,6},{3,1},{4,0},{5,7},{6,2},{7,5},{8,12},{9,11},{10,... | collective-permute-start | bytes 307208 | tf_op jit(solution)/shard_map/ppermute | solution.py:30
  37.2 5.4 %collective-permute-start.19 = (bf16[8,3200]{1,0:T(8,128)(2,1)S(1)}, bf16[8,3200]{1,0:T(8,128)(2,1)S(1)}, u32[]{:S(2)}, u32[]{:S(2)}) collective-permute-start(bf16[8,3200]{1,0:T(8,128)(2,1)S(1)} %get-tuple-element.55), channel_id=1, source_target_pairs={{0,8},{1,9},{2,10},{3,11},{4,12},{5,13},{6,14},{7,15},{8,0},{9,1},... | collective-permute-start | bytes 153608 | tf_op jit(solution)/shard_map/ppermute | solution.py:30
  40.6 2.1 %copy-start.2 = (s32[8,2]{0,1:T(2,128)S(1)}, s32[8,2]{0,1:T(2,128)}, u32[]{:S(2)}) copy-start(s32[8,2]{0,1:T(2,128)} %param.9) | copy-start | bytes 196

commit v6 on v5

--- a/solution.py
+++ b/solution.py
@@ -411,7 +411,7 @@
         in_specs=[VMEM] * 4,
         out_specs=VMEM,
         out_shape=jax.ShapeDtypeStruct((rows, 2 * width + META), BF),
-        compiler_params=params(60),
+        compiler_params=params(),
     )(tokens, grad_out, ids_t, probs_t)
 
     order = [0]
@@ -428,9 +428,9 @@
             held[o] = xor_swap(piece(o ^ bit), bit)
         return held[o]
 
-    early = split_weights(view, 0, width, 2 * hid, 1)
+    early = split_weights(view, 0, width, 2 * hid, 0)
     held[0], early = lax.optimization_barrier((own, early))
-    low = split_weights(view, 0, width, 2 * hid, 0, early)
+    low = split_weights(view, 0, width, 2 * hid, 1, early)
     high = split_weights(view, 1, width, 2 * hid)
     held[far], low = lax.optimization_barrier((piece(far), low))
     held[far + 2], high = lax.optimization_barrier((piece(far + 2), high))

time: 43.6 us -> 41.9 us (0.961)
  Pallas kernels: 17.4 us -> 16 us
    pallas_call x1, Pallas kernels: 1.56 us -> 0.09 us  [shards(): pl.pallas_call(pack_kernel, in_specs=[VMEM] * 4, out_specs=VMEM, out_shap...]
  transfers between devices with their start and end apart: 20 -> 20, of which waited for: 10 -> 9; matrix products, arithmetic and copies ran while one was open for 0% -> 0% of each run, Pallas kernels for 26% -> 23%
where the time goes in v6:
time: 41.9 us; the launch traced here: 41.7 us
  starting transfers between devices  20.8 us (50%)
  Pallas kernels  16 us (38%)
  waiting for transfers between devices  4.09 us (10%)
  between operations  0.83 us (2%)
    ppermute x20, starting transfers between devices, xor_swap(): lax.ppermute(value, 'dev', [(i, i ^ (other if i & 1 else bit)) for i in r...  20.8 us
    pallas_call x3, Pallas kernels, grad_in(): pl.pallas_call(functools.partial(win_kernel, blocks, parity), in_specs=[V...  5.78 us
    pallas_call x3, Pallas kernels, split_weights(): pl.pallas_call(functools.partial(split_kernel, part, when), in_specs=[ANY...  4.13 us
    ppermute x20, waiting for transfers between devices, xor_swap(): lax.ppermute(value, 'dev', [(i, i ^ (other if i & 1 else bit)) for i in r...  4.09 us
    pallas_call x1, Pallas kernels, shards(): pl.pallas_call(functools.partial(main_kernel, n), in_specs=[SMEM] + [VMEM...  3.39 us
    pallas_call x1, Pallas kernels, grad_down(): pl.pallas_call(down_kernel, in_specs=[VMEM] * 3 + [ANY], out_specs=[ANY,...  1.6 us
  transfers between devices with their start and end apart: 20, of which 9 were waited for; matrix products, arithmetic and copies ran while one was open for 0% of the time, Pallas kernels for 23%

profile of v6, /device:TPU:0, one launch (start us, length us, event | category | flops | bytes accessed | tf_op | source)
XLA Modules:
  0.0 41.7 jit_solution(5682953557036743367)
XLA Ops:
  0.7 2.0 %shard_map.103.refs_0_ = bf16[1536,512]{1,0:T(8,128)(2,1)S(1)} custom-call(bf16[12288,128]{1,0:T(8,128)(2,1)} %bitcast.16), custom_call_target="tpu_custom_call" | custom-call | flops 402653184 | bytes 3145728 | tf_op jit(solution)/shard_map/pallas_call | solution.py:142
  2.7 0.1 shard_map.102.refs_0_
  2.8 4.1 %collective-permute-start = (bf16[8,6272]{1,0:T(8,128)(2,1)S(1)}, bf16[8,6272]{1,0:T(8,128)(2,1)S(1)}, u32[]{:S(2)}, u32[]{:S(2)}) collective-permute-start(bf16[8,6272]{1,0:T(8,128)(2,1)S(1)} %shard_map.102.refs_0_), channel_id=1, source_target_pairs={{0,8},{1,9},{2,10},{3,11},{4,12},{5,13},{6,14},{7,15},{8,0},{9,1},... | collective-permute-start | bytes 301064 | tf_op jit(solution)/shard_map/ppermute | solution.py:30
  6.9 1.5 %collective-permute-start.3 = (bf16[8,6272]{1,0:T(8,128)(2,1)S(1)}, bf16[8,6272]{1,0:T(8,128)(2,1)S(1)}, u32[]{:S(2)}, u32[]{:S(2)}) collective-permute-start(bf16[8,6272]{1,0:T(8,128)(2,1)S(1)} %shard_map.102.refs_0_), channel_id=1, source_target_pairs={{0,2},{1,5},{2,0},{3,7},{4,6},{5,1},{6,4},{7,3},{8,10},{9,13},{10,... | collective-permute-start | bytes 301064 | tf_op jit(solution)/shard_map/ppermute | solution.py:30
  8.4 1.6 %collective-permute-start.1 = (bf16[8,6272]{1,0:T(8,128)(2,1)S(1)}, bf16[8,6272]{1,0:T(8,128)(2,1)S(1)}, u32[]{:S(2)}, u32[]{:S(2)}) collective-permute-start(bf16[8,6272]{1,0:T(8,128)(2,1)S(1)} %shard_map.102.refs_0_), channel_id=1, source_target_pairs={{0,4},{1,3},{2,6},{3,1},{4,0},{5,7},{6,2},{7,5},{8,12},{9,11},{10,... | collective-permute-start | bytes 301064 | tf_op jit(solution)/shard_map/ppermute | solution.py:30
  10.0 0.1 shard_map.104.refs_16_
  10.2 0.0 copy-start
  10.2 0.0 copy-start.5
  10.2 1.3 %collective-permute-start.4 = (bf16[8,6272]{1,0:T(8,128)(2,1)S(1)}, bf16[8,6272]{1,0:T(8,128)(2,1)S(1)}, u32[]{:S(2)}, u32[]{:S(2)}) collective-permute-start(bf16[8,6272]{1,0:T(8,128)(2,1)S(1)} %collective-permute-done.refs_1_), channel_id=1, source_target_pairs={{0,2},{1,5},{2,0},{3,7},{4,6},{5,1},{6,4},{7,3},{8,10},{9,13},{10,... | collective-permute-start | bytes 301064 | tf_op jit(solution)/shard_map/ppermute | solution.py:30
  11.5 1.7 %collective-permute-start.2 = (bf16[8,6272]{1,0:T(8,128)(2,1)S(1)}, bf16[8,6272]{1,0:T(8,128)(2,1)S(1)}, u32[]{:S(2)}, u32[]{:S(2)}) collective-permute-start(bf16[8,6272]{1,0:T(8,128)(2,1)S(1)} %collective-permute-done.refs_1_), channel_id=1, source_target_pairs={{0,4},{1,3},{2,6},{3,1},{4,0},{5,7},{6,2},{7,5},{8,12},{9,11},{10,... | collective-permute-start | bytes 301064 | tf_op jit(solution)/shard_map/ppermute | solution.py:30
  13.2 0.5 %collective-permute-start.11 = (bf16[8,6272]{1,0:T(8,128)(2,1)S(1)}, bf16[8,6272]{1,0:T(8,128)(2,1)S(1)}, u32[]{:S(2)}, u32[]{:S(2)}) collective-permute-start(bf16[8,6272]{1,0:T(8,128)(2,1)S(1)} %collective-permute-done.3.refs_4_), channel_id=1, source_target_pairs={{0,1},{1,0},{2,3},{3,2},{4,5},{5,4},{6,7},{7,6},{8,9},{9,8},{10,11... | collective-permute-start | bytes 301064 | tf_op jit(solution)/shard_map/ppermute | solution.py:30
  13.7 0.2 collective-permute-done.1.refs_2_
  13.8 1.2 %collective-permute-start.5 = (bf16[8,6272]{1,0:T(8,128)(2,1)S(1)}, bf16[8,6272]{1,0:T(8,128)(2,1)S(1)}, u32[]{:S(2)}, u32[]{:S(2)}) collective-permute-start(bf16[8,6272]{1,0:T(8,128)(2,1)S(1)} %collective-permute-done.3.refs_4_), channel_id=1, source_target_pairs={{0,4},{1,3},{2,6},{3,1},{4,0},{5,7},{6,2},{7,5},{8,12},{9,11},{10,... | collective-permute-start | bytes 301064 | tf_op jit(solution)/shard_map/ppermute | solution.py:30
  15.0 0.0 collective-permute-done.4.refs_5_
  15.0 0.0 collective-permute-start.9
  15.0 1.1 %collective-permute-done.2.refs_3_ = bf16[8,6272]{1,0:T(8,128)(2,1)S(1)} collective-permute-done((bf16[8,6272]{1,0:T(8,128)(2,1)S(1)}, bf16[8,6272]{1,0:T(8,128)(2,1)S(1)}, u32[]{:S(2)}, u32[]{:S(2)}) %collective-permute-start.2) | collective-permute-done | bytes 100384 | tf_op jit(solution)/shard_map/ppermute | solution.py:30
  16.1 0.8 %collective-permute-start.6 = (bf16[8,6272]{1,0:T(8,128)(2,1)S(1)}, bf16[8,6272]{1,0:T(8,128)(2,1)S(1)}, u32[]{:S(2)}, u32[]{:S(2)}) collective-permute-start(bf16[8,6272]{1,0:T(8,128)(2,1)S(1)} %collective-permute-done.2.refs_3_), channel_id=1, source_target_pairs={{0,2},{1,5},{2,0},{3,7},{4,6},{5,1},{6,4},{7,3},{8,10},{9,13},{10,... | collective-permute-start | bytes 301064 | tf_op jit(solution)/shard_map/ppermute | solution.py:30
  16.9 2.0 %shard_map.105.refs_17_ = bf16[1536,512]{1,0:T(8,128)(2,1)S(1)} custom-call(bf16[12288,128]{1,0:T(8,128)(2,1)} %bitcast.18), custom_call_target="tpu_custom_call" | custom-call | flops 402653184 | bytes 3145728 | tf_op jit(solution)/shard_map/pallas_call | solution.py:142
  18.9 0.0 collective-permute-done.7.refs_8_
  18.9 0.1 collective-permute-start.8
  19.0 0.0 collective-permute-done.11.refs_12_
  19.0 0.5 %collective-permute-start.12 = (bf16[8,6272]{1,0:T(8,128)(2,1)S(1)}, bf16[8,6272]{1,0:T(8,128)(2,1)S(1)}, u32[]{:S(2)}, u32[]{:S(2)}) collective-permute-start(bf16[8,6272]{1,0:T(8,128)(2,1)S(1)} %collective-permute-done.4.refs_5_), channel_id=1, source_target_pairs={{0,1},{1,0},{2,3},{3,2},{4,5},{5,4},{6,7},{7,6},{8,9},{9,8},{10,11... | collective-permute-start | bytes 301064 | tf_op jit(solution)/shard_map/ppermute | solution.py:30
  19.5 0.1 collective-permute-start.13
  19.6 0.0 collective-permute-done.9.refs_10_
  19.6 0.4 %collective-permute-start.10 = (bf16[8,6272]{1,0:T(8,128)(2,1)S(1)}, bf16[8,6272]{1,0:T(8,128)(2,1)S(1)}, u32[]{:S(2)}, u32[]{:S(2)}) collective-permute-start(bf16[8,6272]{1,0:T(8,128)(2,1)S(1)} %collective-permute-done.2.refs_3_), channel_id=1, source_target_pairs={{0,1},{1,0},{2,3},{3,2},{4,5},{5,4},{6,7},{7,6},{8,9},{9,8},{10,11... | collective-permute-start | bytes 301064 | tf_op jit(solution)/shard_map/ppermute | solution.py:30
  20.0 0.7 %collective-permute-done.6.refs_7_ = bf16[8,6272]{1,0:T(8,128)(2,1)S(1)} collective-permute-done((bf16[8,6272]{1,0:T(8,128)(2,1)S(1)}, bf16[8,6272]{1,0:T(8,128)(2,1)S(1)}, u32[]{:S(2)}, u32[]{:S(2)}) %collective-permute-start.6) | collective-permute-done | bytes 100384 | tf_op jit(solution)/shard_map/ppermute | solution.py:30
  20.7 0.0 collective-permute-start.14
  20.7 0.0 collective-permute-done.8.refs_9_
  20.8 0.1 collective-permute-done.13.refs_14_
  20.8 0.2 collective-permute-done.10.refs_11_
  21.0 1.1 %collective-permute-done.14.refs_15_ = bf16[8,6272]{1,0:T(8,128)(2,1)S(1)} collective-permute-done((bf16[8,6272]{1,0:T(8,128)(2,1)S(1)}, bf16[8,6272]{1,0:T(8,128)(2,1)S(1)}, u32[]{:S(2)}, u32[]{:S(2)}) %collective-permute-start.14) | collective-permute-done | bytes 100384 | tf_op jit(solution)/shard_map/ppermute | solution.py:30
  22.1 3.4 %shard_map.106 = (bf16[128,3072]{1,0:T(8,128)(2,1)S(1)}, bf16[128,3072]{1,0:T(8,128)(2,1)S(1)}, bf16[128,512]{1,0:T(8,128)(2,1)S(1)}, bf16[128,256]{1,0:T(8,128)...) custom-call(s32[16]{0:T(128)S(1)} %copy-done.5, ...), custom_call_target="tpu_custom_call" | custom-call | tf_op jit(solution)/shard_map/pallas_call | solution.py:443
  25.5 0.2 collective-permute-start.15
  25.7 1.4 %shard_map.107 = (bf16[12288,128]{1,0:T(8,128)(2,1)}, f32[8,128]{1,0:T(8,128)S(1)}) custom-call(bf16[128,3072]{1,0:T(8,128)(2,1)S(1)} %get-tuple-element.41.tok_ref, bf16[128,512]{1,0:T(8,128)(2,1)S(1)} %get-tuple-element.42.pre_ref, f32[128,128]{1,0:T(8,128)S(1)} %get-tuple-element.43.refs_0_.prob_ref), custom_call_target="tpu_custom_call" | custom-call | flops 67108864 | bytes 1048576 | tf_op jit(solution)/shard_map/pallas_call | solution.py:336
  27.0 0.2 collective-permute-done.15.refs_0_
  27.3 0.2 shard_map.108
  27.4 1.7 %collective-permute-start.16 = (bf16[16,3200]{1,0:T(8,128)(2,1)S(1)}, bf16[16,3200]{1,0:T(8,128)(2,1)S(1)}, u32[]{:S(2)}, u32[]{:S(2)}) collective-permute-start(bf16[16,3200]{1,0:T(8,128)(2,1)S(1)} %get-tuple-element.46), channel_id=1, source_target_pairs={{0,6},{1,7},{2,4},{3,5},{4,2},{5,3},{6,0},{7,1},{8,14},{9,15},{10,... | collective-permute-start | bytes 307208 | tf_op jit(solution)/shard_map/ppermute | solution.py:30
  29.1 1.5 %collective-permute-start.17 = (bf16[16,3200]{1,0:T(8,128)(2,1)S(1)}, bf16[16,3200]{1,0:T(8,128)(2,1)S(1)}, u32[]{:S(2)}, u32[]{:S(2)}) collective-permute-start(bf16[16,3200]{1,0:T(8,128)(2,1)S(1)} %get-tuple-element.47), channel_id=1, source_target_pairs={{0,2},{1,5},{2,0},{3,7},{4,6},{5,1},{6,4},{7,3},{8,10},{9,13},{10,... | collective-permute-start | bytes 307208 | tf_op jit(solution)/shard_map/ppermute | solution.py:30
  30.6 0.4 collective-permute-start.18
  31.0 2.7 %shard_map.109 = (bf16[12288,128]{1,0:T(8,128)(2,1)}, f32[8,128]{1,0:T(8,128)S(1)}) custom-call(bf16[128,3072]{1,0:T(8,128)(2,1)S(1)} %get-tuple-element.41.tok_ref, bf16[128,512]{1,0:T(8,128)(2,1)S(1)} %get-tuple-element.42.pre_ref, f32[16,3200]{1,0:T(8,128)S(1)} %get-tuple-element.45.refs_0_.own_ref, ...), custom_call_target="tpu_custom_call", output_to_operand_aliasing={{0}: (3, {})} | custom-call | flops 201326592 | bytes 3145728 | tf_op jit(solution)/shard_map/pallas_call | solution.py:336
  33.7 1.6 %shard_map.110 = (bf16[256,3072]{1,0:T(8,128)(2,1)}, f32[8,128]{1,0:T(8,128)S(1)}) custom-call(bf16[128,256]{1,0:T(8,128)(2,1)S(1)} %get-tuple-element.49.hid_ref, bf16[128,3072]{1,0:T(8,128)(2,1)S(1)} %get-tuple-element.50.grad_ref, f32[128,128]{1,0:T(8,128)S(1)} %get-tuple-element.43.refs_0_.prob_ref, f32[8,128]{1,0:T(8,128)S(1)} %get-tuple-element.52.after_ref), custom_call_target="tpu_custom_call" | custom-call | flops 201326592 | bytes 3145728 | tf_op jit(solution)/shard_map/pallas_call | solution.py:381
  35.3 0.0 collective-permute-done.16.refs_0_
  35.3 0.2 collective-permute-done.17.refs_1_
  35.5 0.2 shard_map.111
  35.7 3.2 %collective-permute-start.19 = (bf16[8,3200]{1,0:T(8,128)(2,1)S(1)}, bf16[8,3200]{1,0:T(8,128)(2,1)S(1)}, u32[]{:S(2)}, u32[]{:S(2)}) collective-permute-start(bf16[8,3200]{1,0:T(8,128)(2,1)S(1)} %get-tuple-element.55), channel_id=1, source_target_pairs={{0,8},{1,9},{2,10},{3,11},{4,12},{5,13},{6,14},{7,15},{8,0},{9,1},... | collective-permute-start | bytes 153608 | tf_op jit(solution)/shard_map/ppermute | solution.py:30
  38.9 1.7 %shard_map.112 = (bf16[12288,128]{1,0:T(8,128)(2,1)}, f32[8,128]{1,0:T(8,128)S(1)}) custom-call(bf16[128,3072]{1,0:T(8,128)(2,1)S(1)} %get-tuple-element.41.tok_ref, bf16[128,512]{1,0:T(8,128)(2,1)S(1)} %get-tuple-element.42.pre_ref, f32[8,3200]{1,0:T(8,128)S(1)} %get-tuple-element.54.refs_0_.own_ref, ...), custom_call_target="tpu_custom_call", output_to_operand_aliasing={{0}: (3, {})} | custom-call | flops 134217728 | bytes 2097152 | tf_op jit(solution)/shard_map/pallas_call | solution.py:336
  40.6 0.4 collective-permute-done.19.got_ref
  41.0 0.7 %shard_map.113 = (bf16[8,3072]{1,0:T(8,128)(2,1)}, f32[2,8]{1,0:T(2,128)}) custom-call(f32[8,3200]{1,0:T(8,128)S(1)} %get-tuple-element.54.refs_0_.own_ref, bf16[8,3200]{1,0:T(8,128)(2,1)S(1)} %collective-permute-done.19.got_ref, s32[2,8]{1,0:T(2,128)S(1)} %bitcast.14, f32[8,128]{1,0:T(8,128)S(1)} %get-tuple-element.57.after_ref), custom_call_target="tpu_custom_call" | custom-call | tf_op jit(solution)/shard_map/pallas_call | solution.py:477
  (16 shorter events, 0.0 us)
Async XLA Ops:
  0.6 2.1 %copy-start.1 = (bf16[8,3072]{1,0:T(8,128)(2,1)S(1)}, bf16[8,3072]{1,0:T(8,128)(2,1)}, u32[]{:S(2)}) copy-start(bf16[8,3072]{1,0:T(8,128)(2,1)} %tok_ref.1) | copy-start | bytes 147460
  0.6 2.1 %copy-start.2 = (bf16[8,3072]{1,0:T(8,128)(2,1)S(1)}, bf16[8,3072]{1,0:T(8,128)(2,1)}, u32[]{:S(2)}) copy-start(bf16[8,3072]{1,0:T(8,128)(2,1)} %grad_ref.1) | copy-start | bytes 147460
  0.7 2.1 %copy-start.3 = (s32[8,2]{0,1:T(2,128)S(1)}, s32[8,2]{0,1:T(2,128)}, u32[]{:S(2)}) copy-start(s32[8,2]{0,1:T(2,128)} %param.9) | copy-start | bytes 196
  0.7 2.1 %copy-start.4 = (f32[8,2]{0,1:T(2,128)S(1)}, f32[8,2]{0,1:T(2,128)}, u32[]{:S(2)}) copy-start(f32[8,2]{0,1:T(2,128)} %param.10) | copy-start | bytes 196
  2.8 7.4 %collective-permute-start = (bf16[8,6272]{1,0:T(8,128)(2,1)S(1)}, bf16[8,6272]{1,0:T(8,128)(2,1)S(1)}, u32[]{:S(2)}, u32[]{:S(2)}) collective-permute-start(bf16[8,6272]{1,0:T(8,128)(2,1)S(1)} %shard_map.102.refs_0_), channel_id=1, source_target_pairs={{0,8},{1,9},{2,10},{3,11},{4,12},{5,13},{6,14},{7,15},{8,0},{9,1},... | collective-permute-start | bytes 301064 | tf_op jit(solution)/shard_map/ppermute | solution.py:30
  6.9 6.2 %collective-permute-start.3 = (bf16[8,6272]{1,0:T(8,128)(2,1)S(1)}, bf16[8,6272]{1,0:T(8,128)(2,1)S(1)}, u32[]{:S(2)}, u32[]{:S(2)}) collective-permute-start(bf16[8,6272]{1,0:T(8,128)(2,1)S(1)} %shard_map.102.refs_0_), channel_id=1, source_target_pairs={{0,2},{1,5},{2,0},{3,7},{4,6},{5,1},{6,4},{7,3},{8,10},{9,13},{10,... | collective-permute-start | bytes 301064 | tf_op jit(solution)/shard_map/ppermute | solution.py:30
  8.4 5.4 %collective-permute-start.1 = (bf16[8,6272]{1,0:T(8,128)(2,1)S(1)}, bf16[8,6272]{1,0:T(8,128)(2,1)S(1)}, u32[]{:S(2)}, u32[]{:S(2)}) collective-permute-start(bf16[8,6272]{1,0:T(8,128)(2,1)S(1)} %shard_map.102.refs_0_), channel_id=1, source_target_pairs={{0,4},{1,3},{2,6},{3,1},{4,0},{5,7},{6,2},{7,5},{8,12},{9,11},{10,... | collective-permute-start | bytes 301064 | tf_op jit(solution)/shard_map/ppermute | solution.py:30
  10.2 11.9 %copy-start = (bf16[256,3072]{1,0:T(8,128)(2,1)S(1)}, bf16[256,3072]{1,0:T(8,128)(2,1)}, u32[]{:S(2)}) copy-start(bf16[256,3072]{1,0:T(8,128)(2,1)} %refs_18_.1) | copy-start | bytes 4718596
  10.2 11.9 %copy-start.5 = (s32[16]{0:T(128)S(1)}, s32[16]{0:T(128)}, u32[]{:S(2)}) copy-start(s32[16]{0:T(128)} %owner_ref.1) | copy-start | bytes 196
  10.2 4.8 %collective-permute-start.4 = (bf16[8,6272]{1,0:T(8,128)(2,1)S(1)}, bf16[8,6272]{1,0:T(8,128)(2,1)S(1)}, u32[]{:S(2)}, u32[]{:S(2)}) collective-permute-start(bf16[8,6272]{1,0:T(8,128)(2,1)S(1)} %collective-permute-done.refs_1_), channel_id=1, source_target_pairs={{0,2},{1,5},{2,0},{3,7},{4,6},{5,1},{6,4},{7,3},{8,10},{9,13},{10,... | collective-permute-start | bytes 301064 | tf_op jit(solution)/shard_map/ppermute | solution.py:30
  11.5 4.6 %collective-permute-start.2 = (bf16[8,6272]{1,0:T(8,128)(2,1)S(1)}, bf16[8,6272]{1,0:T(8,128)(2,1)S(1)}, u32[]{:S(2)}, u32[]{:S(2)}) collective-permute-start(bf16[8,6272]{1,0:T(8,128)(2,1)S(1)} %collective-permute-done.refs_1_), channel_id=1, source_target_pairs={{0,4},{1,3},{2,6},{3,1},{4,0},{5,7},{6,2},{7,5},{8,12},{9,11},{10,... | collective-permute-start | bytes 301064 | tf_op jit(solution)/shard_map/ppermute | solution.py:30
  13.1 5.8 %collective-permute-start.7 = (bf16[8,6272]{1,0:T(8,128)(2,1)S(1)}, bf16[8,6272]{1,0:T(8,128)(2,1)S(1)}, u32[]{:S(2)}, u32[]{:S(2)}) collective-permute-start(bf16[8,6272]{1,0:T(8,128)(2,1)S(1)} %shard_map.102.refs_0_), channel_id=1, source_target_pairs={{0,1},{1,0},{2,3},{3,2},{4,5},{5,4},{6,7},{7,6},{8,9},{9,8},{10,11... | collective-permute-start | bytes 301064 | tf_op jit(solution)/shard_map/ppermute | solution.py:30
  13.2 5.9 %collective-permute-start.11 = (bf16[8,6272]{1,0:T(8,128)(2,1)S(1)}, bf16[8,6272]{1,0:T(8,128)(2,1)S(1)}, u32[]{:S(2)}, u32[]{:S(2)}) collective-permute-start(bf16[8,6272]{1,0:T(8,128)(2,1)S(1)} %collective-permute-done.3.refs_4_), channel_id=1, source_target_pairs={{0,1},{1,0},{2,3},{3,2},{4,5},{5,4},{6,7},{7,6},{8,9},{9,8},{10,11... | collective-permute-start | bytes 301064 | tf_op jit(solution)/shard_map/ppermute | solution.py:30
  13.8 5.7 %collective-permute-start.5 = (bf16[8,6272]{1,0:T(8,128)(2,1)S(1)}, bf16[8,6272]{1,0:T(8,128)(2,1)S(1)}, u32[]{:S(2)}, u32[]{:S(2)}) collective-permute-start(bf16[8,6272]{1,0:T(8,128)(2,1)S(1)} %collective-permute-done.3.refs_4_), channel_id=1, source_target_pairs={{0,4},{1,3},{2,6},{3,1},{4,0},{5,7},{6,2},{7,5},{8,12},{9,11},{10,... | collective-permute-start | bytes 301064 | tf_op jit(solution)/shard_map/ppermute | solution.py:30
  15.0 4.6 %collective-permute-start.9 = (bf16[8,6272]{1,0:T(8,128)(2,1)S(1)}, bf16[8,6272]{1,0:T(8,128)(2,1)S(1)}, u32[]{:S(2)}, u32[]{:S(2)}) collective-permute-start(bf16[8,6272]{1,0:T(8,128)(2,1)S(1)} %collective-permute-done.1.refs_2_), channel_id=1, source_target_pairs={{0,1},{1,0},{2,3},{3,2},{4,5},{5,4},{6,7},{7,6},{8,9},{9,8},{10,11... | collective-permute-start | bytes 301064 | tf_op jit(solution)/shard_map/ppermute | solution.py:30
  16.1 4.6 %collective-permute-start.6 = (bf16[8,6272]{1,0:T(8,128)(2,1)S(1)}, bf16[8,6272]{1,0:T(8,128)(2,1)S(1)}, u32[]{:S(2)}, u32[]{:S(2)}) collective-permute-start(bf16[8,6272]{1,0:T(8,128)(2,1)S(1)} %collective-permute-done.2.refs_3_), channel_id=1, source_target_pairs={{0,2},{1,5},{2,0},{3,7},{4,6},{5,1},{6,4},{7,3},{8,10},{9,13},{10,... | collective-permute-start | bytes 301064 | tf_op jit(solution)/shard_map/ppermute | solution.py:30
  18.9 1.8 %collective-permute-start.8 = (bf16[8,6272]{1,0:T(8,128)(2,1)S(1)}, bf16[8,6272]{1,0:T(8,128)(2,1)S(1)}, u32[]{:S(2)}, u32[]{:S(2)}) collective-permute-start(bf16[8,6272]{1,0:T(8,128)(2,1)S(1)} %collective-permute-done.refs_1_), channel_id=1, source_target_pairs={{0,1},{1,0},{2,3},{3,2},{4,5},{5,4},{6,7},{7,6},{8,9},{9,8},{10,11... | collective-permute-start | bytes 301064 | tf_op jit(solution)/shard_map/ppermute | solution.py:30
  19.0 1.8 %collective-permute-start.12 = (bf16[8,6272]{1,0:T(8,128)(2,1)S(1)}, bf16[8,6272]{1,0:T(8,128)(2,1)S(1)}, u32[]{:S(2)}, u32[]{:S(2)}) collective-permute-start(bf16[8,6272]{1,0:T(8,128)(2,1)S(1)} %collective-permute-done.4.refs_5_), channel_id=1, source_target_pairs={{0,1},{1,0},{2,3},{3,2},{4,5},{5,4},{6,7},{7,6},{8,9},{9,8},{10,11... | collective-permute-start | bytes 301064 | tf_op jit(solution)/shard_map/ppermute | solution.py:30
  19.5 1.3 %collective-permute-start.13 = (bf16[8,6272]{1,0:T(8,128)(2,1)S(1)}, bf16[8,6272]{1,0:T(8,128)(2,1)S(1)}, u32[]{:S(2)}, u32[]{:S(2)}) collective-permute-start(bf16[8,6272]{1,0:T(8,128)(2,1)S(1)} %collective-permute-done.5.refs_6_), channel_id=1, source_target_pairs={{0,1},{1,0},{2,3},{3,2},{4,5},{5,4},{6,7},{7,6},{8,9},{9,8},{10,11... | collective-permute-start | bytes 301064 | tf_op jit(solution)/shard_map/ppermute | solution.py:30
  19.6 1.4 %collective-permute-start.10 = (bf16[8,6272]{1,0:T(8,128)(2,1)S(1)}, bf16[8,6272]{1,0:T(8,128)(2,1)S(1)}, u32[]{:S(2)}, u32[]{:S(2)}) collective-permute-start(bf16[8,6272]{1,0:T(8,128)(2,1)S(1)} %collective-permute-done.2.refs_3_), channel_id=1, source_target_pairs={{0,1},{1,0},{2,3},{3,2},{4,5},{5,4},{6,7},{7,6},{8,9},{9,8},{10,11... | collective-permute-start | bytes 301064 | tf_op jit(solution)/shard_map/ppermute | solution.py:30
  20.7 1.3 %collective-permute-start.14 = (bf16[8,6272]{1,0:T(8,128)(2,1)S(1)}, bf16[8,6272]{1,0:T(8,128)(2,1)S(1)}, u32[]{:S(2)}, u32[]{:S(2)}) collective-permute-start(bf16[8,6272]{1,0:T(8,128)(2,1)S(1)} %collective-permute-done.6.refs_7_), channel_id=1, source_target_pairs={{0,1},{1,0},{2,3},{3,2},{4,5},{5,4},{6,7},{7,6},{8,9},{9,8},{10,11... | collective-permute-start | bytes 301064 | tf_op jit(solution)/shard_map/ppermute | solution.py:30
  25.5 1.8 %collective-permute-start.15 = (bf16[64,3200]{1,0:T(8,128)(2,1)S(1)}, bf16[64,3200]{1,0:T(8,128)(2,1)S(1)}, u32[]{:S(2)}, u32[]{:S(2)}) collective-permute-start(bf16[64,3200]{1,0:T(8,128)(2,1)S(1)} %get-tuple-element.40), channel_id=1, source_target_pairs={{0,1},{1,0},{2,3},{3,2},{4,5},{5,4},{6,7},{7,6},{8,9},{9,8},{10,11... | collective-permute-start | bytes 1228808 | tf_op jit(solution)/shard_map/ppermute | solution.py:30
  27.4 7.9 %collective-permute-start.16 = (bf16[16,3200]{1,0:T(8,128)(2,1)S(1)}, bf16[16,3200]{1,0:T(8,128)(2,1)S(1)}, u32[]{:S(2)}, u32[]{:S(2)}) collective-permute-start(bf16[16,3200]{1,0:T(8,128)(2,1)S(1)} %get-tuple-element.46), channel_id=1, source_target_pairs={{0,6},{1,7},{2,4},{3,5},{4,2},{5,3},{6,0},{7,1},{8,14},{9,15},{10,... | collective-permute-start | bytes 307208 | tf_op jit(solution)/shard_map/ppermute | solution.py:30
  29.1 6.4 %collective-permute-start.17 = (bf16[16,3200]{1,0:T(8,128)(2,1)S(1)}, bf16[16,3200]{1,0:T(8,128)(2,1)S(1)}, u32[]{:S(2)}, u32[]{:S(2)}) collective-permute-start(bf16[16,3200]{1,0:T(8,128)(2,1)S(1)} %get-tuple-element.47), channel_id=1, source_target_pairs={{0,2},{1,5},{2,0},{3,7},{4,6},{5,1},{6,4},{7,3},{8,10},{9,13},{10,... | collective-permute-start | bytes 307208 | tf_op jit(solution)/shard_map/ppermute | solution.py:30
  30.6 4.9 %collective-permute-start.18 = (bf16[16,3200]{1,0:T(8,128)(2,1)S(1)}, bf16[16,3200]{1,0:T(8,128)(2,1)S(1)}, u32[]{:S(2)}, u32[]{:S(2)}) collective-permute-start(bf16[16,3200]{1,0:T(8,128)(2,1)S(1)} %get-tuple-element.48), channel_id=1, source_target_pairs={{0,4},{1,3},{2,6},{3,1},{4,0},{5,7},{6,2},{7,5},{8,12},{9,11},{10,... | collective-permute-start | bytes 307208 | tf_op jit(solution)/shard_map/ppermute | solution.py:30
  35.7 5.3 %collective-permute-start.19 = (bf16[8,3200]{1,0:T(8,128)(2,1)S(1)}, bf16[8,3200]{1,0:T(8,128)(2,1)S(1)}, u32[]{:S(2)}, u32[]{:S(2)}) collective-permute-start(bf16[8,3200]{1,0:T(8,128)(2,1)S(1)} %get-tuple-element.55), channel_id=1, source_target_pairs={{0,8},{1,9},{2,10},{3,11},{4,12},{5,13},{6,14},{7,15},{8,0},{9,1},... | collective-permute-start | bytes 153608 | tf_op jit(solution)/shard_map/ppermute | solution.py:30

commit v7 on v6

--- a/solution.py
+++ b/solution.py
@@ -20,7 +20,7 @@
 TN = (((0,), (0,)), ((), ()))
 
 
-def params(mib=16):
+def params(mib=20):
     return pltpu.CompilerParams(vmem_limit_bytes=mib << 20)
 
 
@@ -118,7 +118,9 @@
     if when is None:
         split_rows(part, w_hbm, out_ref, w_ref, sems)
         return
-    mine = lax.axis_index("dev") % 2 == when
+    me, n = lax.axis_index("dev"), lax.axis_size("dev")
+    early = (me % 2 == 0) & (me < 3 * n // 4)
+    mine = early if when == 0 else jnp.logical_not(early)
 
     @pl.when(mine)
     def _():

time: 41.9 us -> 41.6 us (level)
  starting transfers between devices: 20.8 us -> 18.8 us
  waiting for transfers between devices: 4.09 us -> 5.73 us
    ppermute x20, starting transfers between devices: 20.8 us -> 18.8 us  [xor_swap(): lax.ppermute(value, 'dev', [(i, i ^ (other if i & 1 else bit)) for i in r...]
    ppermute x20, waiting for transfers between devices: 4.09 us -> 5.73 us  [xor_swap(): lax.ppermute(value, 'dev', [(i, i ^ (other if i & 1 else bit)) for i in r...]
  transfers between devices with their start and end apart: 20 -> 20, of which waited for: 9 -> 11; matrix products, arithmetic and copies ran while one was open for 0% -> 0% of each run, Pallas kernels for 23% -> 23%
where the time goes in v7:
time: 41.6 us; the launch traced here: 41.5 us
  starting transfers between devices  18.8 us (45%)
  Pallas kernels  16 us (38%)
  waiting for transfers between devices  5.73 us (14%)
  between operations  0.83 us (2%)
    ppermute x20, starting transfers between devices, xor_swap(): lax.ppermute(value, 'dev', [(i, i ^ (other if i & 1 else bit)) for i in r...  18.8 us
    pallas_call x3, Pallas kernels, grad_in(): pl.pallas_call(functools.partial(win_kernel, blocks, parity), in_specs=[V...  5.78 us
    ppermute x20, waiting for transfers between devices, xor_swap(): lax.ppermute(value, 'dev', [(i, i ^ (other if i & 1 else bit)) for i in r...  5.73 us
    pallas_call x3, Pallas kernels, split_weights(): pl.pallas_call(functools.partial(split_kernel, part, when), in_specs=[ANY...  4.13 us
    pallas_call x1, Pallas kernels, shards(): pl.pallas_call(functools.partial(main_kernel, n), in_specs=[SMEM] + [VMEM...  3.39 us
    pallas_call x1, Pallas kernels, grad_down(): pl.pallas_call(down_kernel, in_specs=[VMEM] * 3 + [ANY], out_specs=[ANY,...  1.6 us
  transfers between devices with their start and end apart: 20, of which 11 were waited for; matrix products, arithmetic and copies ran while one was open for 0% of the time, Pallas kernels for 23%

profile of v7, /device:TPU:0, one launch (start us, length us, event | category | flops | bytes accessed | tf_op | source)
XLA Modules:
  0.0 41.5 jit_solution(570532674604117275)
XLA Ops:
  0.7 2.0 %shard_map.103.refs_0_ = bf16[1536,512]{1,0:T(8,128)(2,1)S(1)} custom-call(bf16[12288,128]{1,0:T(8,128)(2,1)} %bitcast.16), custom_call_target="tpu_custom_call" | custom-call | flops 402653184 | bytes 3145728 | tf_op jit(solution)/shard_map/pallas_call | solution.py:144
  2.7 0.1 shard_map.102.refs_0_
  2.8 4.1 %collective-permute-start = (bf16[8,6272]{1,0:T(8,128)(2,1)S(1)}, bf16[8,6272]{1,0:T(8,128)(2,1)S(1)}, u32[]{:S(2)}, u32[]{:S(2)}) collective-permute-start(bf16[8,6272]{1,0:T(8,128)(2,1)S(1)} %shard_map.102.refs_0_), channel_id=1, source_target_pairs={{0,8},{1,9},{2,10},{3,11},{4,12},{5,13},{6,14},{7,15},{8,0},{9,1},... | collective-permute-start | bytes 301064 | tf_op jit(solution)/shard_map/ppermute | solution.py:30
  6.9 1.5 %collective-permute-start.3 = (bf16[8,6272]{1,0:T(8,128)(2,1)S(1)}, bf16[8,6272]{1,0:T(8,128)(2,1)S(1)}, u32[]{:S(2)}, u32[]{:S(2)}) collective-permute-start(bf16[8,6272]{1,0:T(8,128)(2,1)S(1)} %shard_map.102.refs_0_), channel_id=1, source_target_pairs={{0,2},{1,5},{2,0},{3,7},{4,6},{5,1},{6,4},{7,3},{8,10},{9,13},{10,... | collective-permute-start | bytes 301064 | tf_op jit(solution)/shard_map/ppermute | solution.py:30
  8.4 0.3 collective-permute-start.1
  8.7 0.1 shard_map.104.refs_16_
  8.9 0.0 copy-start
  8.9 0.0 copy-start.5
  8.9 0.8 %collective-permute-done.refs_1_ = bf16[8,6272]{1,0:T(8,128)(2,1)S(1)} collective-permute-done((bf16[8,6272]{1,0:T(8,128)(2,1)S(1)}, bf16[8,6272]{1,0:T(8,128)(2,1)S(1)}, u32[]{:S(2)}, u32[]{:S(2)}) %collective-permute-start) | collective-permute-done | bytes 100384 | tf_op jit(solution)/shard_map/ppermute | solution.py:30
  9.7 1.8 %collective-permute-start.4 = (bf16[8,6272]{1,0:T(8,128)(2,1)S(1)}, bf16[8,6272]{1,0:T(8,128)(2,1)S(1)}, u32[]{:S(2)}, u32[]{:S(2)}) collective-permute-start(bf16[8,6272]{1,0:T(8,128)(2,1)S(1)} %collective-permute-done.refs_1_), channel_id=1, source_target_pairs={{0,2},{1,5},{2,0},{3,7},{4,6},{5,1},{6,4},{7,3},{8,10},{9,13},{10,... | collective-permute-start | bytes 301064 | tf_op jit(solution)/shard_map/ppermute | solution.py:30
  11.5 1.6 %collective-permute-start.2 = (bf16[8,6272]{1,0:T(8,128)(2,1)S(1)}, bf16[8,6272]{1,0:T(8,128)(2,1)S(1)}, u32[]{:S(2)}, u32[]{:S(2)}) collective-permute-start(bf16[8,6272]{1,0:T(8,128)(2,1)S(1)} %collective-permute-done.refs_1_), channel_id=1, source_target_pairs={{0,4},{1,3},{2,6},{3,1},{4,0},{5,7},{6,2},{7,5},{8,12},{9,11},{10,... | collective-permute-start | bytes 301064 | tf_op jit(solution)/shard_map/ppermute | solution.py:30
  13.1 0.0 collective-permute-start.7
  13.1 0.0 collective-permute-done.3.refs_4_
  13.1 0.5 %collective-permute-start.11 = (bf16[8,6272]{1,0:T(8,128)(2,1)S(1)}, bf16[8,6272]{1,0:T(8,128)(2,1)S(1)}, u32[]{:S(2)}, u32[]{:S(2)}) collective-permute-start(bf16[8,6272]{1,0:T(8,128)(2,1)S(1)} %collective-permute-done.3.refs_4_), channel_id=1, source_target_pairs={{0,1},{1,0},{2,3},{3,2},{4,5},{5,4},{6,7},{7,6},{8,9},{9,8},{10,11... | collective-permute-start | bytes 301064 | tf_op jit(solution)/shard_map/ppermute | solution.py:30
  13.6 0.3 collective-permute-done.1.refs_2_
  13.8 0.2 collective-permute-start.5
  14.0 1.1 %collective-permute-done.4.refs_5_ = bf16[8,6272]{1,0:T(8,128)(2,1)S(1)} collective-permute-done((bf16[8,6272]{1,0:T(8,128)(2,1)S(1)}, bf16[8,6272]{1,0:T(8,128)(2,1)S(1)}, u32[]{:S(2)}, u32[]{:S(2)}) %collective-permute-start.4) | collective-permute-done | bytes 100384 | tf_op jit(solution)/shard_map/ppermute | solution.py:30
  15.1 0.0 collective-permute-start.9
  15.1 1.0 %collective-permute-done.2.refs_3_ = bf16[8,6272]{1,0:T(8,128)(2,1)S(1)} collective-permute-done((bf16[8,6272]{1,0:T(8,128)(2,1)S(1)}, bf16[8,6272]{1,0:T(8,128)(2,1)S(1)}, u32[]{:S(2)}, u32[]{:S(2)}) %collective-permute-start.2) | collective-permute-done | bytes 100384 | tf_op jit(solution)/shard_map/ppermute | solution.py:30
  16.1 1.1 %collective-permute-start.6 = (bf16[8,6272]{1,0:T(8,128)(2,1)S(1)}, bf16[8,6272]{1,0:T(8,128)(2,1)S(1)}, u32[]{:S(2)}, u32[]{:S(2)}) collective-permute-start(bf16[8,6272]{1,0:T(8,128)(2,1)S(1)} %collective-permute-done.2.refs_3_), channel_id=1, source_target_pairs={{0,2},{1,5},{2,0},{3,7},{4,6},{5,1},{6,4},{7,3},{8,10},{9,13},{10,... | collective-permute-start | bytes 301064 | tf_op jit(solution)/shard_map/ppermute | solution.py:30
  17.2 2.0 %shard_map.105.refs_17_ = bf16[1536,512]{1,0:T(8,128)(2,1)S(1)} custom-call(bf16[12288,128]{1,0:T(8,128)(2,1)} %bitcast.18), custom_call_target="tpu_custom_call" | custom-call | flops 402653184 | bytes 3145728 | tf_op jit(solution)/shard_map/pallas_call | solution.py:144
  19.2 0.0 collective-permute-done.7.refs_8_
  19.2 0.1 collective-permute-start.8
  19.3 0.5 %collective-permute-start.12 = (bf16[8,6272]{1,0:T(8,128)(2,1)S(1)}, bf16[8,6272]{1,0:T(8,128)(2,1)S(1)}, u32[]{:S(2)}, u32[]{:S(2)}) collective-permute-start(bf16[8,6272]{1,0:T(8,128)(2,1)S(1)} %collective-permute-done.4.refs_5_), channel_id=1, source_target_pairs={{0,1},{1,0},{2,3},{3,2},{4,5},{5,4},{6,7},{7,6},{8,9},{9,8},{10,11... | collective-permute-start | bytes 301064 | tf_op jit(solution)/shard_map/ppermute | solution.py:30
  19.8 0.0 collective-permute-done.5.refs_6_
  19.8 0.1 collective-permute-start.13
  19.9 0.0 collective-permute-done.9.refs_10_
  19.9 0.4 %collective-permute-start.10 = (bf16[8,6272]{1,0:T(8,128)(2,1)S(1)}, bf16[8,6272]{1,0:T(8,128)(2,1)S(1)}, u32[]{:S(2)}, u32[]{:S(2)}) collective-permute-start(bf16[8,6272]{1,0:T(8,128)(2,1)S(1)} %collective-permute-done.2.refs_3_), channel_id=1, source_target_pairs={{0,1},{1,0},{2,3},{3,2},{4,5},{5,4},{6,7},{7,6},{8,9},{9,8},{10,11... | collective-permute-start | bytes 301064 | tf_op jit(solution)/shard_map/ppermute | solution.py:30
  20.3 0.5 %collective-permute-done.6.refs_7_ = bf16[8,6272]{1,0:T(8,128)(2,1)S(1)} collective-permute-done((bf16[8,6272]{1,0:T(8,128)(2,1)S(1)}, bf16[8,6272]{1,0:T(8,128)(2,1)S(1)}, u32[]{:S(2)}, u32[]{:S(2)}) %collective-permute-start.6) | collective-permute-done | bytes 100384 | tf_op jit(solution)/shard_map/ppermute | solution.py:30
  20.8 0.3 collective-permute-done.13.refs_14_
  21.1 0.2 collective-permute-done.10.refs_11_
  21.2 0.8 %collective-permute-done.14.refs_15_ = bf16[8,6272]{1,0:T(8,128)(2,1)S(1)} collective-permute-done((bf16[8,6272]{1,0:T(8,128)(2,1)S(1)}, bf16[8,6272]{1,0:T(8,128)(2,1)S(1)}, u32[]{:S(2)}, u32[]{:S(2)}) %collective-permute-start.14) | collective-permute-done | bytes 100384 | tf_op jit(solution)/shard_map/ppermute | solution.py:30
  22.1 3.4 %shard_map.106 = (bf16[128,3072]{1,0:T(8,128)(2,1)S(1)}, bf16[128,3072]{1,0:T(8,128)(2,1)S(1)}, bf16[128,512]{1,0:T(8,128)(2,1)S(1)}, bf16[128,256]{1,0:T(8,128)...) custom-call(s32[16]{0:T(128)S(1)} %copy-done.5, ...), custom_call_target="tpu_custom_call" | custom-call | tf_op jit(solution)/shard_map/pallas_call | solution.py:445
  25.5 0.2 collective-permute-start.15
  25.7 1.4 %shard_map.107 = (bf16[12288,128]{1,0:T(8,128)(2,1)}, f32[8,128]{1,0:T(8,128)S(1)}) custom-call(bf16[128,3072]{1,0:T(8,128)(2,1)S(1)} %get-tuple-element.41.tok_ref, bf16[128,512]{1,0:T(8,128)(2,1)S(1)} %get-tuple-element.42.pre_ref, f32[128,128]{1,0:T(8,128)S(1)} %get-tuple-element.43.refs_0_.prob_ref), custom_call_target="tpu_custom_call" | custom-call | flops 67108864 | bytes 1048576 | tf_op jit(solution)/shard_map/pallas_call | solution.py:338
  27.0 0.2 collective-permute-done.15.refs_0_
  27.3 0.2 shard_map.108
  27.4 1.9 %collective-permute-start.16 = (bf16[16,3200]{1,0:T(8,128)(2,1)S(1)}, bf16[16,3200]{1,0:T(8,128)(2,1)S(1)}, u32[]{:S(2)}, u32[]{:S(2)}) collective-permute-start(bf16[16,3200]{1,0:T(8,128)(2,1)S(1)} %get-tuple-element.46), channel_id=1, source_target_pairs={{0,6},{1,7},{2,4},{3,5},{4,2},{5,3},{6,0},{7,1},{8,14},{9,15},{10,... | collective-permute-start | bytes 307208 | tf_op jit(solution)/shard_map/ppermute | solution.py:30
  29.3 1.2 %collective-permute-start.17 = (bf16[16,3200]{1,0:T(8,128)(2,1)S(1)}, bf16[16,3200]{1,0:T(8,128)(2,1)S(1)}, u32[]{:S(2)}, u32[]{:S(2)}) collective-permute-start(bf16[16,3200]{1,0:T(8,128)(2,1)S(1)} %get-tuple-element.47), channel_id=1, source_target_pairs={{0,2},{1,5},{2,0},{3,7},{4,6},{5,1},{6,4},{7,3},{8,10},{9,13},{10,... | collective-permute-start | bytes 307208 | tf_op jit(solution)/shard_map/ppermute | solution.py:30
  30.5 0.4 %collective-permute-start.18 = (bf16[16,3200]{1,0:T(8,128)(2,1)S(1)}, bf16[16,3200]{1,0:T(8,128)(2,1)S(1)}, u32[]{:S(2)}, u32[]{:S(2)}) collective-permute-start(bf16[16,3200]{1,0:T(8,128)(2,1)S(1)} %get-tuple-element.48), channel_id=1, source_target_pairs={{0,4},{1,3},{2,6},{3,1},{4,0},{5,7},{6,2},{7,5},{8,12},{9,11},{10,... | collective-permute-start | bytes 307208 | tf_op jit(solution)/shard_map/ppermute | solution.py:30
  31.0 2.7 %shard_map.109 = (bf16[12288,128]{1,0:T(8,128)(2,1)}, f32[8,128]{1,0:T(8,128)S(1)}) custom-call(bf16[128,3072]{1,0:T(8,128)(2,1)S(1)} %get-tuple-element.41.tok_ref, bf16[128,512]{1,0:T(8,128)(2,1)S(1)} %get-tuple-element.42.pre_ref, f32[16,3200]{1,0:T(8,128)S(1)} %get-tuple-element.45.refs_0_.own_ref, ...), custom_call_target="tpu_custom_call", output_to_operand_aliasing={{0}: (3, {})} | custom-call | flops 201326592 | bytes 3145728 | tf_op jit(solution)/shard_map/pallas_call | solution.py:338
  33.7 1.6 %shard_map.110 = (bf16[256,3072]{1,0:T(8,128)(2,1)}, f32[8,128]{1,0:T(8,128)S(1)}) custom-call(bf16[128,256]{1,0:T(8,128)(2,1)S(1)} %get-tuple-element.49.hid_ref, bf16[128,3072]{1,0:T(8,128)(2,1)S(1)} %get-tuple-element.50.grad_ref, f32[128,128]{1,0:T(8,128)S(1)} %get-tuple-element.43.refs_0_.prob_ref, f32[8,128]{1,0:T(8,128)S(1)} %get-tuple-element.52.after_ref), custom_call_target="tpu_custom_call" | custom-call | flops 201326592 | bytes 3145728 | tf_op jit(solution)/shard_map/pallas_call | solution.py:383
  35.3 0.2 collective-permute-done.17.refs_1_
  35.5 0.2 shard_map.111
  35.7 2.9 %collective-permute-start.19 = (bf16[8,3200]{1,0:T(8,128)(2,1)S(1)}, bf16[8,3200]{1,0:T(8,128)(2,1)S(1)}, u32[]{:S(2)}, u32[]{:S(2)}) collective-permute-start(bf16[8,3200]{1,0:T(8,128)(2,1)S(1)} %get-tuple-element.55), channel_id=1, source_target_pairs={{0,8},{1,9},{2,10},{3,11},{4,12},{5,13},{6,14},{7,15},{8,0},{9,1},... | collective-permute-start | bytes 153608 | tf_op jit(solution)/shard_map/ppermute | solution.py:30
  38.6 1.7 %shard_map.112 = (bf16[12288,128]{1,0:T(8,128)(2,1)}, f32[8,128]{1,0:T(8,128)S(1)}) custom-call(bf16[128,3072]{1,0:T(8,128)(2,1)S(1)} %get-tuple-element.41.tok_ref, bf16[128,512]{1,0:T(8,128)(2,1)S(1)} %get-tuple-element.42.pre_ref, f32[8,3200]{1,0:T(8,128)S(1)} %get-tuple-element.54.refs_0_.own_ref, ...), custom_call_target="tpu_custom_call", output_to_operand_aliasing={{0}: (3, {})} | custom-call | flops 134217728 | bytes 2097152 | tf_op jit(solution)/shard_map/pallas_call | solution.py:338
  40.3 0.4 collective-permute-done.19.got_ref
  40.7 0.7 %shard_map.113 = (bf16[8,3072]{1,0:T(8,128)(2,1)}, f32[2,8]{1,0:T(2,128)}) custom-call(f32[8,3200]{1,0:T(8,128)S(1)} %get-tuple-element.54.refs_0_.own_ref, bf16[8,3200]{1,0:T(8,128)(2,1)S(1)} %collective-permute-done.19.got_ref, s32[2,8]{1,0:T(2,128)S(1)} %bitcast.14, f32[8,128]{1,0:T(8,128)S(1)} %get-tuple-element.57.after_ref), custom_call_target="tpu_custom_call" | custom-call | tf_op jit(solution)/shard_map/pallas_call | solution.py:479
  (16 shorter events, 0.0 us)
Async XLA Ops:
  0.6 2.1 %copy-start.1 = (bf16[8,3072]{1,0:T(8,128)(2,1)S(1)}, bf16[8,3072]{1,0:T(8,128)(2,1)}, u32[]{:S(2)}) copy-start(bf16[8,3072]{1,0:T(8,128)(2,1)} %tok_ref.1) | copy-start | bytes 147460
  0.6 2.1 %copy-start.2 = (bf16[8,3072]{1,0:T(8,128)(2,1)S(1)}, bf16[8,3072]{1,0:T(8,128)(2,1)}, u32[]{:S(2)}) copy-start(bf16[8,3072]{1,0:T(8,128)(2,1)} %grad_ref.1) | copy-start | bytes 147460
  0.7 2.1 %copy-start.3 = (s32[8,2]{0,1:T(2,128)S(1)}, s32[8,2]{0,1:T(2,128)}, u32[]{:S(2)}) copy-start(s32[8,2]{0,1:T(2,128)} %param.9) | copy-start | bytes 196
  0.7 2.1 %copy-start.4 = (f32[8,2]{0,1:T(2,128)S(1)}, f32[8,2]{0,1:T(2,128)}, u32[]{:S(2)}) copy-start(f32[8,2]{0,1:T(2,128)} %param.10) | copy-start | bytes 196
  2.8 6.8 %collective-permute-start = (bf16[8,6272]{1,0:T(8,128)(2,1)S(1)}, bf16[8,6272]{1,0:T(8,128)(2,1)S(1)}, u32[]{:S(2)}, u32[]{:S(2)}) collective-permute-start(bf16[8,6272]{1,0:T(8,128)(2,1)S(1)} %shard_map.102.refs_0_), channel_id=1, source_target_pairs={{0,8},{1,9},{2,10},{3,11},{4,12},{5,13},{6,14},{7,15},{8,0},{9,1},... | collective-permute-start | bytes 301064 | tf_op jit(solution)/shard_map/ppermute | solution.py:30
  6.9 6.1 %collective-permute-start.3 = (bf16[8,6272]{1,0:T(8,128)(2,1)S(1)}, bf16[8,6272]{1,0:T(8,128)(2,1)S(1)}, u32[]{:S(2)}, u32[]{:S(2)}) collective-permute-start(bf16[8,6272]{1,0:T(8,128)(2,1)S(1)} %shard_map.102.refs_0_), channel_id=1, source_target_pairs={{0,2},{1,5},{2,0},{3,7},{4,6},{5,1},{6,4},{7,3},{8,10},{9,13},{10,... | collective-permute-start | bytes 301064 | tf_op jit(solution)/shard_map/ppermute | solution.py:30
  8.4 5.4 %collective-permute-start.1 = (bf16[8,6272]{1,0:T(8,128)(2,1)S(1)}, bf16[8,6272]{1,0:T(8,128)(2,1)S(1)}, u32[]{:S(2)}, u32[]{:S(2)}) collective-permute-start(bf16[8,6272]{1,0:T(8,128)(2,1)S(1)} %shard_map.102.refs_0_), channel_id=1, source_target_pairs={{0,4},{1,3},{2,6},{3,1},{4,0},{5,7},{6,2},{7,5},{8,12},{9,11},{10,... | collective-permute-start | bytes 301064 | tf_op jit(solution)/shard_map/ppermute | solution.py:30
  8.9 13.2 %copy-start = (bf16[256,3072]{1,0:T(8,128)(2,1)S(1)}, bf16[256,3072]{1,0:T(8,128)(2,1)}, u32[]{:S(2)}) copy-start(bf16[256,3072]{1,0:T(8,128)(2,1)} %refs_18_.1) | copy-start | bytes 4718596
  8.9 13.2 %copy-start.5 = (s32[16]{0:T(128)S(1)}, s32[16]{0:T(128)}, u32[]{:S(2)}) copy-start(s32[16]{0:T(128)} %owner_ref.1) | copy-start | bytes 196
  9.7 5.5 %collective-permute-start.4 = (bf16[8,6272]{1,0:T(8,128)(2,1)S(1)}, bf16[8,6272]{1,0:T(8,128)(2,1)S(1)}, u32[]{:S(2)}, u32[]{:S(2)}) collective-permute-start(bf16[8,6272]{1,0:T(8,128)(2,1)S(1)} %collective-permute-done.refs_1_), channel_id=1, source_target_pairs={{0,2},{1,5},{2,0},{3,7},{4,6},{5,1},{6,4},{7,3},{8,10},{9,13},{10,... | collective-permute-start | bytes 301064 | tf_op jit(solution)/shard_map/ppermute | solution.py:30
  11.5 4.6 %collective-permute-start.2 = (bf16[8,6272]{1,0:T(8,128)(2,1)S(1)}, bf16[8,6272]{1,0:T(8,128)(2,1)S(1)}, u32[]{:S(2)}, u32[]{:S(2)}) collective-permute-start(bf16[8,6272]{1,0:T(8,128)(2,1)S(1)} %collective-permute-done.refs_1_), channel_id=1, source_target_pairs={{0,4},{1,3},{2,6},{3,1},{4,0},{5,7},{6,2},{7,5},{8,12},{9,11},{10,... | collective-permute-start | bytes 301064 | tf_op jit(solution)/shard_map/ppermute | solution.py:30
  13.1 6.1 %collective-permute-start.7 = (bf16[8,6272]{1,0:T(8,128)(2,1)S(1)}, bf16[8,6272]{1,0:T(8,128)(2,1)S(1)}, u32[]{:S(2)}, u32[]{:S(2)}) collective-permute-start(bf16[8,6272]{1,0:T(8,128)(2,1)S(1)} %shard_map.102.refs_0_), channel_id=1, source_target_pairs={{0,1},{1,0},{2,3},{3,2},{4,5},{5,4},{6,7},{7,6},{8,9},{9,8},{10,11... | collective-permute-start | bytes 301064 | tf_op jit(solution)/shard_map/ppermute | solution.py:30
  13.1 6.2 %collective-permute-start.11 = (bf16[8,6272]{1,0:T(8,128)(2,1)S(1)}, bf16[8,6272]{1,0:T(8,128)(2,1)S(1)}, u32[]{:S(2)}, u32[]{:S(2)}) collective-permute-start(bf16[8,6272]{1,0:T(8,128)(2,1)S(1)} %collective-permute-done.3.refs_4_), channel_id=1, source_target_pairs={{0,1},{1,0},{2,3},{3,2},{4,5},{5,4},{6,7},{7,6},{8,9},{9,8},{10,11... | collective-permute-start | bytes 301064 | tf_op jit(solution)/shard_map/ppermute | solution.py:30
  13.8 5.9 %collective-permute-start.5 = (bf16[8,6272]{1,0:T(8,128)(2,1)S(1)}, bf16[8,6272]{1,0:T(8,128)(2,1)S(1)}, u32[]{:S(2)}, u32[]{:S(2)}) collective-permute-start(bf16[8,6272]{1,0:T(8,128)(2,1)S(1)} %collective-permute-done.3.refs_4_), channel_id=1, source_target_pairs={{0,4},{1,3},{2,6},{3,1},{4,0},{5,7},{6,2},{7,5},{8,12},{9,11},{10,... | collective-permute-start | bytes 301064 | tf_op jit(solution)/shard_map/ppermute | solution.py:30
  15.1 4.7 %collective-permute-start.9 = (bf16[8,6272]{1,0:T(8,128)(2,1)S(1)}, bf16[8,6272]{1,0:T(8,128)(2,1)S(1)}, u32[]{:S(2)}, u32[]{:S(2)}) collective-permute-start(bf16[8,6272]{1,0:T(8,128)(2,1)S(1)} %collective-permute-done.1.refs_2_), channel_id=1, source_target_pairs={{0,1},{1,0},{2,3},{3,2},{4,5},{5,4},{6,7},{7,6},{8,9},{9,8},{10,11... | collective-permute-start | bytes 301064 | tf_op jit(solution)/shard_map/ppermute | solution.py:30
  16.1 4.6 %collective-permute-start.6 = (bf16[8,6272]{1,0:T(8,128)(2,1)S(1)}, bf16[8,6272]{1,0:T(8,128)(2,1)S(1)}, u32[]{:S(2)}, u32[]{:S(2)}) collective-permute-start(bf16[8,6272]{1,0:T(8,128)(2,1)S(1)} %collective-permute-done.2.refs_3_), channel_id=1, source_target_pairs={{0,2},{1,5},{2,0},{3,7},{4,6},{5,1},{6,4},{7,3},{8,10},{9,13},{10,... | collective-permute-start | bytes 301064 | tf_op jit(solution)/shard_map/ppermute | solution.py:30
  19.2 1.6 %collective-permute-start.8 = (bf16[8,6272]{1,0:T(8,128)(2,1)S(1)}, bf16[8,6272]{1,0:T(8,128)(2,1)S(1)}, u32[]{:S(2)}, u32[]{:S(2)}) collective-permute-start(bf16[8,6272]{1,0:T(8,128)(2,1)S(1)} %collective-permute-done.refs_1_), channel_id=1, source_target_pairs={{0,1},{1,0},{2,3},{3,2},{4,5},{5,4},{6,7},{7,6},{8,9},{9,8},{10,11... | collective-permute-start | bytes 301064 | tf_op jit(solution)/shard_map/ppermute | solution.py:30
  19.3 1.8 %collective-permute-start.12 = (bf16[8,6272]{1,0:T(8,128)(2,1)S(1)}, bf16[8,6272]{1,0:T(8,128)(2,1)S(1)}, u32[]{:S(2)}, u32[]{:S(2)}) collective-permute-start(bf16[8,6272]{1,0:T(8,128)(2,1)S(1)} %collective-permute-done.4.refs_5_), channel_id=1, source_target_pairs={{0,1},{1,0},{2,3},{3,2},{4,5},{5,4},{6,7},{7,6},{8,9},{9,8},{10,11... | collective-permute-start | bytes 301064 | tf_op jit(solution)/shard_map/ppermute | solution.py:30
  19.8 1.3 %collective-permute-start.13 = (bf16[8,6272]{1,0:T(8,128)(2,1)S(1)}, bf16[8,6272]{1,0:T(8,128)(2,1)S(1)}, u32[]{:S(2)}, u32[]{:S(2)}) collective-permute-start(bf16[8,6272]{1,0:T(8,128)(2,1)S(1)} %collective-permute-done.5.refs_6_), channel_id=1, source_target_pairs={{0,1},{1,0},{2,3},{3,2},{4,5},{5,4},{6,7},{7,6},{8,9},{9,8},{10,11... | collective-permute-start | bytes 301064 | tf_op jit(solution)/shard_map/ppermute | solution.py:30
  19.9 1.4 %collective-permute-start.10 = (bf16[8,6272]{1,0:T(8,128)(2,1)S(1)}, bf16[8,6272]{1,0:T(8,128)(2,1)S(1)}, u32[]{:S(2)}, u32[]{:S(2)}) collective-permute-start(bf16[8,6272]{1,0:T(8,128)(2,1)S(1)} %collective-permute-done.2.refs_3_), channel_id=1, source_target_pairs={{0,1},{1,0},{2,3},{3,2},{4,5},{5,4},{6,7},{7,6},{8,9},{9,8},{10,11... | collective-permute-start | bytes 301064 | tf_op jit(solution)/shard_map/ppermute | solution.py:30
  20.7 1.3 %collective-permute-start.14 = (bf16[8,6272]{1,0:T(8,128)(2,1)S(1)}, bf16[8,6272]{1,0:T(8,128)(2,1)S(1)}, u32[]{:S(2)}, u32[]{:S(2)}) collective-permute-start(bf16[8,6272]{1,0:T(8,128)(2,1)S(1)} %collective-permute-done.6.refs_7_), channel_id=1, source_target_pairs={{0,1},{1,0},{2,3},{3,2},{4,5},{5,4},{6,7},{7,6},{8,9},{9,8},{10,11... | collective-permute-start | bytes 301064 | tf_op jit(solution)/shard_map/ppermute | solution.py:30
  25.5 1.8 %collective-permute-start.15 = (bf16[64,3200]{1,0:T(8,128)(2,1)S(1)}, bf16[64,3200]{1,0:T(8,128)(2,1)S(1)}, u32[]{:S(2)}, u32[]{:S(2)}) collective-permute-start(bf16[64,3200]{1,0:T(8,128)(2,1)S(1)} %get-tuple-element.40), channel_id=1, source_target_pairs={{0,1},{1,0},{2,3},{3,2},{4,5},{5,4},{6,7},{7,6},{8,9},{9,8},{10,11... | collective-permute-start | bytes 1228808 | tf_op jit(solution)/shard_map/ppermute | solution.py:30
  27.4 7.9 %collective-permute-start.16 = (bf16[16,3200]{1,0:T(8,128)(2,1)S(1)}, bf16[16,3200]{1,0:T(8,128)(2,1)S(1)}, u32[]{:S(2)}, u32[]{:S(2)}) collective-permute-start(bf16[16,3200]{1,0:T(8,128)(2,1)S(1)} %get-tuple-element.46), channel_id=1, source_target_pairs={{0,6},{1,7},{2,4},{3,5},{4,2},{5,3},{6,0},{7,1},{8,14},{9,15},{10,... | collective-permute-start | bytes 307208 | tf_op jit(solution)/shard_map/ppermute | solution.py:30
  29.3 6.2 %collective-permute-start.17 = (bf16[16,3200]{1,0:T(8,128)(2,1)S(1)}, bf16[16,3200]{1,0:T(8,128)(2,1)S(1)}, u32[]{:S(2)}, u32[]{:S(2)}) collective-permute-start(bf16[16,3200]{1,0:T(8,128)(2,1)S(1)} %get-tuple-element.47), channel_id=1, source_target_pairs={{0,2},{1,5},{2,0},{3,7},{4,6},{5,1},{6,4},{7,3},{8,10},{9,13},{10,... | collective-permute-start | bytes 307208 | tf_op jit(solution)/shard_map/ppermute | solution.py:30
  30.5 5.0 %collective-permute-start.18 = (bf16[16,3200]{1,0:T(8,128)(2,1)S(1)}, bf16[16,3200]{1,0:T(8,128)(2,1)S(1)}, u32[]{:S(2)}, u32[]{:S(2)}) collective-permute-start(bf16[16,3200]{1,0:T(8,128)(2,1)S(1)} %get-tuple-element.48), channel_id=1, source_target_pairs={{0,4},{1,3},{2,6},{3,1},{4,0},{5,7},{6,2},{7,5},{8,12},{9,11},{10,... | collective-permute-start | bytes 307208 | tf_op jit(solution)/shard_map/ppermute | solution.py:30
  35.7 5.1 %collective-permute-start.19 = (bf16[8,3200]{1,0:T(8,128)(2,1)S(1)}, bf16[8,3200]{1,0:T(8,128)(2,1)S(1)}, u32[]{:S(2)}, u32[]{:S(2)}) collective-permute-start(bf16[8,3200]{1,0:T(8,128)(2,1)S(1)} %get-tuple-element.55), channel_id=1, source_target_pairs={{0,8},{1,9},{2,10},{3,11},{4,12},{5,13},{6,14},{7,15},{8,0},{9,1},... | collective-permute-start | bytes 153608 | tf_op jit(solution)/shard_map/ppermute | solution.py:30
